TPU v7x, 256 devices: a whole 4x4x8 slice. The times are simulated.
256 devices in a mesh: node: 32 (over y, z), local: 8 (over x, core).
Axes of the slice: x: 4, y: 4, z: 8, core: 2. Of those that a mesh axis runs over, the one named last changes fastest.
Arguments:
- tokens: bfloat16 [4096, 6144], P('node', 'local'), may hold values from -15 to 15
- weight_values: bfloat16 [6144, 6144], P('node', 'local'), may hold values from -5 to 5
- weight_scales: bfloat16 [192, 48], P('node', 'local'), may hold values from 0.0039978027 to 0.039794922
- out_cotangent: bfloat16 [4096, 6144], P('node', 'local'), may hold values from -15 to 15
Outputs:
- queries: bfloat16 [4096, 6144], P('node', 'local')
- token_grad: bfloat16 [4096, 6144], P('node', 'local')
- weight_grad: float32 [6144, 6144], P('node', 'local')
All inputs are finite; a program needn't handle non-finite values.
Results may differ from a plain program's by a relative error of at most 0.017.
Values may be sent and summed in bfloat16 or wider, within the bound.
No kernel may reach another device: no remote copies, remote signals or barrier semaphores. Data moves between devices by JAX's collectives and lax.ppermute only.
A program may use at most 192 MiB of HBM per device.

v0:
```python
import functools

import jax
import jax.numpy as jnp
from jax import lax
from jax.experimental import pallas as pl
from jax.experimental.pallas import tpu as pltpu
from jax.sharding import Mesh, PartitionSpec as P

BR = 32
BC = 128
TOP = 2.0
STEP = 2


def spread(scales, rows, cols):
    wide = jnp.repeat(scales.astype(jnp.float32), rows, axis=-2)
    return jnp.repeat(wide, cols, axis=-1)


def shift(a, axis, step):
    n = lax.axis_size(axis)
    return lax.ppermute(a, axis, [(i, (i + step) % n) for i in range(n)])


def together(*arrays):
    return lax.optimization_barrier(arrays)


def after(a, *others):
    return lax.optimization_barrier((a,) + others)[0]


def swap_local(a):
    return lax.all_to_all(a, ("x", "core"), split_axis=0, concat_axis=0, tiled=True)


def gather_local(own):
    n = lax.axis_size(("x", "core"))
    return swap_local(jnp.broadcast_to(own, (n,) + own.shape))


def grad_kernel(x_ref, g_ref, o_ref, p_ref):
    @pl.when(pl.program_id(0) == 0)
    def _():
        o_ref[...] = jnp.zeros_like(o_ref)

    ny, rows, width = o_ref.shape
    nb = rows // BR
    d = g_ref[0, rows:, :]
    for k in range(ny):
        p_ref[k] = jnp.dot(x_ref[0, k], d, preferred_element_type=jnp.float32)
        p = p_ref[k].reshape(nb, BR, width)
        col = jnp.sum(p * p, axis=1)
        tot = jnp.concatenate(
            [
                jnp.broadcast_to(jnp.sum(col[:, j : j + BC], axis=1, keepdims=True), (nb, BC))
                for j in range(0, width, BC)
            ],
            axis=1,
        )
        scale = jnp.sqrt(tot * 2.0**-24 + 1e-6).astype(jnp.bfloat16).astype(jnp.float32)
        inv = 0.015625 / scale
        for i in range(nb):
            part = p_ref[k, i * BR : (i + 1) * BR, :]
            level = jnp.clip(part * inv[i : i + 1, :], -TOP, TOP).astype(jnp.bfloat16)
            o_ref[k, i * BR : (i + 1) * BR, :] += level.astype(jnp.float32) * scale[i : i + 1, :]


def weight_gradient(xs, got):
    groups, ny, rows, tok = xs.shape
    cols = got.shape[2]
    return pl.pallas_call(
        grad_kernel,
        grid=(groups,),
        in_specs=[
            pl.BlockSpec((1, ny, rows, tok), lambda g: (g, 0, 0, 0)),
            pl.BlockSpec((1, rows + tok, cols), lambda g: (g, 0, 0)),
        ],
        out_specs=pl.BlockSpec((ny, rows, cols), lambda g: (0, 0, 0)),
        out_shape=jax.ShapeDtypeStruct((ny, rows, cols), jnp.float32),
        scratch_shapes=[pltpu.VMEM((ny, rows, cols), jnp.float32)],
        compiler_params=pltpu.CompilerParams(vmem_limit_bytes=48 * 2**20),
        cost_estimate=pl.CostEstimate(
            flops=8 * 2 * groups * ny * rows * tok * cols, bytes_accessed=2**23, transcendentals=0
        ),
    )(xs, got)


def product_kernel(x_ref, g_ref, d_ref, q_ref, dx_ref, acc):
    ny, n, rows, tok = x_ref.shape
    width = d_ref.shape[2]

    @pl.when(pl.program_id(0) == 0)
    def _():
        acc[...] = jnp.zeros_like(acc)

    w = g_ref[:, :rows, :].reshape(n * rows, width)
    for k in range(ny):
        x = x_ref[k].reshape(n * rows, tok)
        acc[k] += lax.dot_general(
            x, w, (((0,), (0,)), ((), ())), preferred_element_type=jnp.float32
        )
        terms = lax.dot_general(
            w, d_ref[k], (((1,), (1,)), ((), ())), preferred_element_type=jnp.float32
        )
        dx_ref[k] = terms.astype(jnp.bfloat16).reshape(n, rows, tok)

    @pl.when(pl.program_id(0) == pl.num_programs(0) - 1)
    def _():
        q_ref[...] = acc[...].astype(q_ref.dtype)


def products(x, got, d):
    ny, nz, rows, tok = x.shape
    width = d.shape[2]
    return pl.pallas_call(
        product_kernel,
        grid=(nz // STEP,),
        in_specs=[
            pl.BlockSpec((ny, STEP, rows, tok), lambda i: (0, i, 0, 0)),
            pl.BlockSpec((STEP, rows + tok, width), lambda i: (i, 0, 0)),
            pl.BlockSpec((ny, tok, width), lambda i: (0, 0, 0)),
        ],
        out_specs=[
            pl.BlockSpec((ny, tok, width), lambda i: (0, 0, 0)),
            pl.BlockSpec((ny, STEP, rows, tok), lambda i: (0, i, 0, 0)),
        ],
        out_shape=[
            jax.ShapeDtypeStruct((ny, tok, width), jnp.bfloat16),
            jax.ShapeDtypeStruct(x.shape, jnp.bfloat16),
        ],
        scratch_shapes=[pltpu.VMEM((ny, tok, width), jnp.float32)],
        compiler_params=pltpu.CompilerParams(vmem_limit_bytes=48 * 2**20),
        cost_estimate=pl.CostEstimate(
            flops=8 * 4 * ny * nz * rows * width * tok, bytes_accessed=2**23, transcendentals=0
        ),
    )(x, got, d)


def exchange(blocks, axis):
    n, me = lax.axis_size(axis), lax.axis_index(axis)
    parts = [lax.dynamic_index_in_dim(blocks, (me + d) % n, 0, keepdims=False) for d in range(n)]
    return [parts[0]] + [shift(parts[d], axis, d) for d in range(1, n)]


def total(parts):
    return sum(p.astype(jnp.float32) for p in parts).astype(jnp.bfloat16)


def swap_places(a):
    n = lax.axis_size("x")
    return lax.ppermute(a, ("y", "x"), [(i * n + j, j * n + i) for i in range(n) for j in range(n)])


def scatter_local(terms):
    core = lax.axis_index("core")
    mine = lax.dynamic_index_in_dim(terms, core, 1, keepdims=False)
    got = shift(lax.dynamic_index_in_dim(terms, 1 - core, 1, keepdims=False), "core", 1)
    return total(exchange(total([mine, got]), "x"))


def local(tokens, weight_values, weight_scales, out_cotangent):
    core = lax.axis_index("core")
    ny, nz = lax.axis_size("y"), lax.axis_size("z")
    rows, width = weight_values.shape
    tok = tokens.shape[0]
    half = rows // 2

    weights = (weight_values.astype(jnp.float32) * spread(weight_scales, BR, BC)).astype(jnp.bfloat16)
    got = lax.all_gather(jnp.concatenate([weights, out_cotangent]), "z", axis=0)
    cots = lax.all_gather(out_cotangent, "y", axis=0)

    tokens = tokens.T
    with jax.named_scope("token_slab"):
        parts = tokens.reshape(nz // 2, 2, half, tok)
        mine = lax.dynamic_index_in_dim(parts, core, 1, keepdims=False)
        other = shift(lax.dynamic_index_in_dim(parts, 1 - core, 1, keepdims=False), "core", 1)
        piece = jnp.where(core == 0, jnp.stack([mine, other]), jnp.stack([other, mine]))
        piece = piece.reshape(nz, half, tok)
        piece = lax.all_to_all(piece, "z", split_axis=0, concat_axis=0, tiled=True)
        slab = gather_local(piece).transpose(1, 0, 2, 3).reshape(nz, ny, rows, tok)
    with jax.named_scope("token_rows"):
        full = gather_local(swap_places(tokens)).reshape(ny, nz, rows, tok)

    partial_grad = weight_gradient(slab, got)
    weight_grad = lax.psum_scatter(partial_grad, "y", scatter_dimension=0, tiled=False)
    part, dx = products(after(full, partial_grad), got, cots)
    queries = total(exchange(part, "y"))
    dx = scatter_local(dx.reshape(lax.axis_size("x"), 2, -1, tok))
    token_grad = swap_places(dx).T
    return (queries, token_grad, weight_grad)


def solution(mesh):
    cube = Mesh(mesh.devices.reshape(4, 8, 4, 2), ("y", "z", "x", "core"))
    spec = P(("y", "z"), ("x", "core"))
    return jax.shard_map(
        local, mesh=cube, in_specs=(spec,) * 4, out_specs=(spec,) * 3, check_vma=False
    )
```

profile of v0, /device:TPU:7, one launch (start us, length us, event | category | flops | bytes accessed | tf_op | source)
XLA Modules:
  0.0 149.3 jit_solution(5248037008406532783)
XLA Ops:
  7.2 0.7 broadcast_in_dim.14
  7.9 0.3 broadcast_in_dim.15
  8.2 1.1 fusion.1
  9.4 0.8 pad_maximum_fusion
  10.4 0.8 collective-permute-start.1
  11.2 0.9 collective-permute-done.1
  12.2 17.4 %all_to_all.15 = bf16[8,96,128]{2,1,0:T(8,128)(2,1)S(1)} all-to-all(bf16[8,96,128]{2,1,0:T(8,128)(2,1)S(1)} %bitcast.54), channel_id=1, replica_groups=mesh['y'=4,'z'=8,'x'=4,'core'=2] {'z'}, dimensions={0} | all-to-all | bytes 393216 | tf_op jit(solution)/shard_map/token_slab/all_to_all | solution.py:181
  29.6 1.4 broadcast_in_dim.13
  31.0 6.5 %all-to-all-start.2 = ((bf16[8,8,96,128]{3,2,1,0:T(8,128)(2,1)}), bf16[8,8,96,128]{3,2,1,0:T(8,128)(2,1)S(1)}, u32[]{:S(2)}, u32[]{:S(2)}) async-start(bf16[8,8,96,128]{3,2,1,0:T(8,128)(2,1)} %broadcast_in_dim.13), calls=%async_computation.2 | async-start | bytes 3145728 | tf_op jit(solution)/shard_map/token_slab/all_to_all | solution.py:35
  37.6 4.7 %collective-permute-start = (bf16[768,128]{1,0:T(8,128)(2,1)S(1)}, bf16[768,128]{1,0:T(8,128)(2,1)S(1)}, u32[]{:S(2)}, u32[]{:S(2)}) collective-permute-start(bf16[768,128]{1,0:T(8,128)(2,1)S(1)} %bitcast.53), channel_id=1, source_target_pairs={{0,0},{2,64},{4,128},{6,192},{64,2},{66,66},{68,130},{70,194},{128... | collective-permute-start | bytes 589832 | tf_op jit(solution)/shard_map/token_rows/ppermute | solution.py:153
  42.3 24.6 %collective-permute-done = bf16[768,128]{1,0:T(8,128)(2,1)S(1)} collective-permute-done((bf16[768,128]{1,0:T(8,128)(2,1)S(1)}, bf16[768,128]{1,0:T(8,128)(2,1)S(1)}, u32[]{:S(2)}, u32[]{:S(2)}) %collective-permute-start) | collective-permute-done | bytes 196640 | tf_op jit(solution)/shard_map/token_rows/ppermute | solution.py:153
  66.9 1.5 %broadcast_in_dim.12 = bf16[8,768,128]{2,1,0:T(8,128)(2,1)} broadcast(bf16[768,128]{1,0:T(8,128)(2,1)S(1)} %collective-permute-done), dimensions={1,2} | broadcast | bytes 1769472 | tf_op jit(solution)/shard_map/token_rows/broadcast_in_dim | solution.py:40
  68.4 4.7 %all-to-all-start = ((bf16[8,768,128]{2,1,0:T(8,128)(2,1)}), bf16[8,768,128]{2,1,0:T(8,128)(2,1)S(1)}, u32[]{:S(2)}, u32[]{:S(2)}) async-start(bf16[8,768,128]{2,1,0:T(8,128)(2,1)} %broadcast_in_dim.12), calls=%async_computation | async-start | bytes 3145728 | tf_op jit(solution)/shard_map/token_rows/all_to_all | solution.py:35
  73.2 1.5 %copy.17 = bf16[8,8,96,128]{3,2,1,0:T(8,128)(2,1)S(1)} copy(bf16[8,8,96,128]{3,2,0,1:T(8,128)(2,1)} %bitcast.49) | data formatting | bytes 3145728 | tf_op jit(solution)/shard_map/token_slab/transpose | solution.py:182
  74.7 10.8 %shard_map.67 = f32[4,192,768]{2,1,0:T(8,128)} custom-call(bf16[8,4,192,128]{3,2,1,0:T(8,128)(2,1)S(1)} %bitcast.47, bf16[8,320,768]{2,1,0:T(8,128)(2,1)} %bitcast.58), custom_call_target="tpu_custom_call" | custom-call | flops 9663676416 | bytes 8388608 | tf_op jit(solution)/shard_map/pallas_call | solution.py:73
  85.5 13.9 %all-gather.1 = bf16[512,768]{1,0:T(8,128)(2,1)S(1)} all-gather(bf16[128,768]{1,0:T(8,128)(2,1)S(1)} %copy-done.1), channel_id=3, replica_groups=mesh['y'=4,'z'=8,'x'=4,'core'=2] {'y'}, dimensions={0}, use_global_device_ids=true | all-gather | bytes 983040 | tf_op jit(solution)/shard_map/all_gather | solution.py:172
  99.4 6.5 %shard_map.68 = (bf16[4,128,768]{2,1,0:T(8,128)(2,1)S(1)}, bf16[4,8,192,128]{3,2,1,0:T(8,128)(2,1)S(1)}) custom-call(bf16[4,8,192,128]{3,2,1,0:T(8,128)(2,1)S(1)} %bitcast.45, bf16[8,320,768]{2,1,0:T(8,128)(2,1)} %bitcast.59, bf16[4,128,768]{2,1,0:T(8,128)(2,1)S(1)} %bitcast.48), custom_call_target="tpu_custom_call" | custom-call | flops 19327352832 | bytes 8388608 | tf_op jit(solution)/shard_map/pallas_call | solution.py:117
  106.0 0.3 copy.19
  106.3 3.1 %collective-permute-start.5 = (bf16[4,768,128]{1,2,0:T(8,128)(2,1)S(1)}, bf16[4,768,128]{1,2,0:T(8,128)(2,1)}, u32[]{:S(2)}, u32[]{:S(2)}) collective-permute-start(bf16[4,768,128]{1,2,0:T(8,128)(2,1)S(1)} %bitcast.51), channel_id=1, source_target_pairs={{0,1},{1,0},{2,3},{3,2},{4,5},{5,4},{6,7},{7,6},{8,9},{9,8},{10,11... | collective-permute-start | bytes 2359304 | tf_op jit(solution)/shard_map/ppermute | solution.py:23
  109.4 0.3 copy.20
  109.6 1.8 %collective-permute-done.5 = bf16[4,768,128]{1,2,0:T(8,128)(2,1)} collective-permute-done((bf16[4,768,128]{1,2,0:T(8,128)(2,1)S(1)}, bf16[4,768,128]{1,2,0:T(8,128)(2,1)}, u32[]{:S(2)}, u32[]{:S(2)}) %collective-permute-start.5) | collective-permute-done | bytes 786464 | tf_op jit(solution)/shard_map/ppermute | solution.py:23
  111.4 1.3 fusion
  112.9 2.4 %collective-permute-start.7 = (bf16[768,128]{0,1:T(8,128)(2,1)S(1)}, bf16[768,128]{0,1:T(8,128)(2,1)S(1)}, u32[]{:S(2)}, u32[]{:S(2)}) collective-permute-start(bf16[768,128]{0,1:T(8,128)(2,1)S(1)} %get-tuple-element.13), channel_id=1, source_target_pairs={{0,4},{2,6},{4,0},{6,2},{1,5},{3,7},{5,1},{7,3},{8,12},{10,14},{12... | collective-permute-start | bytes 589832 | tf_op jit(solution)/shard_map/ppermute | solution.py:23
  115.4 2.4 %collective-permute-start.3 = (bf16[128,768]{1,0:T(8,128)(2,1)S(1)}, bf16[128,768]{1,0:T(8,128)(2,1)S(1)}, u32[]{:S(2)}, u32[]{:S(2)}) collective-permute-start(bf16[128,768]{1,0:T(8,128)(2,1)S(1)} %get-tuple-element.16), channel_id=1, source_target_pairs={{0,128},{64,192},{128,0},{192,64},{1,129},{65,193},{129,1},{193,65... | collective-permute-start | bytes 589832 | tf_op jit(solution)/shard_map/ppermute | solution.py:23
  117.8 1.1 collective-permute-done.6
  119.0 1.3 collective-permute-start.4
  120.3 0.3 collective-permute-done.7
  120.6 4.9 %collective-permute-done.8 = bf16[768,128]{0,1:T(8,128)(2,1)S(1)} collective-permute-done((bf16[768,128]{0,1:T(8,128)(2,1)S(1)}, bf16[768,128]{0,1:T(8,128)(2,1)S(1)}, u32[]{:S(2)}, u32[]{:S(2)}) %collective-permute-start.8) | collective-permute-done | bytes 196640 | tf_op jit(solution)/shard_map/ppermute | solution.py:23
  125.6 3.0 %collective-permute-start.9 = (bf16[768,128]{0,1:T(8,128)(2,1)S(1)}, bf16[768,128]{0,1:T(8,128)(2,1)S(1)}, u32[]{:S(2)}, u32[]{:S(2)}) collective-permute-start(bf16[768,128]{0,1:T(8,128)(2,1)S(1)} %fusion.4), channel_id=1, source_target_pairs={{0,0},{2,64},{4,128},{6,192},{64,2},{66,66},{68,130},{70,194},{128... | collective-permute-start | bytes 589832 | tf_op jit(solution)/shard_map/ppermute | solution.py:153
  128.7 0.8 fusion.7
  129.4 12.3 %collective-permute-done.9 = bf16[768,128]{0,1:T(8,128)(2,1)S(1)} collective-permute-done((bf16[768,128]{0,1:T(8,128)(2,1)S(1)}, bf16[768,128]{0,1:T(8,128)(2,1)S(1)}, u32[]{:S(2)}, u32[]{:S(2)}) %collective-permute-start.9) | collective-permute-done | bytes 196640 | tf_op jit(solution)/shard_map/ppermute | solution.py:153
  141.8 0.7 copy.24
  (27 shorter events, 0.8 us)
Async XLA Ops:
  7.2 2.2 %copy-start.1 = (bf16[128,768]{1,0:T(8,128)(2,1)S(1)}, bf16[128,768]{1,0:T(8,128)(2,1)}, u32[]{:S(2)}) copy-start(bf16[128,768]{1,0:T(8,128)(2,1)} %param.7) | copy-start | bytes 589828
  7.2 67.6 %all-gather.4.cloned.1.call-start = ((), (), s32[]{:S(2)}) async-start(), calls=%async_computation.5 | async-start | bytes 4423680 | tf_op jit(solution)/shard_map/all_gather | solution.py:171
  8.2 2.0 %copy-start.2 = (bf16[128,768]{1,0:T(8,128)(2,1)S(1)}, bf16[128,768]{1,0:T(8,128)(2,1)}, u32[]{:S(2)}) copy-start(bf16[128,768]{1,0:T(8,128)(2,1)} %param.4) | copy-start | bytes 589828
  10.4 1.7 %collective-permute-start.1 = (bf16[4,96,128]{2,1,0:T(8,128)(2,1)S(1)}, bf16[4,96,128]{2,1,0:T(8,128)(2,1)S(1)}, u32[]{:S(2)}, u32[]{:S(2)}) collective-permute-start(bf16[4,96,128]{2,1,0:T(8,128)(2,1)S(1)} %get-tuple-element.18), channel_id=1, source_target_pairs={{0,1},{1,0},{2,3},{3,2},{4,5},{5,4},{6,7},{7,6},{8,9},{9,8},{10,11... | collective-permute-start | bytes 294920 | tf_op jit(solution)/shard_map/token_slab/ppermute | solution.py:23
  31.0 35.9 %all-to-all-start.2 = ((bf16[8,8,96,128]{3,2,1,0:T(8,128)(2,1)}), bf16[8,8,96,128]{3,2,1,0:T(8,128)(2,1)S(1)}, u32[]{:S(2)}, u32[]{:S(2)}) async-start(bf16[8,8,96,128]{3,2,1,0:T(8,128)(2,1)} %broadcast_in_dim.13), calls=%async_computation.2 | async-start | bytes 3145728 | tf_op jit(solution)/shard_map/token_slab/all_to_all | solution.py:35
  37.6 29.4 %collective-permute-start = (bf16[768,128]{1,0:T(8,128)(2,1)S(1)}, bf16[768,128]{1,0:T(8,128)(2,1)S(1)}, u32[]{:S(2)}, u32[]{:S(2)}) collective-permute-start(bf16[768,128]{1,0:T(8,128)(2,1)S(1)} %bitcast.53), channel_id=1, source_target_pairs={{0,0},{2,64},{4,128},{6,192},{64,2},{66,66},{68,130},{70,194},{128... | collective-permute-start | bytes 589832 | tf_op jit(solution)/shard_map/token_rows/ppermute | solution.py:153
  66.9 6.2 %copy-start = (bf16[8,8,96,128]{3,2,1,0:T(8,128)(2,1)}, bf16[8,8,96,128]{3,2,1,0:T(8,128)(2,1)S(1)}, u32[]{:S(2)}) copy-start(bf16[8,8,96,128]{3,2,1,0:T(8,128)(2,1)S(1)} %all-to-all-done.2) | copy-start | bytes 4718596
  68.4 31.0 %all-to-all-start = ((bf16[8,768,128]{2,1,0:T(8,128)(2,1)}), bf16[8,768,128]{2,1,0:T(8,128)(2,1)S(1)}, u32[]{:S(2)}, u32[]{:S(2)}) async-start(bf16[8,768,128]{2,1,0:T(8,128)(2,1)} %broadcast_in_dim.12), calls=%async_computation | async-start | bytes 3145728 | tf_op jit(solution)/shard_map/token_rows/all_to_all | solution.py:35
  73.2 68.6 %reduce-scatter.2.cloned.1.call-start = ((), (), s32[]{:S(2)}) async-start(), calls=%async_computation.4 | async-start | bytes 2949120 | tf_op jit(solution)/shard_map/reduce_scatter | solution.py:187
  106.3 5.1 %collective-permute-start.5 = (bf16[4,768,128]{1,2,0:T(8,128)(2,1)S(1)}, bf16[4,768,128]{1,2,0:T(8,128)(2,1)}, u32[]{:S(2)}, u32[]{:S(2)}) collective-permute-start(bf16[4,768,128]{1,2,0:T(8,128)(2,1)S(1)} %bitcast.51), channel_id=1, source_target_pairs={{0,1},{1,0},{2,3},{3,2},{4,5},{5,4},{6,7},{7,6},{8,9},{9,8},{10,11... | collective-permute-start | bytes 2359304 | tf_op jit(solution)/shard_map/ppermute | solution.py:23
  112.8 6.2 %collective-permute-start.6 = (bf16[768,128]{0,1:T(8,128)(2,1)S(1)}, bf16[768,128]{0,1:T(8,128)(2,1)S(1)}, u32[]{:S(2)}, u32[]{:S(2)}) collective-permute-start(bf16[768,128]{0,1:T(8,128)(2,1)S(1)} %get-tuple-element.11), channel_id=1, source_target_pairs={{0,2},{2,4},{4,6},{6,0},{1,3},{3,5},{5,7},{7,1},{8,10},{10,12},{12... | collective-permute-start | bytes 589832 | tf_op jit(solution)/shard_map/ppermute | solution.py:23
  112.9 7.7 %collective-permute-start.7 = (bf16[768,128]{0,1:T(8,128)(2,1)S(1)}, bf16[768,128]{0,1:T(8,128)(2,1)S(1)}, u32[]{:S(2)}, u32[]{:S(2)}) collective-permute-start(bf16[768,128]{0,1:T(8,128)(2,1)S(1)} %get-tuple-element.13), channel_id=1, source_target_pairs={{0,4},{2,6},{4,0},{6,2},{1,5},{3,7},{5,1},{7,3},{8,12},{10,14},{12... | collective-permute-start | bytes 589832 | tf_op jit(solution)/shard_map/ppermute | solution.py:23
  115.3 10.2 %collective-permute-start.8 = (bf16[768,128]{0,1:T(8,128)(2,1)S(1)}, bf16[768,128]{0,1:T(8,128)(2,1)S(1)}, u32[]{:S(2)}, u32[]{:S(2)}) collective-permute-start(bf16[768,128]{0,1:T(8,128)(2,1)S(1)} %get-tuple-element.12), channel_id=1, source_target_pairs={{0,6},{2,0},{4,2},{6,4},{1,7},{3,1},{5,3},{7,5},{8,14},{10,8},{12,... | collective-permute-start | bytes 589832 | tf_op jit(solution)/shard_map/ppermute | solution.py:23
  115.3 13.3 %collective-permute-start.2 = (bf16[128,768]{1,0:T(8,128)(2,1)S(1)}, bf16[128,768]{1,0:T(8,128)(2,1)S(1)}, u32[]{:S(2)}, u32[]{:S(2)}) collective-permute-start(bf16[128,768]{1,0:T(8,128)(2,1)S(1)} %get-tuple-element.14), channel_id=1, source_target_pairs={{0,64},{64,128},{128,192},{192,0},{1,65},{65,129},{129,193},{193,1... | collective-permute-start | bytes 589832 | tf_op jit(solution)/shard_map/ppermute | solution.py:23
  115.4 13.2 %collective-permute-start.3 = (bf16[128,768]{1,0:T(8,128)(2,1)S(1)}, bf16[128,768]{1,0:T(8,128)(2,1)S(1)}, u32[]{:S(2)}, u32[]{:S(2)}) collective-permute-start(bf16[128,768]{1,0:T(8,128)(2,1)S(1)} %get-tuple-element.16), channel_id=1, source_target_pairs={{0,128},{64,192},{128,0},{192,64},{1,129},{65,193},{129,1},{193,65... | collective-permute-start | bytes 589832 | tf_op jit(solution)/shard_map/ppermute | solution.py:23
  119.0 9.7 %collective-permute-start.4 = (bf16[128,768]{1,0:T(8,128)(2,1)S(1)}, bf16[128,768]{1,0:T(8,128)(2,1)S(1)}, u32[]{:S(2)}, u32[]{:S(2)}) collective-permute-start(bf16[128,768]{1,0:T(8,128)(2,1)S(1)} %get-tuple-element.15), channel_id=1, source_target_pairs={{0,192},{64,0},{128,64},{192,128},{1,193},{65,1},{129,65},{193,129... | collective-permute-start | bytes 589832 | tf_op jit(solution)/shard_map/ppermute | solution.py:23
  125.6 16.1 %collective-permute-start.9 = (bf16[768,128]{0,1:T(8,128)(2,1)S(1)}, bf16[768,128]{0,1:T(8,128)(2,1)S(1)}, u32[]{:S(2)}, u32[]{:S(2)}) collective-permute-start(bf16[768,128]{0,1:T(8,128)(2,1)S(1)} %fusion.4), channel_id=1, source_target_pairs={{0,0},{2,64},{4,128},{6,192},{64,2},{66,66},{68,130},{70,194},{128... | collective-permute-start | bytes 589832 | tf_op jit(solution)/shard_map/ppermute | solution.py:153
Sparse Core Ops, SparseCore 0:
  10.4 55.8 all-gather.3
  85.6 32.3 reduce-scatter.1
where the time goes:
time: 150 us; the launch traced here: 149 us
  waiting for transfers between devices  46.1 us (31%)
  blocking collectives  31.3 us (21%)
  starting transfers between devices  29.1 us (19%)
  Pallas kernels  17.3 us (12%)
  between operations  14.2 us (9%)
  local copies, waits for them, and re-layouts  7.1 us (5%)
  other arithmetic  4.18 us (3%)
    ppermute x2, waiting for transfers between devices, swap_places(): lax.ppermute(a, ('y', 'x'), [(i * n + j, j * n + i) for i in range(n) for...  37 us
    all_to_all x1, blocking collectives, local(): piece = lax.all_to_all(piece, 'z', split_axis=0, concat_axis=0, tiled=True)  17.4 us
    all_gather x1, blocking collectives, local(): cots = lax.all_gather(out_cotangent, 'y', axis=0)  13.9 us
    all_to_all x2, starting transfers between devices, swap_local(): lax.all_to_all(a, ('x', 'core'), split_axis=0, concat_axis=0, tiled=True)  11.3 us
    pallas_call x1, Pallas kernels, weight_gradient(): pl.pallas_call(grad_kernel, grid=(groups,), in_specs=[pl.BlockSpec((1, ny...  10.8 us
    ppermute x8, starting transfers between devices, shift(): return lax.ppermute(a, axis, [(i, (i + step) % n) for i in range(n)])  10.1 us
    ppermute x8, waiting for transfers between devices, shift(): return lax.ppermute(a, axis, [(i, (i + step) % n) for i in range(n)])  9.07 us
    ppermute x2, starting transfers between devices, swap_places(): lax.ppermute(a, ('y', 'x'), [(i * n + j, j * n + i) for i in range(n) for...  7.71 us
  transfers between devices with their start and end apart: 14, of which 7 were waited for; matrix products, arithmetic and copies ran while one was open for 5% of the time, Pallas kernels for 12%

commit v1 on v0

--- a/solution.py
+++ b/solution.py
@@ -40,16 +40,15 @@
     return swap_local(jnp.broadcast_to(own, (n,) + own.shape))
 
 
-def grad_kernel(x_ref, g_ref, o_ref, p_ref):
+def grad_kernel(x_ref, d_ref, o_ref, acc, p_ref):
     @pl.when(pl.program_id(0) == 0)
     def _():
-        o_ref[...] = jnp.zeros_like(o_ref)
+        acc[...] = jnp.zeros_like(acc)
 
-    ny, rows, width = o_ref.shape
+    nz, rows, width = o_ref.shape
     nb = rows // BR
-    d = g_ref[0, rows:, :]
-    for k in range(ny):
-        p_ref[k] = jnp.dot(x_ref[0, k], d, preferred_element_type=jnp.float32)
+    for k in range(nz):
+        p_ref[k] = jnp.dot(x_ref[0, k], d_ref[0], preferred_element_type=jnp.float32)
         p = p_ref[k].reshape(nb, BR, width)
         col = jnp.sum(p * p, axis=1)
         tot = jnp.concatenate(
@@ -64,27 +63,31 @@
         for i in range(nb):
             part = p_ref[k, i * BR : (i + 1) * BR, :]
             level = jnp.clip(part * inv[i : i + 1, :], -TOP, TOP).astype(jnp.bfloat16)
-            o_ref[k, i * BR : (i + 1) * BR, :] += level.astype(jnp.float32) * scale[i : i + 1, :]
+            acc[k, i * BR : (i + 1) * BR, :] += level.astype(jnp.float32) * scale[i : i + 1, :]
+
+    @pl.when(pl.program_id(0) == pl.num_programs(0) - 1)
+    def _():
+        o_ref[...] = acc[...].astype(o_ref.dtype)
 
 
-def weight_gradient(xs, got):
-    groups, ny, rows, tok = xs.shape
-    cols = got.shape[2]
+def weight_gradient(xs, cots):
+    groups, nz, rows, tok = xs.shape
+    cols = cots.shape[2]
     return pl.pallas_call(
         grad_kernel,
         grid=(groups,),
         in_specs=[
-            pl.BlockSpec((1, ny, rows, tok), lambda g: (g, 0, 0, 0)),
-            pl.BlockSpec((1, rows + tok, cols), lambda g: (g, 0, 0)),
+            pl.BlockSpec((1, nz, rows, tok), lambda g: (g, 0, 0, 0)),
+            pl.BlockSpec((1, tok, cols), lambda g: (g, 0, 0)),
         ],
-        out_specs=pl.BlockSpec((ny, rows, cols), lambda g: (0, 0, 0)),
-        out_shape=jax.ShapeDtypeStruct((ny, rows, cols), jnp.float32),
-        scratch_shapes=[pltpu.VMEM((ny, rows, cols), jnp.float32)],
+        out_specs=pl.BlockSpec((nz, rows, cols), lambda g: (0, 0, 0)),
+        out_shape=jax.ShapeDtypeStruct((nz, rows, cols), jnp.bfloat16),
+        scratch_shapes=[pltpu.VMEM((nz, rows, cols), jnp.float32)] * 2,
         compiler_params=pltpu.CompilerParams(vmem_limit_bytes=48 * 2**20),
         cost_estimate=pl.CostEstimate(
-            flops=8 * 2 * groups * ny * rows * tok * cols, bytes_accessed=2**23, transcendentals=0
+            flops=8 * 2 * groups * nz * rows * tok * cols, bytes_accessed=2**23, transcendentals=0
         ),
-    )(xs, got)
+    )(xs, cots)
 
 
 def product_kernel(x_ref, g_ref, d_ref, q_ref, dx_ref, acc):
@@ -95,7 +98,7 @@
     def _():
         acc[...] = jnp.zeros_like(acc)
 
-    w = g_ref[:, :rows, :].reshape(n * rows, width)
+    w = g_ref[...].reshape(n * rows, width)
     for k in range(ny):
         x = x_ref[k].reshape(n * rows, tok)
         acc[k] += lax.dot_general(
@@ -119,7 +122,7 @@
         grid=(nz // STEP,),
         in_specs=[
             pl.BlockSpec((ny, STEP, rows, tok), lambda i: (0, i, 0, 0)),
-            pl.BlockSpec((STEP, rows + tok, width), lambda i: (i, 0, 0)),
+            pl.BlockSpec((STEP, rows, width), lambda i: (i, 0, 0)),
             pl.BlockSpec((ny, tok, width), lambda i: (0, 0, 0)),
         ],
         out_specs=[
@@ -161,31 +164,20 @@
 
 
 def local(tokens, weight_values, weight_scales, out_cotangent):
-    core = lax.axis_index("core")
     ny, nz = lax.axis_size("y"), lax.axis_size("z")
-    rows, width = weight_values.shape
+    rows = weight_values.shape[0]
     tok = tokens.shape[0]
-    half = rows // 2
 
     weights = (weight_values.astype(jnp.float32) * spread(weight_scales, BR, BC)).astype(jnp.bfloat16)
-    got = lax.all_gather(jnp.concatenate([weights, out_cotangent]), "z", axis=0)
+    weights = lax.all_gather(weights, "z", axis=0)
     cots = lax.all_gather(out_cotangent, "y", axis=0)
+    full = gather_local(swap_places(tokens.T)).reshape(ny, nz, rows, tok)
 
-    tokens = tokens.T
-    with jax.named_scope("token_slab"):
-        parts = tokens.reshape(nz // 2, 2, half, tok)
-        mine = lax.dynamic_index_in_dim(parts, core, 1, keepdims=False)
-        other = shift(lax.dynamic_index_in_dim(parts, 1 - core, 1, keepdims=False), "core", 1)
-        piece = jnp.where(core == 0, jnp.stack([mine, other]), jnp.stack([other, mine]))
-        piece = piece.reshape(nz, half, tok)
-        piece = lax.all_to_all(piece, "z", split_axis=0, concat_axis=0, tiled=True)
-        slab = gather_local(piece).transpose(1, 0, 2, 3).reshape(nz, ny, rows, tok)
-    with jax.named_scope("token_rows"):
-        full = gather_local(swap_places(tokens)).reshape(ny, nz, rows, tok)
-
-    partial_grad = weight_gradient(slab, got)
-    weight_grad = lax.psum_scatter(partial_grad, "y", scatter_dimension=0, tiled=False)
-    part, dx = products(after(full, partial_grad), got, cots)
+    partial_grad = weight_gradient(full, cots)
+    weight_grad = lax.psum_scatter(partial_grad, "z", scatter_dimension=0, tiled=False)
+    weight_grad = weight_grad.astype(jnp.float32)
+    weights = after(weights, partial_grad)
+    part, dx = products(full, weights, cots)
     queries = total(exchange(part, "y"))
     dx = scatter_local(dx.reshape(lax.axis_size("x"), 2, -1, tok))
     token_grad = swap_places(dx).T

time: 150 us -> 116 us (0.77)
  the two profiles are of different devices: /device:TPU:7 before, /device:TPU:2 now
where the time goes in v1:
time: 116 us
  waiting for transfers between devices  38.4 us (33%)
  starting transfers between devices  24.1 us (21%)
  Pallas kernels  15.9 us (14%)
  between operations  14.2 us (12%)
  blocking collectives  13.5 us (12%)
  other arithmetic  5.83 us (5%)
  local copies, waits for them, and re-layouts  3.95 us (3%)
    all_gather x1, blocking collectives, local(): cots = lax.all_gather(out_cotangent, 'y', axis=0)  13.5 us
    ppermute x2, waiting for transfers between devices, swap_places(): lax.ppermute(a, ('y', 'x'), [(i * n + j, j * n + i) for i in range(n) for...  11.5 us
    all_to_all x1, starting transfers between devices, swap_local(): lax.all_to_all(a, ('x', 'core'), split_axis=0, concat_axis=0, tiled=True)  10.8 us
    ppermute x7, waiting for transfers between devices, shift(): return lax.ppermute(a, axis, [(i, (i + step) % n) for i in range(n)])  10.2 us
    reduce_scatter x1, waiting for transfers between devices, local(): lax.psum_scatter(partial_grad, 'z', scatter_dimension=0, tiled=False)  10.1 us
    pallas_call x1, Pallas kernels, weight_gradient(): pl.pallas_call(grad_kernel, grid=(groups,), in_specs=[pl.BlockSpec((1, nz...  9.54 us
    ppermute x2, starting transfers between devices, swap_places(): lax.ppermute(a, ('y', 'x'), [(i * n + j, j * n + i) for i in range(n) for...  6.74 us
    all_to_all x1, waiting for transfers between devices, swap_local(): lax.all_to_all(a, ('x', 'core'), split_axis=0, concat_axis=0, tiled=True)  6.57 us
  transfers between devices with their start and end apart: 12, of which 8 were waited for; matrix products, arithmetic and copies ran while one was open for 4% of the time, Pallas kernels for 14%

profile of v1, /device:TPU:2, one launch (start us, length us, event | category | flops | bytes accessed | tf_op | source)
XLA Modules:
  0.0 116.0 jit_solution(16146964542988768983)
XLA Ops:
  7.2 0.7 broadcast_in_dim.10
  7.9 0.3 broadcast_in_dim.11
  8.2 1.8 %fusion.1 = bf16[192,768]{1,0:T(8,128)(2,1)} fusion(f32[24,8,6,128]{3,2,1,0:T(8,128)S(1)} %bitcast.42, bf16[192,768]{1,0:T(8,128)(2,1)} %param.5), kind=kLoop, calls=%fused_computation.3 | loop fusion | flops 442368 | bytes 1179648 | tf_op jit(solution)/shard_map/convert_element_type | solution.py:171
  10.1 3.5 %collective-permute-start = (bf16[768,128]{0,1:T(8,128)(2,1)S(1)}, bf16[768,128]{0,1:T(8,128)(2,1)S(1)}, u32[]{:S(2)}, u32[]{:S(2)}) collective-permute-start(bf16[768,128]{0,1:T(8,128)(2,1)S(1)} %bitcast.47), channel_id=1, source_target_pairs={{0,0},{2,64},{4,128},{6,192},{64,2},{66,66},{68,130},{70,194},{128... | collective-permute-start | bytes 589832 | tf_op jit(solution)/shard_map/ppermute | solution.py:156
  13.5 6.8 %collective-permute-done = bf16[768,128]{0,1:T(8,128)(2,1)S(1)} collective-permute-done((bf16[768,128]{0,1:T(8,128)(2,1)S(1)}, bf16[768,128]{0,1:T(8,128)(2,1)S(1)}, u32[]{:S(2)}, u32[]{:S(2)}) %collective-permute-start) | collective-permute-done | bytes 196640 | tf_op jit(solution)/shard_map/ppermute | solution.py:156
  20.3 0.2 copy.10
  20.5 1.4 %broadcast_in_dim.9 = bf16[8,768,128]{2,1,0:T(8,128)(2,1)} broadcast(bf16[768,128]{1,0:T(8,128)(2,1)S(1)} %copy.10), dimensions={1,2} | broadcast | bytes 1769472 | tf_op jit(solution)/shard_map/broadcast_in_dim | solution.py:40
  21.8 10.8 %all-to-all-start = ((bf16[8,768,128]{2,1,0:T(8,128)(2,1)}), bf16[8,768,128]{2,1,0:T(8,128)(2,1)S(1)}, u32[]{:S(2)}, u32[]{:S(2)}) async-start(bf16[8,768,128]{2,1,0:T(8,128)(2,1)} %broadcast_in_dim.9), calls=%async_computation | async-start | bytes 3145728 | tf_op jit(solution)/shard_map/all_to_all | solution.py:35
  32.6 13.5 %all-gather.1 = bf16[512,768]{1,0:T(8,128)(2,1)S(1)} all-gather(bf16[128,768]{1,0:T(8,128)(2,1)S(1)} %copy-done), channel_id=3, replica_groups=mesh['y'=4,'z'=8,'x'=4,'core'=2] {'y'}, dimensions={0}, use_global_device_ids=true | all-gather | bytes 983040 | tf_op jit(solution)/shard_map/all_gather | solution.py:173
  46.1 6.6 %all-to-all-done = bf16[8,768,128]{2,1,0:T(8,128)(2,1)S(1)} async-done(((bf16[8,768,128]{2,1,0:T(8,128)(2,1)}), bf16[8,768,128]{2,1,0:T(8,128)(2,1)S(1)}, u32[]{:S(2)}, u32[]{:S(2)}) %all-to-all-start) | async-done | bytes 1572896 | tf_op jit(solution)/shard_map/all_to_all | solution.py:35
  52.7 9.5 %shard_map.67 = bf16[8,192,768]{2,1,0:T(8,128)(2,1)} custom-call(bf16[4,8,192,128]{3,2,1,0:T(8,128)(2,1)S(1)} %bitcast.37, bf16[4,128,768]{2,1,0:T(8,128)(2,1)S(1)} %bitcast.40), custom_call_target="tpu_custom_call" | custom-call | flops 9663676416 | bytes 8388608 | tf_op jit(solution)/shard_map/pallas_call | solution.py:76
  62.3 6.4 %shard_map.68 = (bf16[4,128,768]{2,1,0:T(8,128)(2,1)S(1)}, bf16[4,8,192,128]{3,2,1,0:T(8,128)(2,1)S(1)}) custom-call(bf16[4,8,192,128]{3,2,1,0:T(8,128)(2,1)S(1)} %bitcast.38, bf16[8,192,768]{2,1,0:T(8,128)(2,1)} %bitcast.46, bf16[4,128,768]{2,1,0:T(8,128)(2,1)S(1)} %bitcast.41), custom_call_target="tpu_custom_call" | custom-call | flops 19327352832 | bytes 8388608 | tf_op jit(solution)/shard_map/pallas_call | solution.py:120
  68.7 0.1 constant_dynamic-slice_fusion.1
  68.8 0.3 copy.12
  69.1 0.1 collective-permute-start.4
  69.3 0.3 copy.13
  69.6 2.1 %collective-permute-done.4 = bf16[4,768,128]{1,2,0:T(8,128)(2,1)} collective-permute-done((bf16[4,768,128]{1,2,0:T(8,128)(2,1)S(1)}, bf16[4,768,128]{1,2,0:T(8,128)(2,1)}, u32[]{:S(2)}, u32[]{:S(2)}) %collective-permute-start.4) | collective-permute-done | bytes 786464 | tf_op jit(solution)/shard_map/ppermute | solution.py:23
  71.6 1.3 %fusion = bf16[4,768,128]{1,2,0:T(8,128)(2,1)S(1)} fusion(bf16[4,768,128]{1,2,0:T(8,128)(2,1)} %collective-permute-done.4, bf16[4,1,768,128]{2,3,0,1:T(8,128)(2,1)S(1)} %copy.13), kind=kLoop, calls=%fused_computation.1 | loop fusion | flops 1572864 | bytes 2359296 | tf_op jit(solution)/shard_map/convert_element_type | solution.py:151
  73.0 1.5 %collective-permute-start.7 = (bf16[768,128]{0,1:T(8,128)(2,1)S(1)}, bf16[768,128]{0,1:T(8,128)(2,1)S(1)}, u32[]{:S(2)}, u32[]{:S(2)}) collective-permute-start(bf16[768,128]{0,1:T(8,128)(2,1)S(1)} %get-tuple-element.12), channel_id=1, source_target_pairs={{0,6},{2,0},{4,2},{6,4},{1,7},{3,1},{5,3},{7,5},{8,14},{10,8},{12,... | collective-permute-start | bytes 589832 | tf_op jit(solution)/shard_map/ppermute | solution.py:23
  74.5 0.1 collective-permute-start.6
  74.6 2.5 %collective-permute-start.5 = (bf16[768,128]{0,1:T(8,128)(2,1)S(1)}, bf16[768,128]{0,1:T(8,128)(2,1)S(1)}, u32[]{:S(2)}, u32[]{:S(2)}) collective-permute-start(bf16[768,128]{0,1:T(8,128)(2,1)S(1)} %get-tuple-element.11), channel_id=1, source_target_pairs={{0,2},{2,4},{4,6},{6,0},{1,3},{3,5},{5,7},{7,1},{8,10},{10,12},{12... | collective-permute-start | bytes 589832 | tf_op jit(solution)/shard_map/ppermute | solution.py:23
  77.2 2.3 %collective-permute-start.3 = (bf16[128,768]{1,0:T(8,128)(2,1)S(1)}, bf16[128,768]{1,0:T(8,128)(2,1)S(1)}, u32[]{:S(2)}, u32[]{:S(2)}) collective-permute-start(bf16[128,768]{1,0:T(8,128)(2,1)S(1)} %get-tuple-element.15), channel_id=1, source_target_pairs={{0,192},{64,0},{128,64},{192,128},{1,193},{65,1},{129,65},{193,129... | collective-permute-start | bytes 589832 | tf_op jit(solution)/shard_map/ppermute | solution.py:23
  79.5 4.7 %collective-permute-done.7 = bf16[768,128]{0,1:T(8,128)(2,1)S(1)} collective-permute-done((bf16[768,128]{0,1:T(8,128)(2,1)S(1)}, bf16[768,128]{0,1:T(8,128)(2,1)S(1)}, u32[]{:S(2)}, u32[]{:S(2)}) %collective-permute-start.7) | collective-permute-done | bytes 196640 | tf_op jit(solution)/shard_map/ppermute | solution.py:23
  84.2 1.8 %collective-permute-done.5 = bf16[768,128]{0,1:T(8,128)(2,1)S(1)} collective-permute-done((bf16[768,128]{0,1:T(8,128)(2,1)S(1)}, bf16[768,128]{0,1:T(8,128)(2,1)S(1)}, u32[]{:S(2)}, u32[]{:S(2)}) %collective-permute-start.5) | collective-permute-done | bytes 196640 | tf_op jit(solution)/shard_map/ppermute | solution.py:23
  86.1 0.1 fusion.4
  86.2 3.3 %collective-permute-start.8 = (bf16[768,128]{0,1:T(8,128)(2,1)S(1)}, bf16[768,128]{0,1:T(8,128)(2,1)S(1)}, u32[]{:S(2)}, u32[]{:S(2)}) collective-permute-start(bf16[768,128]{0,1:T(8,128)(2,1)S(1)} %fusion.4), channel_id=1, source_target_pairs={{0,0},{2,64},{4,128},{6,192},{64,2},{66,66},{68,130},{70,194},{128... | collective-permute-start | bytes 589832 | tf_op jit(solution)/shard_map/ppermute | solution.py:156
  89.5 1.6 %collective-permute-done.1 = bf16[128,768]{1,0:T(8,128)(2,1)S(1)} collective-permute-done((bf16[128,768]{1,0:T(8,128)(2,1)S(1)}, bf16[128,768]{1,0:T(8,128)(2,1)S(1)}, u32[]{:S(2)}, u32[]{:S(2)}) %collective-permute-start.1) | collective-permute-done | bytes 196640 | tf_op jit(solution)/shard_map/ppermute | solution.py:23
  91.1 0.8 fusion.7
  91.9 4.7 %collective-permute-done.8 = bf16[768,128]{0,1:T(8,128)(2,1)S(1)} collective-permute-done((bf16[768,128]{0,1:T(8,128)(2,1)S(1)}, bf16[768,128]{0,1:T(8,128)(2,1)S(1)}, u32[]{:S(2)}, u32[]{:S(2)}) %collective-permute-start.8) | collective-permute-done | bytes 196640 | tf_op jit(solution)/shard_map/ppermute | solution.py:156
  96.6 10.1 %reduce-scatter.2.cloned.1.call-done = bf16[1,192,768]{2,1,0:T(8,128)(2,1)} async-done(((bf16[8,192,768]{2,1,0:T(8,128)(2,1)}), bf16[1,192,768]{2,1,0:T(8,128)(2,1)}) %reduce-scatter.2.cloned.1.call-update) | async-done | bytes 294928 | tf_op jit(solution)/shard_map/reduce_scatter | solution.py:177
  106.7 1.8 %bitcast_convert_fusion = f32[192,768]{1,0:T(8,128)} fusion(bf16[1,192,768]{2,1,0:T(8,128)(2,1)} %reduce-scatter.2.cloned.1.call-done), kind=kLoop, calls=%fused_computation.12 | loop fusion | flops 147456 | bytes 884736 | tf_op jit(solution)/shard_map/convert_element_type | solution.py:178
  108.5 0.7 copy.17
  (16 shorter events, 0.2 us)
Async XLA Ops:
  7.2 2.9 %copy-start.1 = (bf16[128,768]{1,0:T(8,128)(2,1)S(1)}, bf16[128,768]{1,0:T(8,128)(2,1)}, u32[]{:S(2)}) copy-start(bf16[128,768]{1,0:T(8,128)(2,1)} %param.4) | copy-start | bytes 589828
  7.2 55.1 %all-gather.4.cloned.1.call-start = ((), (), s32[]{:S(2)}) async-start(), calls=%async_computation.3 | async-start | bytes 2654208 | tf_op jit(solution)/shard_map/all_gather | solution.py:172
  10.1 10.2 %collective-permute-start = (bf16[768,128]{0,1:T(8,128)(2,1)S(1)}, bf16[768,128]{0,1:T(8,128)(2,1)S(1)}, u32[]{:S(2)}, u32[]{:S(2)}) collective-permute-start(bf16[768,128]{0,1:T(8,128)(2,1)S(1)} %bitcast.47), channel_id=1, source_target_pairs={{0,0},{2,64},{4,128},{6,192},{64,2},{66,66},{68,130},{70,194},{128... | collective-permute-start | bytes 589832 | tf_op jit(solution)/shard_map/ppermute | solution.py:156
  21.8 10.8 %copy-start = (bf16[128,768]{1,0:T(8,128)(2,1)S(1)}, bf16[128,768]{1,0:T(8,128)(2,1)}, u32[]{:S(2)}) copy-start(bf16[128,768]{1,0:T(8,128)(2,1)} %param.7) | copy-start | bytes 589828
  21.8 30.9 %all-to-all-start = ((bf16[8,768,128]{2,1,0:T(8,128)(2,1)}), bf16[8,768,128]{2,1,0:T(8,128)(2,1)S(1)}, u32[]{:S(2)}, u32[]{:S(2)}) async-start(bf16[8,768,128]{2,1,0:T(8,128)(2,1)} %broadcast_in_dim.9), calls=%async_computation | async-start | bytes 3145728 | tf_op jit(solution)/shard_map/all_to_all | solution.py:35
  32.6 74.1 %reduce-scatter.2.cloned.1.call-start = ((), (), s32[]{:S(2)}) async-start(), calls=%async_computation.2 | async-start | bytes 2654208 | tf_op jit(solution)/shard_map/reduce_scatter | solution.py:177
  69.1 2.5 %collective-permute-start.4 = (bf16[4,768,128]{1,2,0:T(8,128)(2,1)S(1)}, bf16[4,768,128]{1,2,0:T(8,128)(2,1)}, u32[]{:S(2)}, u32[]{:S(2)}) collective-permute-start(bf16[4,768,128]{1,2,0:T(8,128)(2,1)S(1)} %bitcast.43), channel_id=1, source_target_pairs={{0,1},{1,0},{2,3},{3,2},{4,5},{5,4},{6,7},{7,6},{8,9},{9,8},{10,11... | collective-permute-start | bytes 2359304 | tf_op jit(solution)/shard_map/ppermute | solution.py:23
  73.0 11.2 %collective-permute-start.7 = (bf16[768,128]{0,1:T(8,128)(2,1)S(1)}, bf16[768,128]{0,1:T(8,128)(2,1)S(1)}, u32[]{:S(2)}, u32[]{:S(2)}) collective-permute-start(bf16[768,128]{0,1:T(8,128)(2,1)S(1)} %get-tuple-element.12), channel_id=1, source_target_pairs={{0,6},{2,0},{4,2},{6,4},{1,7},{3,1},{5,3},{7,5},{8,14},{10,8},{12,... | collective-permute-start | bytes 589832 | tf_op jit(solution)/shard_map/ppermute | solution.py:23
  74.5 9.7 %collective-permute-start.6 = (bf16[768,128]{0,1:T(8,128)(2,1)S(1)}, bf16[768,128]{0,1:T(8,128)(2,1)S(1)}, u32[]{:S(2)}, u32[]{:S(2)}) collective-permute-start(bf16[768,128]{0,1:T(8,128)(2,1)S(1)} %get-tuple-element.13), channel_id=1, source_target_pairs={{0,4},{2,6},{4,0},{6,2},{1,5},{3,7},{5,1},{7,3},{8,12},{10,14},{12... | collective-permute-start | bytes 589832 | tf_op jit(solution)/shard_map/ppermute | solution.py:23
  74.6 11.4 %collective-permute-start.5 = (bf16[768,128]{0,1:T(8,128)(2,1)S(1)}, bf16[768,128]{0,1:T(8,128)(2,1)S(1)}, u32[]{:S(2)}, u32[]{:S(2)}) collective-permute-start(bf16[768,128]{0,1:T(8,128)(2,1)S(1)} %get-tuple-element.11), channel_id=1, source_target_pairs={{0,2},{2,4},{4,6},{6,0},{1,3},{3,5},{5,7},{7,1},{8,10},{10,12},{12... | collective-permute-start | bytes 589832 | tf_op jit(solution)/shard_map/ppermute | solution.py:23
  77.2 12.3 %collective-permute-start.3 = (bf16[128,768]{1,0:T(8,128)(2,1)S(1)}, bf16[128,768]{1,0:T(8,128)(2,1)S(1)}, u32[]{:S(2)}, u32[]{:S(2)}) collective-permute-start(bf16[128,768]{1,0:T(8,128)(2,1)S(1)} %get-tuple-element.15), channel_id=1, source_target_pairs={{0,192},{64,0},{128,64},{192,128},{1,193},{65,1},{129,65},{193,129... | collective-permute-start | bytes 589832 | tf_op jit(solution)/shard_map/ppermute | solution.py:23
  79.5 10.0 %collective-permute-start.2 = (bf16[128,768]{1,0:T(8,128)(2,1)S(1)}, bf16[128,768]{1,0:T(8,128)(2,1)S(1)}, u32[]{:S(2)}, u32[]{:S(2)}) collective-permute-start(bf16[128,768]{1,0:T(8,128)(2,1)S(1)} %get-tuple-element.16), channel_id=1, source_target_pairs={{0,128},{64,192},{128,0},{192,64},{1,129},{65,193},{129,1},{193,65... | collective-permute-start | bytes 589832 | tf_op jit(solution)/shard_map/ppermute | solution.py:23
  84.2 6.9 %collective-permute-start.1 = (bf16[128,768]{1,0:T(8,128)(2,1)S(1)}, bf16[128,768]{1,0:T(8,128)(2,1)S(1)}, u32[]{:S(2)}, u32[]{:S(2)}) collective-permute-start(bf16[128,768]{1,0:T(8,128)(2,1)S(1)} %get-tuple-element.14), channel_id=1, source_target_pairs={{0,64},{64,128},{128,192},{192,0},{1,65},{65,129},{129,193},{193,1... | collective-permute-start | bytes 589832 | tf_op jit(solution)/shard_map/ppermute | solution.py:23
  86.2 10.5 %collective-permute-start.8 = (bf16[768,128]{0,1:T(8,128)(2,1)S(1)}, bf16[768,128]{0,1:T(8,128)(2,1)S(1)}, u32[]{:S(2)}, u32[]{:S(2)}) collective-permute-start(bf16[768,128]{0,1:T(8,128)(2,1)S(1)} %fusion.4), channel_id=1, source_target_pairs={{0,0},{2,64},{4,128},{6,192},{64,2},{66,66},{68,130},{70,194},{128... | collective-permute-start | bytes 589832 | tf_op jit(solution)/shard_map/ppermute | solution.py:156
Sparse Core Ops, SparseCore 0:
  10.4 44.5 all-gather.3
  62.4 44.2 reduce-scatter.1

commit v2 on v1

--- a/solution.py
+++ b/solution.py
@@ -107,7 +107,7 @@
         terms = lax.dot_general(
             w, d_ref[k], (((1,), (1,)), ((), ())), preferred_element_type=jnp.float32
         )
-        dx_ref[k] = terms.astype(jnp.bfloat16).reshape(n, rows, tok)
+        dx_ref[0, k] = terms.astype(jnp.bfloat16).reshape(n, rows, tok)
 
     @pl.when(pl.program_id(0) == pl.num_programs(0) - 1)
     def _():
@@ -117,6 +117,7 @@
 def products(x, got, d):
     ny, nz, rows, tok = x.shape
     width = d.shape[2]
+    steps = nz // STEP // 2
     return pl.pallas_call(
         product_kernel,
         grid=(nz // STEP,),
@@ -127,11 +128,11 @@
         ],
         out_specs=[
             pl.BlockSpec((ny, tok, width), lambda i: (0, 0, 0)),
-            pl.BlockSpec((ny, STEP, rows, tok), lambda i: (0, i, 0, 0)),
+            pl.BlockSpec((1, ny, STEP, rows, tok), lambda i: (i // steps, 0, i % steps, 0, 0)),
         ],
         out_shape=[
             jax.ShapeDtypeStruct((ny, tok, width), jnp.bfloat16),
-            jax.ShapeDtypeStruct(x.shape, jnp.bfloat16),
+            jax.ShapeDtypeStruct((2, ny, nz // 2, rows, tok), jnp.bfloat16),
         ],
         scratch_shapes=[pltpu.VMEM((ny, tok, width), jnp.float32)],
         compiler_params=pltpu.CompilerParams(vmem_limit_bytes=48 * 2**20),
@@ -142,45 +143,63 @@
 
 
 def exchange(blocks, axis):
-    n, me = lax.axis_size(axis), lax.axis_index(axis)
-    parts = [lax.dynamic_index_in_dim(blocks, (me + d) % n, 0, keepdims=False) for d in range(n)]
-    return [parts[0]] + [shift(parts[d], axis, d) for d in range(1, n)]
+    return [blocks[0]] + [shift(blocks[d], axis, d) for d in range(1, len(blocks))]
 
 
 def total(parts):
     return sum(p.astype(jnp.float32) for p in parts).astype(jnp.bfloat16)
 
 
-def swap_places(a):
+def around(a, k):
     n = lax.axis_size("x")
-    return lax.ppermute(a, ("y", "x"), [(i * n + j, j * n + i) for i in range(n) for j in range(n)])
-
-
-def scatter_local(terms):
+    pairs = [(i * n + j, j * n + (i + k) % n) for i in range(n) for j in range(n)]
+    return lax.ppermute(a, ("y", "x"), pairs)
+
+
+def sum_cores(terms):
     core = lax.axis_index("core")
-    mine = lax.dynamic_index_in_dim(terms, core, 1, keepdims=False)
-    got = shift(lax.dynamic_index_in_dim(terms, 1 - core, 1, keepdims=False), "core", 1)
-    return total(exchange(total([mine, got]), "x"))
+    mine = lax.dynamic_index_in_dim(terms, core, 0, keepdims=False)
+    got = shift(lax.dynamic_index_in_dim(terms, 1 - core, 0, keepdims=False), "core", 1)
+    return total([mine, got])
+
+
+def scatter_plane(terms):
+    x, y, n = lax.axis_index("x"), lax.axis_index("y"), lax.axis_size("x")
+    pick = lambda a, i: lax.dynamic_index_in_dim(a, i % n, 0, keepdims=False)
+    rows = jnp.stack(exchange([pick(terms, x - y - d) for d in range(n)], "y"))
+    return total(exchange([pick(rows, y - x - d) for d in range(n)], "x"))
 
 
 def local(tokens, weight_values, weight_scales, out_cotangent):
+    x, y = lax.axis_index("x"), lax.axis_index("y")
     ny, nz = lax.axis_size("y"), lax.axis_size("z")
     rows = weight_values.shape[0]
     tok = tokens.shape[0]
 
     weights = (weight_values.astype(jnp.float32) * spread(weight_scales, BR, BC)).astype(jnp.bfloat16)
     weights = lax.all_gather(weights, "z", axis=0)
-    cots = lax.all_gather(out_cotangent, "y", axis=0)
-    full = gather_local(swap_places(tokens.T)).reshape(ny, nz, rows, tok)
+    tokens = tokens.T
+    mine = [around(tokens, k) for k in range(ny)]
+    cots = [out_cotangent] + [shift(out_cotangent, "y", -d) for d in range(1, ny)]
+    *mine, c1, c2, c3 = together(*mine, *cots[1:])
+    cots = jnp.stack([out_cotangent, c1, c2, c3])
+    cots = jnp.stack([lax.dynamic_index_in_dim(cots, (x - k - y) % ny, 0, keepdims=False) for k in range(ny)])
+    mine = jnp.stack(mine)
+    other = shift(mine, "core", 1)
+    first = lax.axis_index("core") == 0
+    full = jnp.stack([jnp.where(first, mine, other), jnp.where(first, other, mine)], axis=1)
+    full = full.reshape(ny, nz, rows, tok)
 
     partial_grad = weight_gradient(full, cots)
     weight_grad = lax.psum_scatter(partial_grad, "z", scatter_dimension=0, tiled=False)
     weight_grad = weight_grad.astype(jnp.float32)
     weights = after(weights, partial_grad)
     part, dx = products(full, weights, cots)
+    dx = sum_cores(dx.reshape(2, ny, -1, tok))
+    part = after(part, dx)
+    part = [lax.dynamic_index_in_dim(part, (x - y - d) % ny, 0, keepdims=False) for d in range(ny)]
     queries = total(exchange(part, "y"))
-    dx = scatter_local(dx.reshape(lax.axis_size("x"), 2, -1, tok))
-    token_grad = swap_places(dx).T
+    token_grad = scatter_plane(dx).T
     return (queries, token_grad, weight_grad)
 
 

time: 116 us -> 109 us (0.940)
  blocking collectives: 13.5 us -> 0 us
  starting transfers between devices: 24.1 us -> 33.3 us
  waiting for transfers between devices: 38.4 us -> 32.4 us
  other arithmetic: 5.83 us -> 8.35 us
    ppermute x7 -> x14, starting transfers between devices: 6.57 us -> 23 us  [shift(): return lax.ppermute(a, axis, [(i, (i + step) % n) for i in range(n)])]
    ppermute x7 -> x14, waiting for transfers between devices: 10.2 us -> 24.6 us  [shift(): return lax.ppermute(a, axis, [(i, (i + step) % n) for i in range(n)])]
    all_gather x1 -> x0, blocking collectives: 13.5 us -> none  [local(): cots = lax.all_gather(out_cotangent, 'y', axis=0)]
    all_to_all x1 -> x0, starting transfers between devices: 10.8 us -> none  [swap_local(): lax.all_to_all(a, ('x', 'core'), split_axis=0, concat_axis=0, tiled=True)]
    ppermute x2 -> x4, waiting for transfers between devices: 11.5 us -> 0.87 us  [around(): return lax.ppermute(a, ('y', 'x'), pairs)]
    all_to_all x1 -> x0, waiting for transfers between devices: 6.57 us -> none  [swap_local(): lax.all_to_all(a, ('x', 'core'), split_axis=0, concat_axis=0, tiled=True)]
    reduce_scatter x1, waiting for transfers between devices: 10.1 us -> 6.25 us  [local(): lax.psum_scatter(partial_grad, 'z', scatter_dimension=0, tiled=False)]
    ppermute x2 -> x4, starting transfers between devices: 6.74 us -> 10.3 us  [around(): return lax.ppermute(a, ('y', 'x'), pairs)]
  transfers between devices with their start and end apart: 12 -> 20, of which waited for: 8 -> 14; matrix products, arithmetic and copies ran while one was open for 4% -> 7% of each run, Pallas kernels for 14% -> 15%
where the time goes in v2:
time: 109 us; the launch traced here: 108 us
  starting transfers between devices  33.3 us (31%)
  waiting for transfers between devices  32.4 us (30%)
  Pallas kernels  16.1 us (15%)
  between operations  14.4 us (13%)
  other arithmetic  8.35 us (8%)
  local copies, waits for them, and re-layouts  3.86 us (4%)
    ppermute x14, waiting for transfers between devices, shift(): return lax.ppermute(a, axis, [(i, (i + step) % n) for i in range(n)])  24.6 us
    ppermute x14, starting transfers between devices, shift(): return lax.ppermute(a, axis, [(i, (i + step) % n) for i in range(n)])  23 us
    ppermute x4, starting transfers between devices, around(): return lax.ppermute(a, ('y', 'x'), pairs)  10.3 us
    pallas_call x1, Pallas kernels, weight_gradient(): pl.pallas_call(grad_kernel, grid=(groups,), in_specs=[pl.BlockSpec((1, nz...  9.6 us
    pallas_call x1, Pallas kernels, products(): pl.pallas_call(product_kernel, grid=(nz // STEP,), in_specs=[pl.BlockSpec...  6.45 us
    reduce_scatter x1, waiting for transfers between devices, local(): lax.psum_scatter(partial_grad, 'z', scatter_dimension=0, tiled=False)  6.25 us
  transfers between devices with their start and end apart: 20, of which 14 were waited for; matrix products, arithmetic and copies ran while one was open for 7% of the time, Pallas kernels for 15%

profile of v2, /device:TPU:2, one launch (start us, length us, event | category | flops | bytes accessed | tf_op | source)
XLA Modules:
  0.0 108.4 jit_solution(3738911292115035251)
XLA Ops:
  7.2 0.8 broadcast_in_dim.6
  8.3 1.8 %fusion.1 = bf16[192,768]{1,0:T(8,128)(2,1)} fusion(f32[24,8,6,128]{3,2,1,0:T(8,128)S(1)} %bitcast.61, bf16[192,768]{1,0:T(8,128)(2,1)} %param.5), kind=kLoop, calls=%fused_computation.10 | loop fusion | flops 442368 | bytes 1179648 | tf_op jit(solution)/shard_map/convert_element_type | solution.py:179
  10.2 3.5 %collective-permute-start = (bf16[768,128]{0,1:T(8,128)(2,1)S(1)}, bf16[768,128]{0,1:T(8,128)(2,1)S(1)}, u32[]{:S(2)}, u32[]{:S(2)}) collective-permute-start(bf16[768,128]{0,1:T(8,128)(2,1)S(1)} %bitcast.80), channel_id=1, source_target_pairs={{0,0},{2,64},{4,128},{6,192},{64,2},{66,66},{68,130},{70,194},{128... | collective-permute-start | bytes 589832 | tf_op jit(solution)/shard_map/ppermute | solution.py:156
  13.7 2.6 %collective-permute-start.2 = (bf16[768,128]{0,1:T(8,128)(2,1)S(1)}, bf16[768,128]{0,1:T(8,128)(2,1)S(1)}, u32[]{:S(2)}, u32[]{:S(2)}) collective-permute-start(bf16[768,128]{0,1:T(8,128)(2,1)S(1)} %bitcast.82), channel_id=1, source_target_pairs={{0,4},{2,68},{4,132},{6,196},{64,6},{66,70},{68,134},{70,198},{128... | collective-permute-start | bytes 589832 | tf_op jit(solution)/shard_map/ppermute | solution.py:156
  16.3 4.2 %collective-permute-start.3 = (bf16[768,128]{0,1:T(8,128)(2,1)S(1)}, bf16[768,128]{0,1:T(8,128)(2,1)S(1)}, u32[]{:S(2)}, u32[]{:S(2)}) collective-permute-start(bf16[768,128]{0,1:T(8,128)(2,1)S(1)} %bitcast.83), channel_id=1, source_target_pairs={{0,6},{2,70},{4,134},{6,198},{64,0},{66,64},{68,128},{70,192},{128... | collective-permute-start | bytes 589832 | tf_op jit(solution)/shard_map/ppermute | solution.py:156
  21.2 5.9 %collective-permute-start.5 = (bf16[128,768]{1,0:T(8,128)(2,1)S(1)}, bf16[128,768]{1,0:T(8,128)(2,1)S(1)}, u32[]{:S(2)}, u32[]{:S(2)}) collective-permute-start(bf16[128,768]{1,0:T(8,128)(2,1)S(1)} %copy-done), channel_id=1, source_target_pairs={{0,128},{64,192},{128,0},{192,64},{1,129},{65,193},{129,1},{193,65... | collective-permute-start | bytes 589832 | tf_op jit(solution)/shard_map/ppermute | solution.py:23
  27.2 2.9 %collective-permute-start.6 = (bf16[128,768]{1,0:T(8,128)(2,1)S(1)}, bf16[128,768]{1,0:T(8,128)(2,1)S(1)}, u32[]{:S(2)}, u32[]{:S(2)}) collective-permute-start(bf16[128,768]{1,0:T(8,128)(2,1)S(1)} %copy-done), channel_id=1, source_target_pairs={{0,64},{64,128},{128,192},{192,0},{1,65},{65,129},{129,193},{193,1... | collective-permute-start | bytes 589832 | tf_op jit(solution)/shard_map/ppermute | solution.py:23
  30.1 0.9 collective-permute-done.3
  31.0 4.5 %collective-permute-done.4 = bf16[128,768]{1,0:T(8,128)(2,1)S(1)} collective-permute-done((bf16[128,768]{1,0:T(8,128)(2,1)S(1)}, bf16[128,768]{1,0:T(8,128)(2,1)S(1)}, u32[]{:S(2)}, u32[]{:S(2)}) %collective-permute-start.4) | collective-permute-done | bytes 196640 | tf_op jit(solution)/shard_map/ppermute | solution.py:23
  35.9 3.0 %collective-permute-done.6 = bf16[128,768]{1,0:T(8,128)(2,1)S(1)} collective-permute-done((bf16[128,768]{1,0:T(8,128)(2,1)S(1)}, bf16[128,768]{1,0:T(8,128)(2,1)S(1)}, u32[]{:S(2)}, u32[]{:S(2)}) %collective-permute-start.6) | collective-permute-done | bytes 196640 | tf_op jit(solution)/shard_map/ppermute | solution.py:23
  39.4 1.9 %collective-permute-done.7 = bf16[4,768,128]{1,2,0:T(8,128)(2,1)S(1)} collective-permute-done((bf16[4,768,128]{1,2,0:T(8,128)(2,1)S(1)}, bf16[4,768,128]{1,2,0:T(8,128)(2,1)S(1)}, u32[]{:S(2)}, u32[]{:S(2)}) %collective-permute-start.7) | collective-permute-done | bytes 786464 | tf_op jit(solution)/shard_map/ppermute | solution.py:23
  41.4 1.3 %pad_maximum_fusion = bf16[4,2,768,128]{2,3,0,1:T(8,128)(2,1)} fusion(bf16[4,1,768,128]{2,3,0,1:T(8,128)(2,1)S(1)} %get-tuple-element.28, bf16[4,1,768,128]{2,3,0,1:T(8,128)(2,1)S(1)} %get-tuple-element.27), kind=kLoop, calls=%fused_computation | loop fusion | flops 786432 | bytes 3145728 | tf_op jit(solution)/shard_map/stack | solution.py:190
  42.7 1.9 %copy.10 = bf16[4,2,768,128]{3,2,1,0:T(8,128)(2,1)S(1)} copy(bf16[4,2,768,128]{2,3,0,1:T(8,128)(2,1)} %pad_maximum_fusion) | data formatting | bytes 3145728 | tf_op jit(solution)/shard_map/stack | solution.py:190
  44.7 9.6 %shard_map.67 = bf16[8,192,768]{2,1,0:T(8,128)(2,1)} custom-call(bf16[4,8,192,128]{3,2,1,0:T(8,128)(2,1)S(1)} %bitcast.58, bf16[4,128,768]{2,1,0:T(8,128)(2,1)S(1)} %pad_maximum_fusion.3.d_ref), custom_call_target="tpu_custom_call" | custom-call | flops 9663676416 | bytes 8388608 | tf_op jit(solution)/shard_map/pallas_call | solution.py:76
  55.0 6.5 %shard_map.68 = (bf16[4,128,768]{2,1,0:T(8,128)(2,1)S(1)}, bf16[2,4,4,192,128]{4,3,2,1,0:T(8,128)(2,1)S(1)}) custom-call(bf16[4,8,192,128]{3,2,1,0:T(8,128)(2,1)S(1)} %bitcast.59, bf16[8,192,768]{2,1,0:T(8,128)(2,1)} %bitcast.79, bf16[4,128,768]{2,1,0:T(8,128)(2,1)S(1)} %pad_maximum_fusion.3.d_ref), custom_call_target="tpu_custom_call" | custom-call | flops 19327352832 | bytes 8388608 | tf_op jit(solution)/shard_map/pallas_call | solution.py:121
  62.3 2.1 %collective-permute-done.8 = bf16[4,768,128]{1,2,0:T(8,128)(2,1)} collective-permute-done((bf16[4,768,128]{1,2,0:T(8,128)(2,1)S(1)}, bf16[4,768,128]{1,2,0:T(8,128)(2,1)}, u32[]{:S(2)}, u32[]{:S(2)}) %collective-permute-start.8) | collective-permute-done | bytes 786464 | tf_op jit(solution)/shard_map/ppermute | solution.py:23
  64.3 1.3 %fusion = bf16[4,768,128]{1,2,0:T(8,128)(2,1)S(1)} fusion(bf16[4,768,128]{1,2,0:T(8,128)(2,1)} %collective-permute-done.8, bf16[1,4,768,128]{2,3,1,0:T(8,128)(2,1)S(1)} %copy.13), kind=kLoop, calls=%fused_computation.2 | loop fusion | flops 1572864 | bytes 2359296 | tf_op jit(solution)/shard_map/convert_element_type | solution.py:150
  65.7 1.9 %collective-permute-start.12 = (bf16[768,128]{0,1:T(8,128)(2,1)S(1)}, bf16[768,128]{0,1:T(8,128)(2,1)S(1)}, u32[]{:S(2)}, u32[]{:S(2)}) collective-permute-start(bf16[768,128]{0,1:T(8,128)(2,1)S(1)} %get-tuple-element.35), channel_id=1, source_target_pairs={{0,64},{64,128},{128,192},{192,0},{1,65},{65,129},{129,193},{193,1... | collective-permute-start | bytes 589832 | tf_op jit(solution)/shard_map/ppermute | solution.py:23
  67.6 2.6 %collective-permute-start.13 = (bf16[768,128]{0,1:T(8,128)(2,1)S(1)}, bf16[768,128]{0,1:T(8,128)(2,1)S(1)}, u32[]{:S(2)}, u32[]{:S(2)}) collective-permute-start(bf16[768,128]{0,1:T(8,128)(2,1)S(1)} %get-tuple-element.34), channel_id=1, source_target_pairs={{0,128},{64,192},{128,0},{192,64},{1,129},{65,193},{129,1},{193,65... | collective-permute-start | bytes 589832 | tf_op jit(solution)/shard_map/ppermute | solution.py:23
  70.2 1.4 %collective-permute-start.14 = (bf16[768,128]{0,1:T(8,128)(2,1)S(1)}, bf16[768,128]{0,1:T(8,128)(2,1)S(1)}, u32[]{:S(2)}, u32[]{:S(2)}) collective-permute-start(bf16[768,128]{0,1:T(8,128)(2,1)S(1)} %get-tuple-element.33), channel_id=1, source_target_pairs={{0,192},{64,0},{128,64},{192,128},{1,193},{65,1},{129,65},{193,129... | collective-permute-start | bytes 589832 | tf_op jit(solution)/shard_map/ppermute | solution.py:23
  72.3 2.7 %collective-permute-start.11 = (bf16[128,768]{1,0:T(8,128)(2,1)S(1)}, bf16[128,768]{1,0:T(8,128)(2,1)S(1)}, u32[]{:S(2)}, u32[]{:S(2)}) collective-permute-start(bf16[128,768]{1,0:T(8,128)(2,1)S(1)} %get-tuple-element.37), channel_id=1, source_target_pairs={{0,192},{64,0},{128,64},{192,128},{1,193},{65,1},{129,65},{193,129... | collective-permute-start | bytes 589832 | tf_op jit(solution)/shard_map/ppermute | solution.py:23
  75.3 4.9 %collective-permute-done.13 = bf16[768,128]{0,1:T(8,128)(2,1)S(1)} collective-permute-done((bf16[768,128]{0,1:T(8,128)(2,1)S(1)}, bf16[768,128]{0,1:T(8,128)(2,1)S(1)}, u32[]{:S(2)}, u32[]{:S(2)}) %collective-permute-start.13) | collective-permute-done | bytes 196640 | tf_op jit(solution)/shard_map/ppermute | solution.py:23
  80.4 1.7 %collective-permute-start.15 = (bf16[768,128]{0,1:T(8,128)(2,1)S(1)}, bf16[768,128]{0,1:T(8,128)(2,1)S(1)}, u32[]{:S(2)}, u32[]{:S(2)}) collective-permute-start(bf16[768,128]{0,1:T(8,128)(2,1)S(1)} %get-tuple-element.29), channel_id=1, source_target_pairs={{0,2},{2,4},{4,6},{6,0},{1,3},{3,5},{5,7},{7,1},{8,10},{10,12},{12... | collective-permute-start | bytes 589832 | tf_op jit(solution)/shard_map/ppermute | solution.py:23
  82.0 1.2 %collective-permute-start.16 = (bf16[768,128]{0,1:T(8,128)(2,1)S(1)}, bf16[768,128]{0,1:T(8,128)(2,1)S(1)}, u32[]{:S(2)}, u32[]{:S(2)}) collective-permute-start(bf16[768,128]{0,1:T(8,128)(2,1)S(1)} %get-tuple-element.31), channel_id=1, source_target_pairs={{0,4},{2,6},{4,0},{6,2},{1,5},{3,7},{5,1},{7,3},{8,12},{10,14},{12... | collective-permute-start | bytes 589832 | tf_op jit(solution)/shard_map/ppermute | solution.py:23
  83.2 1.2 %collective-permute-done.10 = bf16[128,768]{1,0:T(8,128)(2,1)S(1)} collective-permute-done((bf16[128,768]{1,0:T(8,128)(2,1)S(1)}, bf16[128,768]{1,0:T(8,128)(2,1)S(1)}, u32[]{:S(2)}, u32[]{:S(2)}) %collective-permute-start.10) | collective-permute-done | bytes 196640 | tf_op jit(solution)/shard_map/ppermute | solution.py:23
  84.4 0.8 collective-permute-start.17
  85.2 2.2 %collective-permute-done.11 = bf16[128,768]{1,0:T(8,128)(2,1)S(1)} collective-permute-done((bf16[128,768]{1,0:T(8,128)(2,1)S(1)}, bf16[128,768]{1,0:T(8,128)(2,1)S(1)}, u32[]{:S(2)}, u32[]{:S(2)}) %collective-permute-start.11) | collective-permute-done | bytes 196640 | tf_op jit(solution)/shard_map/ppermute | solution.py:23
  87.7 0.8 fusion.7
  88.5 2.2 %collective-permute-done.16 = bf16[768,128]{0,1:T(8,128)(2,1)S(1)} collective-permute-done((bf16[768,128]{0,1:T(8,128)(2,1)S(1)}, bf16[768,128]{0,1:T(8,128)(2,1)S(1)}, u32[]{:S(2)}, u32[]{:S(2)}) %collective-permute-start.16) | collective-permute-done | bytes 196640 | tf_op jit(solution)/shard_map/ppermute | solution.py:23
  90.8 1.9 %collective-permute-done.17 = bf16[768,128]{0,1:T(8,128)(2,1)S(1)} collective-permute-done((bf16[768,128]{0,1:T(8,128)(2,1)S(1)}, bf16[768,128]{0,1:T(8,128)(2,1)S(1)}, u32[]{:S(2)}, u32[]{:S(2)}) %collective-permute-start.17) | collective-permute-done | bytes 196640 | tf_op jit(solution)/shard_map/ppermute | solution.py:23
  93.5 6.2 %reduce-scatter.2.cloned.1.call-done = bf16[1,192,768]{2,1,0:T(8,128)(2,1)} async-done(((bf16[8,192,768]{2,1,0:T(8,128)(2,1)}), bf16[1,192,768]{2,1,0:T(8,128)(2,1)}) %reduce-scatter.2.cloned.1.call-update) | async-done | bytes 294928 | tf_op jit(solution)/shard_map/reduce_scatter | solution.py:194
  99.7 1.8 %bitcast_convert_fusion = f32[192,768]{1,0:T(8,128)} fusion(bf16[1,192,768]{2,1,0:T(8,128)(2,1)} %reduce-scatter.2.cloned.1.call-done), kind=kLoop, calls=%fused_computation.19 | loop fusion | flops 147456 | bytes 884736 | tf_op jit(solution)/shard_map/convert_element_type | solution.py:195
  (37 shorter events, 5.9 us)
Async XLA Ops:
  7.2 3.0 %copy-start.1 = (bf16[128,768]{1,0:T(8,128)(2,1)S(1)}, bf16[128,768]{1,0:T(8,128)(2,1)}, u32[]{:S(2)}) copy-start(bf16[128,768]{1,0:T(8,128)(2,1)} %param.4) | copy-start | bytes 589828
  7.2 13.3 %copy-start = (bf16[128,768]{1,0:T(8,128)(2,1)S(1)}, bf16[128,768]{1,0:T(8,128)(2,1)}, u32[]{:S(2)}) copy-start(bf16[128,768]{1,0:T(8,128)(2,1)} %param.7) | copy-start | bytes 589828
  7.2 47.8 %all-gather.3.cloned.1.call-start = ((), (), s32[]{:S(2)}) async-start(), calls=%async_computation.2 | async-start | bytes 2654208 | tf_op jit(solution)/shard_map/all_gather | solution.py:180
  10.1 89.6 %reduce-scatter.2.cloned.1.call-start = ((), (), s32[]{:S(2)}) async-start(), calls=%async_computation.1 | async-start | bytes 2654208 | tf_op jit(solution)/shard_map/reduce_scatter | solution.py:194
  10.2 11.0 %collective-permute-start = (bf16[768,128]{0,1:T(8,128)(2,1)S(1)}, bf16[768,128]{0,1:T(8,128)(2,1)S(1)}, u32[]{:S(2)}, u32[]{:S(2)}) collective-permute-start(bf16[768,128]{0,1:T(8,128)(2,1)S(1)} %bitcast.80), channel_id=1, source_target_pairs={{0,0},{2,64},{4,128},{6,192},{64,2},{66,66},{68,130},{70,194},{128... | collective-permute-start | bytes 589832 | tf_op jit(solution)/shard_map/ppermute | solution.py:156
  13.6 13.5 %collective-permute-start.1 = (bf16[768,128]{0,1:T(8,128)(2,1)S(1)}, bf16[768,128]{0,1:T(8,128)(2,1)S(1)}, u32[]{:S(2)}, u32[]{:S(2)}) collective-permute-start(bf16[768,128]{0,1:T(8,128)(2,1)S(1)} %bitcast.81), channel_id=1, source_target_pairs={{0,2},{2,66},{4,130},{6,194},{64,4},{66,68},{68,132},{70,196},{128... | collective-permute-start | bytes 589832 | tf_op jit(solution)/shard_map/ppermute | solution.py:156
  13.7 16.4 %collective-permute-start.2 = (bf16[768,128]{0,1:T(8,128)(2,1)S(1)}, bf16[768,128]{0,1:T(8,128)(2,1)S(1)}, u32[]{:S(2)}, u32[]{:S(2)}) collective-permute-start(bf16[768,128]{0,1:T(8,128)(2,1)S(1)} %bitcast.82), channel_id=1, source_target_pairs={{0,4},{2,68},{4,132},{6,196},{64,6},{66,70},{68,134},{70,198},{128... | collective-permute-start | bytes 589832 | tf_op jit(solution)/shard_map/ppermute | solution.py:156
  16.3 14.7 %collective-permute-start.3 = (bf16[768,128]{0,1:T(8,128)(2,1)S(1)}, bf16[768,128]{0,1:T(8,128)(2,1)S(1)}, u32[]{:S(2)}, u32[]{:S(2)}) collective-permute-start(bf16[768,128]{0,1:T(8,128)(2,1)S(1)} %bitcast.83), channel_id=1, source_target_pairs={{0,6},{2,70},{4,134},{6,198},{64,0},{66,64},{68,128},{70,192},{128... | collective-permute-start | bytes 589832 | tf_op jit(solution)/shard_map/ppermute | solution.py:156
  20.5 14.9 %collective-permute-start.4 = (bf16[128,768]{1,0:T(8,128)(2,1)S(1)}, bf16[128,768]{1,0:T(8,128)(2,1)S(1)}, u32[]{:S(2)}, u32[]{:S(2)}) collective-permute-start(bf16[128,768]{1,0:T(8,128)(2,1)S(1)} %copy-done), channel_id=1, source_target_pairs={{0,192},{64,0},{128,64},{192,128},{1,193},{65,1},{129,65},{193,129... | collective-permute-start | bytes 589832 | tf_op jit(solution)/shard_map/ppermute | solution.py:23
  21.2 14.6 %collective-permute-start.5 = (bf16[128,768]{1,0:T(8,128)(2,1)S(1)}, bf16[128,768]{1,0:T(8,128)(2,1)S(1)}, u32[]{:S(2)}, u32[]{:S(2)}) collective-permute-start(bf16[128,768]{1,0:T(8,128)(2,1)S(1)} %copy-done), channel_id=1, source_target_pairs={{0,128},{64,192},{128,0},{192,64},{1,129},{65,193},{129,1},{193,65... | collective-permute-start | bytes 589832 | tf_op jit(solution)/shard_map/ppermute | solution.py:23
  27.2 11.7 %collective-permute-start.6 = (bf16[128,768]{1,0:T(8,128)(2,1)S(1)}, bf16[128,768]{1,0:T(8,128)(2,1)S(1)}, u32[]{:S(2)}, u32[]{:S(2)}) collective-permute-start(bf16[128,768]{1,0:T(8,128)(2,1)S(1)} %copy-done), channel_id=1, source_target_pairs={{0,64},{64,128},{128,192},{192,0},{1,65},{65,129},{129,193},{193,1... | collective-permute-start | bytes 589832 | tf_op jit(solution)/shard_map/ppermute | solution.py:23
  38.9 2.4 %collective-permute-start.7 = (bf16[4,768,128]{1,2,0:T(8,128)(2,1)S(1)}, bf16[4,768,128]{1,2,0:T(8,128)(2,1)S(1)}, u32[]{:S(2)}, u32[]{:S(2)}) collective-permute-start(bf16[4,768,128]{1,2,0:T(8,128)(2,1)S(1)} %pad_maximum_fusion.1), channel_id=1, source_target_pairs={{0,1},{1,0},{2,3},{3,2},{4,5},{5,4},{6,7},{7,6},{8,9},{9,8},{10,11... | collective-permute-start | bytes 2359304 | tf_op jit(solution)/shard_map/ppermute | solution.py:23
  61.8 2.5 %collective-permute-start.8 = (bf16[4,768,128]{1,2,0:T(8,128)(2,1)S(1)}, bf16[4,768,128]{1,2,0:T(8,128)(2,1)}, u32[]{:S(2)}, u32[]{:S(2)}) collective-permute-start(bf16[4,768,128]{1,2,0:T(8,128)(2,1)S(1)} %bitcast.62), channel_id=1, source_target_pairs={{0,1},{1,0},{2,3},{3,2},{4,5},{5,4},{6,7},{7,6},{8,9},{9,8},{10,11... | collective-permute-start | bytes 2359304 | tf_op jit(solution)/shard_map/ppermute | solution.py:23
  65.7 9.3 %collective-permute-start.12 = (bf16[768,128]{0,1:T(8,128)(2,1)S(1)}, bf16[768,128]{0,1:T(8,128)(2,1)S(1)}, u32[]{:S(2)}, u32[]{:S(2)}) collective-permute-start(bf16[768,128]{0,1:T(8,128)(2,1)S(1)} %get-tuple-element.35), channel_id=1, source_target_pairs={{0,64},{64,128},{128,192},{192,0},{1,65},{65,129},{129,193},{193,1... | collective-permute-start | bytes 589832 | tf_op jit(solution)/shard_map/ppermute | solution.py:23
  67.6 12.6 %collective-permute-start.13 = (bf16[768,128]{0,1:T(8,128)(2,1)S(1)}, bf16[768,128]{0,1:T(8,128)(2,1)S(1)}, u32[]{:S(2)}, u32[]{:S(2)}) collective-permute-start(bf16[768,128]{0,1:T(8,128)(2,1)S(1)} %get-tuple-element.34), channel_id=1, source_target_pairs={{0,128},{64,192},{128,0},{192,64},{1,129},{65,193},{129,1},{193,65... | collective-permute-start | bytes 589832 | tf_op jit(solution)/shard_map/ppermute | solution.py:23
  70.2 10.0 %collective-permute-start.14 = (bf16[768,128]{0,1:T(8,128)(2,1)S(1)}, bf16[768,128]{0,1:T(8,128)(2,1)S(1)}, u32[]{:S(2)}, u32[]{:S(2)}) collective-permute-start(bf16[768,128]{0,1:T(8,128)(2,1)S(1)} %get-tuple-element.33), channel_id=1, source_target_pairs={{0,192},{64,0},{128,64},{192,128},{1,193},{65,1},{129,65},{193,129... | collective-permute-start | bytes 589832 | tf_op jit(solution)/shard_map/ppermute | solution.py:23
  71.6 12.7 %collective-permute-start.10 = (bf16[128,768]{1,0:T(8,128)(2,1)S(1)}, bf16[128,768]{1,0:T(8,128)(2,1)S(1)}, u32[]{:S(2)}, u32[]{:S(2)}) collective-permute-start(bf16[128,768]{1,0:T(8,128)(2,1)S(1)} %get-tuple-element.38), channel_id=1, source_target_pairs={{0,128},{64,192},{128,0},{192,64},{1,129},{65,193},{129,1},{193,65... | collective-permute-start | bytes 589832 | tf_op jit(solution)/shard_map/ppermute | solution.py:23
  72.3 15.1 %collective-permute-start.11 = (bf16[128,768]{1,0:T(8,128)(2,1)S(1)}, bf16[128,768]{1,0:T(8,128)(2,1)S(1)}, u32[]{:S(2)}, u32[]{:S(2)}) collective-permute-start(bf16[128,768]{1,0:T(8,128)(2,1)S(1)} %get-tuple-element.37), channel_id=1, source_target_pairs={{0,192},{64,0},{128,64},{192,128},{1,193},{65,1},{129,65},{193,129... | collective-permute-start | bytes 589832 | tf_op jit(solution)/shard_map/ppermute | solution.py:23
  75.0 12.7 %collective-permute-start.9 = (bf16[128,768]{1,0:T(8,128)(2,1)S(1)}, bf16[128,768]{1,0:T(8,128)(2,1)S(1)}, u32[]{:S(2)}, u32[]{:S(2)}) collective-permute-start(bf16[128,768]{1,0:T(8,128)(2,1)S(1)} %get-tuple-element.36), channel_id=1, source_target_pairs={{0,64},{64,128},{128,192},{192,0},{1,65},{65,129},{129,193},{193,1... | collective-permute-start | bytes 589832 | tf_op jit(solution)/shard_map/ppermute | solution.py:23
  80.4 8.1 %collective-permute-start.15 = (bf16[768,128]{0,1:T(8,128)(2,1)S(1)}, bf16[768,128]{0,1:T(8,128)(2,1)S(1)}, u32[]{:S(2)}, u32[]{:S(2)}) collective-permute-start(bf16[768,128]{0,1:T(8,128)(2,1)S(1)} %get-tuple-element.29), channel_id=1, source_target_pairs={{0,2},{2,4},{4,6},{6,0},{1,3},{3,5},{5,7},{7,1},{8,10},{10,12},{12... | collective-permute-start | bytes 589832 | tf_op jit(solution)/shard_map/ppermute | solution.py:23
  82.0 8.7 %collective-permute-start.16 = (bf16[768,128]{0,1:T(8,128)(2,1)S(1)}, bf16[768,128]{0,1:T(8,128)(2,1)S(1)}, u32[]{:S(2)}, u32[]{:S(2)}) collective-permute-start(bf16[768,128]{0,1:T(8,128)(2,1)S(1)} %get-tuple-element.31), channel_id=1, source_target_pairs={{0,4},{2,6},{4,0},{6,2},{1,5},{3,7},{5,1},{7,3},{8,12},{10,14},{12... | collective-permute-start | bytes 589832 | tf_op jit(solution)/shard_map/ppermute | solution.py:23
  84.4 8.3 %collective-permute-start.17 = (bf16[768,128]{0,1:T(8,128)(2,1)S(1)}, bf16[768,128]{0,1:T(8,128)(2,1)S(1)}, u32[]{:S(2)}, u32[]{:S(2)}) collective-permute-start(bf16[768,128]{0,1:T(8,128)(2,1)S(1)} %get-tuple-element.30), channel_id=1, source_target_pairs={{0,6},{2,0},{4,2},{6,4},{1,7},{3,1},{5,3},{7,5},{8,14},{10,8},{12,... | collective-permute-start | bytes 589832 | tf_op jit(solution)/shard_map/ppermute | solution.py:23
Sparse Core Ops, SparseCore 0:
  10.4 44.5 all-gather.2
  57.5 42.1 reduce-scatter.1

commit v3 on v2

v3 whole, which is shorter than its diff:
```python
import functools

import jax
import jax.numpy as jnp
from jax import lax
from jax.experimental import pallas as pl
from jax.experimental.pallas import tpu as pltpu
from jax.sharding import Mesh, PartitionSpec as P

BR = 32
BC = 128
TOP = 2.0
STEP = 2


def shift(a, axis, step):
    n = lax.axis_size(axis)
    return lax.ppermute(a, axis, [(i, (i + step) % n) for i in range(n)])


def together(*arrays):
    return lax.optimization_barrier(arrays)


def after(a, *others):
    return lax.optimization_barrier((a,) + others)[0]


def scale_kernel(v_ref, s_ref, o_ref):
    rows, width = v_ref.shape
    for i in range(0, rows, BR):
        for j in range(0, width, BC):
            scale = s_ref[i // BR : i // BR + 1, j // BC : j // BC + 1].astype(jnp.float32)
            value = v_ref[i : i + BR, j : j + BC].astype(jnp.float32)
            o_ref[i : i + BR, j : j + BC] = (value * scale).astype(o_ref.dtype)


def widen_kernel(a_ref, o_ref):
    o_ref[...] = a_ref[...].astype(o_ref.dtype)


def grad_kernel(core_ref, mine_ref, other_ref, d_ref, o_ref, acc, p_ref):
    @pl.when(pl.program_id(0) == 0)
    def _():
        acc[...] = jnp.zeros_like(acc)

    half, rows, width = o_ref.shape[0] // 2, *o_ref.shape[1:]
    nb = rows // BR
    for k in range(2 * half):
        x = (mine_ref if k < half else other_ref)[0, k % half]
        p_ref[k] = jnp.dot(x, d_ref[0], preferred_element_type=jnp.float32)
        p = p_ref[k].reshape(nb, BR, width)
        col = jnp.sum(p * p, axis=1)
        tot = jnp.concatenate(
            [
                jnp.broadcast_to(jnp.sum(col[:, j : j + BC], axis=1, keepdims=True), (nb, BC))
                for j in range(0, width, BC)
            ],
            axis=1,
        )
        scale = jnp.sqrt(tot * 2.0**-24 + 1e-6).astype(jnp.bfloat16).astype(jnp.float32)
        inv = 0.015625 / scale
        for i in range(nb):
            part = p_ref[k, i * BR : (i + 1) * BR, :]
            level = jnp.clip(part * inv[i : i + 1, :], -TOP, TOP).astype(jnp.bfloat16)
            acc[k, i * BR : (i + 1) * BR, :] += level.astype(jnp.float32) * scale[i : i + 1, :]

    @pl.when(pl.program_id(0) == pl.num_programs(0) - 1)
    def _():
        for r in range(2):
            at = lax.rem(core_ref[0] + r, 2) * half
            o_ref[pl.ds(at, half)] = acc[r * half : (r + 1) * half].astype(o_ref.dtype)


def weight_gradient(core, mine, other, cots):
    groups, half, rows, tok = mine.shape
    cols = cots.shape[2]
    whole = (2 * half, rows, cols)
    return pl.pallas_call(
        grad_kernel,
        grid_spec=pltpu.PrefetchScalarGridSpec(
            num_scalar_prefetch=1,
            grid=(groups,),
            in_specs=[
                pl.BlockSpec((1, half, rows, tok), lambda g, c: (g, 0, 0, 0)),
                pl.BlockSpec((1, half, rows, tok), lambda g, c: (g, 0, 0, 0)),
                pl.BlockSpec((1, tok, cols), lambda g, c: (g, 0, 0)),
            ],
            out_specs=pl.BlockSpec(whole, lambda g, c: (0, 0, 0)),
            scratch_shapes=[pltpu.VMEM(whole, jnp.float32)] * 2,
        ),
        out_shape=jax.ShapeDtypeStruct(whole, jnp.bfloat16),
        compiler_params=pltpu.CompilerParams(vmem_limit_bytes=48 * 2**20),
        cost_estimate=pl.CostEstimate(
            flops=16 * 2 * groups * half * rows * tok * cols, bytes_accessed=2**23, transcendentals=0
        ),
    )(core, mine, other, cots)


def terms_kernel(core_ref, w_ref, d_ref, dx_ref):
    n, rows, width = w_ref.shape
    ny, tok = d_ref.shape[:2]
    terms = lax.dot_general(
        w_ref[...].reshape(n * rows, width),
        d_ref[...].reshape(ny * tok, width),
        (((1,), (1,)), ((), ())),
        preferred_element_type=jnp.float32,
    ).astype(jnp.bfloat16)
    for k in range(ny):
        dx_ref[0, k] = terms[:, k * tok : (k + 1) * tok].reshape(n, rows, tok)


def query_kernel(core_ref, mine_ref, other_ref, w_ref, q_ref, acc):
    i = pl.program_id(0)
    n, rows, width = w_ref.shape
    ny, half, _, tok = mine_ref.shape
    steps = half // n

    @pl.when(i == 0)
    def _():
        acc[...] = jnp.zeros_like(acc)

    w = w_ref[...].reshape(n * rows, width)

    def add(x_ref, at):
        for k in range(ny):
            x = x_ref[k, at : at + n].reshape(n * rows, tok)
            acc[k] += lax.dot_general(
                x, w, (((0,), (0,)), ((), ())), preferred_element_type=jnp.float32
            )

    for s in range(2 * steps):
        pl.when(i == s)(functools.partial(add, mine_ref if s < steps else other_ref, s % steps * n))

    @pl.when(i == 2 * steps - 1)
    def _():
        q_ref[...] = acc[...].astype(q_ref.dtype)


def weight_blocks(rows, width, steps):
    return pl.BlockSpec(
        (STEP, rows, width), lambda i, c: (lax.rem(c[0] + i // steps, 2) * steps + i % steps, 0, 0)
    )


def gradient_terms(core, weights, cots):
    nz, rows, width = weights.shape
    ny, tok = cots.shape[:2]
    steps = nz // STEP // 2
    return pl.pallas_call(
        terms_kernel,
        grid_spec=pltpu.PrefetchScalarGridSpec(
            num_scalar_prefetch=1,
            grid=(2 * steps,),
            in_specs=[
                weight_blocks(rows, width, steps),
                pl.BlockSpec((ny, tok, width), lambda i, c: (0, 0, 0)),
            ],
            out_specs=pl.BlockSpec(
                (1, ny, STEP, rows, tok), lambda i, c: (i // steps, 0, i % steps, 0, 0)
            ),
        ),
        out_shape=jax.ShapeDtypeStruct((2, ny, nz // 2, rows, tok), jnp.bfloat16),
        compiler_params=pltpu.CompilerParams(vmem_limit_bytes=48 * 2**20),
        cost_estimate=pl.CostEstimate(
            flops=8 * 2 * ny * nz * rows * width * tok, bytes_accessed=2**22, transcendentals=0
        ),
    )(core, weights, cots)


def query_parts(core, mine, other, weights):
    nz, rows, width = weights.shape
    ny, half, _, tok = mine.shape
    steps = half // STEP
    tokens = pl.BlockSpec((ny, half, rows, tok), lambda i, c: (0, 0, 0, 0))
    return pl.pallas_call(
        query_kernel,
        grid_spec=pltpu.PrefetchScalarGridSpec(
            num_scalar_prefetch=1,
            grid=(2 * steps,),
            in_specs=[tokens, tokens, weight_blocks(rows, width, steps)],
            out_specs=pl.BlockSpec((ny, tok, width), lambda i, c: (0, 0, 0)),
            scratch_shapes=[pltpu.VMEM((ny, tok, width), jnp.float32)],
        ),
        out_shape=jax.ShapeDtypeStruct((ny, tok, width), jnp.bfloat16),
        compiler_params=pltpu.CompilerParams(vmem_limit_bytes=48 * 2**20),
        cost_estimate=pl.CostEstimate(
            flops=8 * 2 * ny * nz * rows * width * tok, bytes_accessed=2**22, transcendentals=0
        ),
    )(core, mine, other, weights)


def exchange(blocks, axis):
    return [blocks[0]] + [shift(blocks[d], axis, d) for d in range(1, len(blocks))]


def total(parts):
    return sum(p.astype(jnp.float32) for p in parts).astype(jnp.bfloat16)


def around(a, k):
    n = lax.axis_size("x")
    pairs = [(i * n + j, j * n + (i + k) % n) for i in range(n) for j in range(n)]
    return lax.ppermute(a, ("y", "x"), pairs)


def sum_cores(terms):
    return total([terms[0], shift(terms[1], "core", 1)])


def scatter_plane(terms):
    x, y, n = lax.axis_index("x"), lax.axis_index("y"), lax.axis_size("x")
    pick = lambda a, i: lax.dynamic_index_in_dim(a, i % n, 0, keepdims=False)
    rows = jnp.stack(exchange([pick(terms, x - y - d) for d in range(n)], "y"))
    return total(exchange([pick(rows, y - x - d) for d in range(n)], "x"))


def local(tokens, weight_values, weight_scales, out_cotangent):
    x, y = lax.axis_index("x"), lax.axis_index("y")
    core = lax.axis_index("core").astype(jnp.int32).reshape(1)
    ny, nz = lax.axis_size("y"), lax.axis_size("z")
    rows, width = weight_values.shape
    tok = tokens.shape[0]

    weights = pl.pallas_call(
        scale_kernel, out_shape=jax.ShapeDtypeStruct((rows, width), jnp.bfloat16)
    )(weight_values, weight_scales)
    weights = lax.all_gather(weights, "z", axis=0)
    tokens = tokens.T
    cots = [shift(out_cotangent, "y", -d) for d in range(1, ny)]
    mine = [around(tokens, k) for k in range(2)]
    tokens = after(tokens, cots[0])
    mine += [around(tokens, k) for k in range(2, ny)]
    *mine, c1, c2, c3 = together(*mine, *cots)
    cots = jnp.stack([out_cotangent, c1, c2, c3])
    cots = jnp.stack([lax.dynamic_index_in_dim(cots, (x - k - y) % ny, 0, keepdims=False) for k in range(ny)])
    mine = jnp.stack(mine).reshape(ny, nz // 2, rows, tok)
    other = shift(mine, "core", 1)

    partial_grad = weight_gradient(core, mine, other, cots)
    weight_grad = lax.psum_scatter(partial_grad, "z", scatter_dimension=0, tiled=False)
    weight_grad = pl.pallas_call(
        widen_kernel, out_shape=jax.ShapeDtypeStruct((rows, width), jnp.float32)
    )(weight_grad)
    weights = after(weights, partial_grad)
    dx = gradient_terms(core, weights, cots)
    part = query_parts(core, mine, other, after(weights, dx))
    dx = sum_cores(dx.reshape(2, ny, -1, tok))
    part = after(part, dx)
    part = [lax.dynamic_index_in_dim(part, (x - y - d) % ny, 0, keepdims=False) for d in range(ny)]
    queries = total(exchange(part, "y"))
    token_grad = scatter_plane(dx).T
    return (queries, token_grad, weight_grad)


def solution(mesh):
    cube = Mesh(mesh.devices.reshape(4, 8, 4, 2), ("y", "z", "x", "core"))
    spec = P(("y", "z"), ("x", "core"))
    return jax.shard_map(
        local, mesh=cube, in_specs=(spec,) * 4, out_specs=(spec,) * 3, check_vma=False
    )
```

time: 109 us -> 108 us (level)
  other arithmetic: 8.35 us -> 3.4 us
  waiting for transfers between devices: 32.4 us -> 36.3 us
  starting transfers between devices: 33.3 us -> 29.7 us
  local copies, waits for them, and re-layouts: 3.86 us -> 6.2 us
  Pallas kernels: 16.1 us -> 18.2 us
    ppermute x14, starting transfers between devices: 23 us -> 17.8 us  [shift(): return lax.ppermute(a, axis, [(i, (i + step) % n) for i in range(n)])]
    convert_element_type x2 -> x0, other arithmetic: 3.63 us -> none  [the longest x1 1.82 us: local(): (weight_values.astype(jnp.float32) * spread(weight_scales, BR, BC)).astyp...]
    ppermute x14, waiting for transfers between devices: 24.6 us -> 28 us  [shift(): return lax.ppermute(a, axis, [(i, (i + step) % n) for i in range(n)])]
    all_gather x1, waiting for transfers between devices: 0.66 us -> 3.55 us  [local(): weights = lax.all_gather(weights, 'z', axis=0)]
    pallas_call x2 -> x5, Pallas kernels: 16.1 us -> 18.2 us  [the longest x1 9.57 us: weight_gradient(): pl.pallas_call(grad_kernel, grid_spec=pltpu.PrefetchScalarGridSpec(num_sc...]
    another operation x1 -> x0, local copies, waits for them, and re-layouts: 1.91 us -> none  [local(): jnp.stack([jnp.where(first, mine, other), jnp.where(first, other, mine)],...]
    reduce_scatter x1, waiting for transfers between devices: 6.25 us -> 4.64 us  [local(): lax.psum_scatter(partial_grad, 'z', scatter_dimension=0, tiled=False)]
    ppermute x4, starting transfers between devices: 10.3 us -> 11.9 us  [around(): return lax.ppermute(a, ('y', 'x'), pairs)]
  transfers between devices with their start and end apart: 20 -> 20, of which waited for: 14 -> 12; matrix products, arithmetic and copies ran while one was open for 7% -> 7% of each run, Pallas kernels for 15% -> 13%
where the time goes in v3:
time: 108 us
  waiting for transfers between devices  36.3 us (34%)
  starting transfers between devices  29.7 us (28%)
  Pallas kernels  18.2 us (17%)
  between operations  14.3 us (13%)
  local copies, waits for them, and re-layouts  6.2 us (6%)
  other arithmetic  3.4 us (3%)
    ppermute x14, waiting for transfers between devices, shift(): return lax.ppermute(a, axis, [(i, (i + step) % n) for i in range(n)])  28 us
    ppermute x14, starting transfers between devices, shift(): return lax.ppermute(a, axis, [(i, (i + step) % n) for i in range(n)])  17.8 us
    ppermute x4, starting transfers between devices, around(): return lax.ppermute(a, ('y', 'x'), pairs)  11.9 us
    pallas_call x1, Pallas kernels, weight_gradient(): pl.pallas_call(grad_kernel, grid_spec=pltpu.PrefetchScalarGridSpec(num_sc...  9.57 us
    reduce_scatter x1, waiting for transfers between devices, local(): lax.psum_scatter(partial_grad, 'z', scatter_dimension=0, tiled=False)  4.64 us
    all_gather x1, waiting for transfers between devices, local(): weights = lax.all_gather(weights, 'z', axis=0)  3.55 us
    pallas_call x1, Pallas kernels, query_parts(): pl.pallas_call(query_kernel, grid_spec=pltpu.PrefetchScalarGridSpec(num_s...  2.77 us
    convert_element_type x2, other arithmetic, total(): return sum((p.astype(jnp.float32) for p in parts)).astype(jnp.bfloat16)  2.22 us
  transfers between devices with their start and end apart: 20, of which 12 were waited for; matrix products, arithmetic and copies ran while one was open for 7% of the time, Pallas kernels for 13%

profile of v3, /device:TPU:2, one launch (start us, length us, event | category | flops | bytes accessed | tf_op | source)
XLA Modules:
  0.0 108.0 jit_solution(10348605220632247570)
XLA Ops:
  7.2 1.8 %shard_map.67 = bf16[192,768]{1,0:T(8,128)(2,1)} custom-call(bf16[192,768]{1,0:T(8,128)(2,1)} %v_ref.1, bf16[6,6]{1,0:T(8,128)(2,1)} %s_ref.1), custom_call_target="tpu_custom_call" | custom-call | tf_op jit(solution)/shard_map/pallas_call | solution.py:225
  9.1 3.1 %collective-permute-start.2 = (bf16[128,768]{1,0:T(8,128)(2,1)}, bf16[128,768]{1,0:T(8,128)(2,1)S(1)}, u32[]{:S(2)}, u32[]{:S(2)}) collective-permute-start(bf16[128,768]{1,0:T(8,128)(2,1)} %param.7), channel_id=1, source_target_pairs={{0,192},{64,0},{128,64},{192,128},{1,193},{65,1},{129,65},{193,129... | collective-permute-start | bytes 589832 | tf_op jit(solution)/shard_map/ppermute | solution.py:18
  12.2 6.4 %collective-permute-start = (bf16[768,128]{0,1:T(8,128)(2,1)}, bf16[768,128]{0,1:T(8,128)(2,1)S(1)}, u32[]{:S(2)}, u32[]{:S(2)}) collective-permute-start(bf16[768,128]{0,1:T(8,128)(2,1)} %bitcast.61), channel_id=1, source_target_pairs={{0,0},{2,64},{4,128},{6,192},{64,2},{66,66},{68,130},{70,194},{128... | collective-permute-start | bytes 589832 | tf_op jit(solution)/shard_map/ppermute | solution.py:204
  18.7 2.5 %collective-permute-start.6 = (bf16[128,768]{1,0:T(8,128)(2,1)}, bf16[128,768]{1,0:T(8,128)(2,1)S(1)}, u32[]{:S(2)}, u32[]{:S(2)}) collective-permute-start(bf16[128,768]{1,0:T(8,128)(2,1)} %param.7), channel_id=1, source_target_pairs={{0,64},{64,128},{128,192},{192,0},{1,65},{65,129},{129,193},{193,1... | collective-permute-start | bytes 589832 | tf_op jit(solution)/shard_map/ppermute | solution.py:18
  21.2 3.0 %collective-permute-done.2 = bf16[128,768]{1,0:T(8,128)(2,1)S(1)} collective-permute-done((bf16[128,768]{1,0:T(8,128)(2,1)}, bf16[128,768]{1,0:T(8,128)(2,1)S(1)}, u32[]{:S(2)}, u32[]{:S(2)}) %collective-permute-start.2) | collective-permute-done | bytes 196640 | tf_op jit(solution)/shard_map/ppermute | solution.py:18
  24.1 5.5 %collective-permute-start.3 = (bf16[768,128]{0,1:T(8,128)(2,1)}, bf16[768,128]{0,1:T(8,128)(2,1)S(1)}, u32[]{:S(2)}, u32[]{:S(2)}) collective-permute-start(bf16[768,128]{0,1:T(8,128)(2,1)} %bitcast.63), channel_id=1, source_target_pairs={{0,4},{2,68},{4,132},{6,196},{64,6},{66,70},{68,134},{70,198},{128... | collective-permute-start | bytes 589832 | tf_op jit(solution)/shard_map/ppermute | solution.py:204
  29.7 7.6 %collective-permute-done.5 = bf16[128,768]{1,0:T(8,128)(2,1)S(1)} collective-permute-done((bf16[128,768]{1,0:T(8,128)(2,1)}, bf16[128,768]{1,0:T(8,128)(2,1)S(1)}, u32[]{:S(2)}, u32[]{:S(2)}) %collective-permute-start.5) | collective-permute-done | bytes 196640 | tf_op jit(solution)/shard_map/ppermute | solution.py:18
  37.2 1.4 %collective-permute-done.6 = bf16[128,768]{1,0:T(8,128)(2,1)S(1)} collective-permute-done((bf16[128,768]{1,0:T(8,128)(2,1)}, bf16[128,768]{1,0:T(8,128)(2,1)S(1)}, u32[]{:S(2)}, u32[]{:S(2)}) %collective-permute-start.6) | collective-permute-done | bytes 196640 | tf_op jit(solution)/shard_map/ppermute | solution.py:18
  39.9 1.9 %collective-permute-done.7.other_ref = bf16[4,4,192,128]{3,2,1,0:T(8,128)(2,1)S(1)} collective-permute-done((bf16[4,4,192,128]{3,2,1,0:T(8,128)(2,1)S(1)}, bf16[4,4,192,128]{3,2,1,0:T(8,128)(2,1)S(1)}, u32[]{:S(2)}, u32[]{:S(2)}) %collective-permute-start.7) | collective-permute-done | bytes 786464 | tf_op jit(solution)/shard_map/ppermute | solution.py:18
  41.8 9.6 %shard_map.68 = bf16[8,192,768]{2,1,0:T(8,128)(2,1)} custom-call(s32[1]{0:T(128)} %bitcast.core_ref, bf16[4,4,192,128]{3,2,1,0:T(8,128)(2,1)S(1)} %pad_maximum_fusion.mine_ref, bf16[4,4,192,128]{3,2,1,0:T(8,128)(2,1)S(1)} %collective-permute-done.7.other_ref, bf16[4,128,768]{2,1,0:T(8,128)(2,1)S(1)} %pad_maximum_fusion.2.d_ref), custom_call_target="tpu_custom_call" | custom-call | flops 9663676416 | bytes 8388608 | tf_op jit(solution)/shard_map/pallas_call | solution.py:79
  51.4 3.5 %all-gather.3.cloned.1.call-done = bf16[1536,768]{1,0:T(8,128)(2,1)} async-done(((bf16[192,768]{1,0:T(8,128)(2,1)}), bf16[1536,768]{1,0:T(8,128)(2,1)}) %all-gather.3.cloned.1.call-update) | async-done | bytes 2359312 | tf_op jit(solution)/shard_map/all_gather | solution.py:228
  54.9 1.7 %copy-done = bf16[1536,768]{1,0:T(8,128)(2,1)S(1)} copy-done((bf16[1536,768]{1,0:T(8,128)(2,1)S(1)}, bf16[1536,768]{1,0:T(8,128)(2,1)}, u32[]{:S(2)}) %copy-start) | copy-done | bytes 2359320
  56.6 2.2 %shard_map.69 = bf16[2,4,4,192,128]{4,3,2,1,0:T(8,128)(2,1)S(1)} custom-call(s32[1]{0:T(128)} %bitcast.core_ref, bf16[8,192,768]{2,1,0:T(8,128)(2,1)S(1)} %bitcast.44, bf16[4,128,768]{2,1,0:T(8,128)(2,1)S(1)} %pad_maximum_fusion.2.d_ref), custom_call_target="tpu_custom_call" | custom-call | flops 9663676416 | bytes 4194304 | tf_op jit(solution)/shard_map/pallas_call | solution.py:150
  58.8 1.1 fusion.7
  59.8 1.2 %copy.11 = bf16[4,768,128]{1,2,0:T(8,128)(2,1)} copy(bf16[4,768,128]{2,1,0:T(8,128)(2,1)S(1)} %bitcast.46) | data formatting | bytes 1572864 | tf_op jit(solution)/shard_map/squeeze | solution.py:208
  61.0 1.4 %copy.12 = f32[4,768,128]{1,2,0:T(8,128)S(1)} copy(bf16[4,768,128]{2,1,0:T(8,128)(2,1)} %bitcast.47) | data formatting | bytes 2359296 | tf_op jit(solution)/shard_map/convert_element_type | solution.py:198
  62.4 1.2 %collective-permute-done.8 = bf16[4,768,128]{1,2,0:T(8,128)(2,1)} collective-permute-done((bf16[4,768,128]{1,2,0:T(8,128)(2,1)}, bf16[4,768,128]{1,2,0:T(8,128)(2,1)}, u32[]{:S(2)}, u32[]{:S(2)}) %collective-permute-start.8) | collective-permute-done | bytes 786464 | tf_op jit(solution)/shard_map/ppermute | solution.py:18
  63.6 1.4 %add_convert_fusion = bf16[4,768,128]{1,2,0:T(8,128)(2,1)S(1)} fusion(f32[4,768,128]{1,2,0:T(8,128)S(1)} %copy.12, bf16[4,768,128]{1,2,0:T(8,128)(2,1)} %collective-permute-done.8), kind=kLoop, calls=%fused_computation | loop fusion | flops 1179648 | bytes 3145728 | tf_op jit(solution)/shard_map/convert_element_type | solution.py:198
  65.2 2.8 %collective-permute-start.14 = (bf16[768,128]{0,1:T(8,128)(2,1)S(1)}, bf16[768,128]{0,1:T(8,128)(2,1)S(1)}, u32[]{:S(2)}, u32[]{:S(2)}) collective-permute-start(bf16[768,128]{0,1:T(8,128)(2,1)S(1)} %get-tuple-element.31), channel_id=1, source_target_pairs={{0,192},{64,0},{128,64},{192,128},{1,193},{65,1},{129,65},{193,129... | collective-permute-start | bytes 589832 | tf_op jit(solution)/shard_map/ppermute | solution.py:18
  68.0 0.9 collective-permute-start.13
  69.7 2.8 %shard_map.70 = bf16[4,128,768]{2,1,0:T(8,128)(2,1)S(1)} custom-call(s32[1]{0:T(128)} %bitcast.core_ref, bf16[4,4,192,128]{3,2,1,0:T(8,128)(2,1)S(1)} %pad_maximum_fusion.mine_ref, bf16[4,4,192,128]{3,2,1,0:T(8,128)(2,1)S(1)} %collective-permute-done.7.other_ref, bf16[8,192,768]{2,1,0:T(8,128)(2,1)S(1)} %bitcast.45), custom_call_target="tpu_custom_call" | custom-call | flops 9663676416 | bytes 4194304 | tf_op jit(solution)/shard_map/pallas_call | solution.py:176
  72.5 1.9 %collective-permute-start.9 = (bf16[128,768]{1,0:T(8,128)(2,1)S(1)}, bf16[128,768]{1,0:T(8,128)(2,1)S(1)}, u32[]{:S(2)}, u32[]{:S(2)}) collective-permute-start(bf16[128,768]{1,0:T(8,128)(2,1)S(1)} %get-tuple-element.34), channel_id=1, source_target_pairs={{0,64},{64,128},{128,192},{192,0},{1,65},{65,129},{129,193},{193,1... | collective-permute-start | bytes 589832 | tf_op jit(solution)/shard_map/ppermute | solution.py:18
  74.4 1.4 %collective-permute-start.11 = (bf16[128,768]{1,0:T(8,128)(2,1)S(1)}, bf16[128,768]{1,0:T(8,128)(2,1)S(1)}, u32[]{:S(2)}, u32[]{:S(2)}) collective-permute-start(bf16[128,768]{1,0:T(8,128)(2,1)S(1)} %get-tuple-element.35), channel_id=1, source_target_pairs={{0,192},{64,0},{128,64},{192,128},{1,193},{65,1},{129,65},{193,129... | collective-permute-start | bytes 589832 | tf_op jit(solution)/shard_map/ppermute | solution.py:18
  75.8 1.6 %collective-permute-done.14 = bf16[768,128]{0,1:T(8,128)(2,1)S(1)} collective-permute-done((bf16[768,128]{0,1:T(8,128)(2,1)S(1)}, bf16[768,128]{0,1:T(8,128)(2,1)S(1)}, u32[]{:S(2)}, u32[]{:S(2)}) %collective-permute-start.14) | collective-permute-done | bytes 196640 | tf_op jit(solution)/shard_map/ppermute | solution.py:18
  77.4 3.0 %collective-permute-done.12 = bf16[768,128]{0,1:T(8,128)(2,1)S(1)} collective-permute-done((bf16[768,128]{0,1:T(8,128)(2,1)S(1)}, bf16[768,128]{0,1:T(8,128)(2,1)S(1)}, u32[]{:S(2)}, u32[]{:S(2)}) %collective-permute-start.12) | collective-permute-done | bytes 196640 | tf_op jit(solution)/shard_map/ppermute | solution.py:18
  80.6 1.5 %collective-permute-start.15 = (bf16[768,128]{0,1:T(8,128)(2,1)S(1)}, bf16[768,128]{0,1:T(8,128)(2,1)S(1)}, u32[]{:S(2)}, u32[]{:S(2)}) collective-permute-start(bf16[768,128]{0,1:T(8,128)(2,1)S(1)} %get-tuple-element.27), channel_id=1, source_target_pairs={{0,2},{2,4},{4,6},{6,0},{1,3},{3,5},{5,7},{7,1},{8,10},{10,12},{12... | collective-permute-start | bytes 589832 | tf_op jit(solution)/shard_map/ppermute | solution.py:18
  82.7 2.9 %collective-permute-done.9 = bf16[128,768]{1,0:T(8,128)(2,1)S(1)} collective-permute-done((bf16[128,768]{1,0:T(8,128)(2,1)S(1)}, bf16[128,768]{1,0:T(8,128)(2,1)S(1)}, u32[]{:S(2)}, u32[]{:S(2)}) %collective-permute-start.9) | collective-permute-done | bytes 196640 | tf_op jit(solution)/shard_map/ppermute | solution.py:18
  85.6 2.1 %collective-permute-start.16 = (bf16[768,128]{0,1:T(8,128)(2,1)S(1)}, bf16[768,128]{0,1:T(8,128)(2,1)S(1)}, u32[]{:S(2)}, u32[]{:S(2)}) collective-permute-start(bf16[768,128]{0,1:T(8,128)(2,1)S(1)} %get-tuple-element.29), channel_id=1, source_target_pairs={{0,4},{2,6},{4,0},{6,2},{1,5},{3,7},{5,1},{7,3},{8,12},{10,14},{12... | collective-permute-start | bytes 589832 | tf_op jit(solution)/shard_map/ppermute | solution.py:18
  87.7 1.1 %collective-permute-done.10 = bf16[128,768]{1,0:T(8,128)(2,1)S(1)} collective-permute-done((bf16[128,768]{1,0:T(8,128)(2,1)S(1)}, bf16[128,768]{1,0:T(8,128)(2,1)S(1)}, u32[]{:S(2)}, u32[]{:S(2)}) %collective-permute-start.10) | collective-permute-done | bytes 196640 | tf_op jit(solution)/shard_map/ppermute | solution.py:18
  89.6 4.4 %collective-permute-done.16 = bf16[768,128]{0,1:T(8,128)(2,1)S(1)} collective-permute-done((bf16[768,128]{0,1:T(8,128)(2,1)S(1)}, bf16[768,128]{0,1:T(8,128)(2,1)S(1)}, u32[]{:S(2)}, u32[]{:S(2)}) %collective-permute-start.16) | collective-permute-done | bytes 196640 | tf_op jit(solution)/shard_map/ppermute | solution.py:18
  94.7 4.6 %reduce-scatter.2.cloned.1.call-done = bf16[1,192,768]{2,1,0:T(8,128)(2,1)} async-done(((bf16[8,192,768]{2,1,0:T(8,128)(2,1)}), bf16[1,192,768]{2,1,0:T(8,128)(2,1)}) %reduce-scatter.2.cloned.1.call-update) | async-done | bytes 294928 | tf_op jit(solution)/shard_map/reduce_scatter | solution.py:241
  99.4 1.8 %shard_map.71 = f32[192,768]{1,0:T(8,128)} custom-call(bf16[192,768]{1,0:T(8,128)(2,1)} %bitcast.52), custom_call_target="tpu_custom_call" | custom-call | tf_op jit(solution)/shard_map/pallas_call | solution.py:242
  (39 shorter events, 4.5 us)
Async XLA Ops:
  7.2 47.8 %all-gather.3.cloned.1.call-start = ((), (), s32[]{:S(2)}) async-start(), calls=%async_computation.2 | async-start | bytes 2654208 | tf_op jit(solution)/shard_map/all_gather | solution.py:228
  9.1 90.3 %reduce-scatter.2.cloned.1.call-start = ((), (), s32[]{:S(2)}) async-start(), calls=%async_computation.1 | async-start | bytes 2654208 | tf_op jit(solution)/shard_map/reduce_scatter | solution.py:241
  9.1 15.0 %collective-permute-start.2 = (bf16[128,768]{1,0:T(8,128)(2,1)}, bf16[128,768]{1,0:T(8,128)(2,1)S(1)}, u32[]{:S(2)}, u32[]{:S(2)}) collective-permute-start(bf16[128,768]{1,0:T(8,128)(2,1)} %param.7), channel_id=1, source_target_pairs={{0,192},{64,0},{128,64},{192,128},{1,193},{65,1},{129,65},{193,129... | collective-permute-start | bytes 589832 | tf_op jit(solution)/shard_map/ppermute | solution.py:18
  12.2 27.4 %copy-start.2 = (bf16[128,768]{1,0:T(8,128)(2,1)S(1)}, bf16[128,768]{1,0:T(8,128)(2,1)}, u32[]{:S(2)}) copy-start(bf16[128,768]{1,0:T(8,128)(2,1)} %param.7) | copy-start | bytes 589828
  12.2 11.9 %collective-permute-start.1 = (bf16[768,128]{0,1:T(8,128)(2,1)}, bf16[768,128]{0,1:T(8,128)(2,1)S(1)}, u32[]{:S(2)}, u32[]{:S(2)}) collective-permute-start(bf16[768,128]{0,1:T(8,128)(2,1)} %bitcast.60), channel_id=1, source_target_pairs={{0,2},{2,66},{4,130},{6,194},{64,4},{66,68},{68,132},{70,196},{128... | collective-permute-start | bytes 589832 | tf_op jit(solution)/shard_map/ppermute | solution.py:204
  12.2 17.4 %collective-permute-start = (bf16[768,128]{0,1:T(8,128)(2,1)}, bf16[768,128]{0,1:T(8,128)(2,1)S(1)}, u32[]{:S(2)}, u32[]{:S(2)}) collective-permute-start(bf16[768,128]{0,1:T(8,128)(2,1)} %bitcast.61), channel_id=1, source_target_pairs={{0,0},{2,64},{4,128},{6,192},{64,2},{66,66},{68,130},{70,194},{128... | collective-permute-start | bytes 589832 | tf_op jit(solution)/shard_map/ppermute | solution.py:204
  18.6 18.7 %collective-permute-start.5 = (bf16[128,768]{1,0:T(8,128)(2,1)}, bf16[128,768]{1,0:T(8,128)(2,1)S(1)}, u32[]{:S(2)}, u32[]{:S(2)}) collective-permute-start(bf16[128,768]{1,0:T(8,128)(2,1)} %param.7), channel_id=1, source_target_pairs={{0,128},{64,192},{128,0},{192,64},{1,129},{65,193},{129,1},{193,65... | collective-permute-start | bytes 589832 | tf_op jit(solution)/shard_map/ppermute | solution.py:18
  18.7 19.9 %collective-permute-start.6 = (bf16[128,768]{1,0:T(8,128)(2,1)}, bf16[128,768]{1,0:T(8,128)(2,1)S(1)}, u32[]{:S(2)}, u32[]{:S(2)}) collective-permute-start(bf16[128,768]{1,0:T(8,128)(2,1)} %param.7), channel_id=1, source_target_pairs={{0,64},{64,128},{128,192},{192,0},{1,65},{65,129},{129,193},{193,1... | collective-permute-start | bytes 589832 | tf_op jit(solution)/shard_map/ppermute | solution.py:18
  24.1 14.5 %collective-permute-start.4 = (bf16[768,128]{0,1:T(8,128)(2,1)}, bf16[768,128]{0,1:T(8,128)(2,1)S(1)}, u32[]{:S(2)}, u32[]{:S(2)}) collective-permute-start(bf16[768,128]{0,1:T(8,128)(2,1)} %bitcast.62), channel_id=1, source_target_pairs={{0,6},{2,70},{4,134},{6,198},{64,0},{66,64},{68,128},{70,192},{128... | collective-permute-start | bytes 589832 | tf_op jit(solution)/shard_map/ppermute | solution.py:204
  24.1 14.5 %collective-permute-start.3 = (bf16[768,128]{0,1:T(8,128)(2,1)}, bf16[768,128]{0,1:T(8,128)(2,1)S(1)}, u32[]{:S(2)}, u32[]{:S(2)}) collective-permute-start(bf16[768,128]{0,1:T(8,128)(2,1)} %bitcast.63), channel_id=1, source_target_pairs={{0,4},{2,68},{4,132},{6,196},{64,6},{66,70},{68,134},{70,198},{128... | collective-permute-start | bytes 589832 | tf_op jit(solution)/shard_map/ppermute | solution.py:204
  39.4 2.4 %collective-permute-start.7 = (bf16[4,4,192,128]{3,2,1,0:T(8,128)(2,1)S(1)}, bf16[4,4,192,128]{3,2,1,0:T(8,128)(2,1)S(1)}, u32[]{:S(2)}, u32[]{:S(2)}) collective-permute-start(bf16[4,4,192,128]{3,2,1,0:T(8,128)(2,1)S(1)} %pad_maximum_fusion.mine_ref), channel_id=1, source_target_pairs={{0,1},{1,0},{2,3},{3,2},{4,5},{5,4},{6,7},{7,6},{8,9},{9,8},{10,11... | collective-permute-start | bytes 2359304 | tf_op jit(solution)/shard_map/ppermute | solution.py:18
  54.9 1.7 %copy-start = (bf16[1536,768]{1,0:T(8,128)(2,1)S(1)}, bf16[1536,768]{1,0:T(8,128)(2,1)}, u32[]{:S(2)}) copy-start(bf16[1536,768]{1,0:T(8,128)(2,1)} %all-gather.3.cloned.1.call-done) | copy-start | bytes 7077892
  61.0 2.6 %collective-permute-start.8 = (bf16[4,768,128]{1,2,0:T(8,128)(2,1)}, bf16[4,768,128]{1,2,0:T(8,128)(2,1)}, u32[]{:S(2)}, u32[]{:S(2)}) collective-permute-start(bf16[4,768,128]{1,2,0:T(8,128)(2,1)} %copy.11), channel_id=1, source_target_pairs={{0,1},{1,0},{2,3},{3,2},{4,5},{5,4},{6,7},{7,6},{8,9},{9,8},{10,11... | collective-permute-start | bytes 2359304 | tf_op jit(solution)/shard_map/ppermute | solution.py:18
  63.6 6.0 %copy-start.1 = (bf16[1536,768]{1,0:T(8,128)(2,1)S(1)}, bf16[1536,768]{1,0:T(8,128)(2,1)}, u32[]{:S(2)}) copy-start(bf16[1536,768]{1,0:T(8,128)(2,1)} %all-gather.3.cloned.1.call-done) | copy-start | bytes 7077892
  65.2 12.3 %collective-permute-start.14 = (bf16[768,128]{0,1:T(8,128)(2,1)S(1)}, bf16[768,128]{0,1:T(8,128)(2,1)S(1)}, u32[]{:S(2)}, u32[]{:S(2)}) collective-permute-start(bf16[768,128]{0,1:T(8,128)(2,1)S(1)} %get-tuple-element.31), channel_id=1, source_target_pairs={{0,192},{64,0},{128,64},{192,128},{1,193},{65,1},{129,65},{193,129... | collective-permute-start | bytes 589832 | tf_op jit(solution)/shard_map/ppermute | solution.py:18
  68.0 9.5 %collective-permute-start.13 = (bf16[768,128]{0,1:T(8,128)(2,1)S(1)}, bf16[768,128]{0,1:T(8,128)(2,1)S(1)}, u32[]{:S(2)}, u32[]{:S(2)}) collective-permute-start(bf16[768,128]{0,1:T(8,128)(2,1)S(1)} %get-tuple-element.32), channel_id=1, source_target_pairs={{0,128},{64,192},{128,0},{192,64},{1,129},{65,193},{129,1},{193,65... | collective-permute-start | bytes 589832 | tf_op jit(solution)/shard_map/ppermute | solution.py:18
  68.9 11.5 %collective-permute-start.12 = (bf16[768,128]{0,1:T(8,128)(2,1)S(1)}, bf16[768,128]{0,1:T(8,128)(2,1)S(1)}, u32[]{:S(2)}, u32[]{:S(2)}) collective-permute-start(bf16[768,128]{0,1:T(8,128)(2,1)S(1)} %get-tuple-element.33), channel_id=1, source_target_pairs={{0,64},{64,128},{128,192},{192,0},{1,65},{65,129},{129,193},{193,1... | collective-permute-start | bytes 589832 | tf_op jit(solution)/shard_map/ppermute | solution.py:18
  72.5 13.1 %collective-permute-start.9 = (bf16[128,768]{1,0:T(8,128)(2,1)S(1)}, bf16[128,768]{1,0:T(8,128)(2,1)S(1)}, u32[]{:S(2)}, u32[]{:S(2)}) collective-permute-start(bf16[128,768]{1,0:T(8,128)(2,1)S(1)} %get-tuple-element.34), channel_id=1, source_target_pairs={{0,64},{64,128},{128,192},{192,0},{1,65},{65,129},{129,193},{193,1... | collective-permute-start | bytes 589832 | tf_op jit(solution)/shard_map/ppermute | solution.py:18
  74.4 13.4 %collective-permute-start.11 = (bf16[128,768]{1,0:T(8,128)(2,1)S(1)}, bf16[128,768]{1,0:T(8,128)(2,1)S(1)}, u32[]{:S(2)}, u32[]{:S(2)}) collective-permute-start(bf16[128,768]{1,0:T(8,128)(2,1)S(1)} %get-tuple-element.35), channel_id=1, source_target_pairs={{0,192},{64,0},{128,64},{192,128},{1,193},{65,1},{129,65},{193,129... | collective-permute-start | bytes 589832 | tf_op jit(solution)/shard_map/ppermute | solution.py:18
  77.4 11.4 %collective-permute-start.10 = (bf16[128,768]{1,0:T(8,128)(2,1)S(1)}, bf16[128,768]{1,0:T(8,128)(2,1)S(1)}, u32[]{:S(2)}, u32[]{:S(2)}) collective-permute-start(bf16[128,768]{1,0:T(8,128)(2,1)S(1)} %get-tuple-element.36), channel_id=1, source_target_pairs={{0,128},{64,192},{128,0},{192,64},{1,129},{65,193},{129,1},{193,65... | collective-permute-start | bytes 589832 | tf_op jit(solution)/shard_map/ppermute | solution.py:18
  80.6 9.0 %collective-permute-start.15 = (bf16[768,128]{0,1:T(8,128)(2,1)S(1)}, bf16[768,128]{0,1:T(8,128)(2,1)S(1)}, u32[]{:S(2)}, u32[]{:S(2)}) collective-permute-start(bf16[768,128]{0,1:T(8,128)(2,1)S(1)} %get-tuple-element.27), channel_id=1, source_target_pairs={{0,2},{2,4},{4,6},{6,0},{1,3},{3,5},{5,7},{7,1},{8,10},{10,12},{12... | collective-permute-start | bytes 589832 | tf_op jit(solution)/shard_map/ppermute | solution.py:18
  82.1 7.4 %collective-permute-start.17 = (bf16[768,128]{0,1:T(8,128)(2,1)S(1)}, bf16[768,128]{0,1:T(8,128)(2,1)S(1)}, u32[]{:S(2)}, u32[]{:S(2)}) collective-permute-start(bf16[768,128]{0,1:T(8,128)(2,1)S(1)} %get-tuple-element.28), channel_id=1, source_target_pairs={{0,6},{2,0},{4,2},{6,4},{1,7},{3,1},{5,3},{7,5},{8,14},{10,8},{12,... | collective-permute-start | bytes 589832 | tf_op jit(solution)/shard_map/ppermute | solution.py:18
  85.6 8.3 %collective-permute-start.16 = (bf16[768,128]{0,1:T(8,128)(2,1)S(1)}, bf16[768,128]{0,1:T(8,128)(2,1)S(1)}, u32[]{:S(2)}, u32[]{:S(2)}) collective-permute-start(bf16[768,128]{0,1:T(8,128)(2,1)S(1)} %get-tuple-element.29), channel_id=1, source_target_pairs={{0,4},{2,6},{4,0},{6,2},{1,5},{3,7},{5,1},{7,3},{8,12},{10,14},{12... | collective-permute-start | bytes 589832 | tf_op jit(solution)/shard_map/ppermute | solution.py:18
Sparse Core Ops, SparseCore 0:
  10.4 44.5 all-gather.2
  57.5 41.8 reduce-scatter.1

commit v4 on v3

--- a/solution.py
+++ b/solution.py
@@ -10,6 +10,7 @@
 BR = 32
 BC = 128
 TOP = 2.0
+REST = 128
 STEP = 2
 
 
@@ -35,16 +36,18 @@
             o_ref[i : i + BR, j : j + BC] = (value * scale).astype(o_ref.dtype)
 
 
-def widen_kernel(a_ref, o_ref):
-    o_ref[...] = a_ref[...].astype(o_ref.dtype)
-
-
-def grad_kernel(core_ref, mine_ref, other_ref, d_ref, o_ref, acc, p_ref):
+def finish_kernel(a_ref, parts_ref, o_ref):
+    cut = a_ref.shape[1]
+    o_ref[:, :cut] = a_ref[...].astype(jnp.float32)
+    o_ref[:, cut:] = jnp.sum(parts_ref[...].astype(jnp.float32), axis=0)
+
+
+def grad_kernel(core_ref, mine_ref, other_ref, d_ref, o_ref, rest_ref, acc, p_ref):
     @pl.when(pl.program_id(0) == 0)
     def _():
         acc[...] = jnp.zeros_like(acc)
 
-    half, rows, width = o_ref.shape[0] // 2, *o_ref.shape[1:]
+    half, rows, width = acc.shape[0] // 2, *acc.shape[1:]
     nb = rows // BR
     for k in range(2 * half):
         x = (mine_ref if k < half else other_ref)[0, k % half]
@@ -69,13 +72,17 @@
     def _():
         for r in range(2):
             at = lax.rem(core_ref[0] + r, 2) * half
-            o_ref[pl.ds(at, half)] = acc[r * half : (r + 1) * half].astype(o_ref.dtype)
+            done = acc[r * half : (r + 1) * half].astype(o_ref.dtype)
+            cut = o_ref.shape[2]
+            o_ref[pl.ds(at, half)] = done[:, :, :cut]
+            rest_ref[pl.ds(at, half)] = done[:, :, cut:]
 
 
 def weight_gradient(core, mine, other, cots):
     groups, half, rows, tok = mine.shape
     cols = cots.shape[2]
     whole = (2 * half, rows, cols)
+    shapes = [(2 * half, rows, cols - REST), (2 * half, rows, REST)]
     return pl.pallas_call(
         grad_kernel,
         grid_spec=pltpu.PrefetchScalarGridSpec(
@@ -86,10 +93,10 @@
                 pl.BlockSpec((1, half, rows, tok), lambda g, c: (g, 0, 0, 0)),
                 pl.BlockSpec((1, tok, cols), lambda g, c: (g, 0, 0)),
             ],
-            out_specs=pl.BlockSpec(whole, lambda g, c: (0, 0, 0)),
+            out_specs=[pl.BlockSpec(s, lambda g, c: (0, 0, 0)) for s in shapes],
             scratch_shapes=[pltpu.VMEM(whole, jnp.float32)] * 2,
         ),
-        out_shape=jax.ShapeDtypeStruct(whole, jnp.bfloat16),
+        out_shape=[jax.ShapeDtypeStruct(s, jnp.bfloat16) for s in shapes],
         compiler_params=pltpu.CompilerParams(vmem_limit_bytes=48 * 2**20),
         cost_estimate=pl.CostEstimate(
             flops=16 * 2 * groups * half * rows * tok * cols, bytes_accessed=2**23, transcendentals=0
@@ -237,11 +244,11 @@
     mine = jnp.stack(mine).reshape(ny, nz // 2, rows, tok)
     other = shift(mine, "core", 1)
 
-    partial_grad = weight_gradient(core, mine, other, cots)
+    partial_grad, rest = weight_gradient(core, mine, other, cots)
     weight_grad = lax.psum_scatter(partial_grad, "z", scatter_dimension=0, tiled=False)
     weight_grad = pl.pallas_call(
-        widen_kernel, out_shape=jax.ShapeDtypeStruct((rows, width), jnp.float32)
-    )(weight_grad)
+        finish_kernel, out_shape=jax.ShapeDtypeStruct((rows, width), jnp.float32)
+    )(weight_grad, lax.all_to_all(rest, "z", split_axis=0, concat_axis=0, tiled=True))
     weights = after(weights, partial_grad)
     dx = gradient_terms(core, weights, cots)
     part = query_parts(core, mine, other, after(weights, dx))

time: 108 us -> 114 us (1.056)
  starting transfers between devices: 29.7 us -> 36.2 us
  waiting for transfers between devices: 36.3 us -> 35.1 us
    ppermute x14, waiting for transfers between devices: 28 us -> 20.2 us  [shift(): return lax.ppermute(a, axis, [(i, (i + step) % n) for i in range(n)])]
    reduce_scatter x1, waiting for transfers between devices: 4.64 us -> 11.9 us  [local(): lax.psum_scatter(partial_grad, 'z', scatter_dimension=0, tiled=False)]
    all_to_all x0 -> x1, starting transfers between devices: none -> 5.64 us  [local(): lax.all_to_all(rest, 'z', split_axis=0, concat_axis=0, tiled=True)]
  transfers between devices with their start and end apart: 20 -> 21, of which waited for: 12 -> 9; matrix products, arithmetic and copies ran while one was open for 7% -> 6% of each run, Pallas kernels for 13% -> 15%
where the time goes in v4:
time: 114 us
  starting transfers between devices  36.2 us (32%)
  waiting for transfers between devices  35.1 us (31%)
  Pallas kernels  18.4 us (16%)
  between operations  14.3 us (13%)
  local copies, waits for them, and re-layouts  6.26 us (5%)
  other arithmetic  3.41 us (3%)
    ppermute x14, waiting for transfers between devices, shift(): return lax.ppermute(a, axis, [(i, (i + step) % n) for i in range(n)])  20.2 us
    ppermute x14, starting transfers between devices, shift(): return lax.ppermute(a, axis, [(i, (i + step) % n) for i in range(n)])  18.6 us
    reduce_scatter x1, waiting for transfers between devices, local(): lax.psum_scatter(partial_grad, 'z', scatter_dimension=0, tiled=False)  11.9 us
    ppermute x4, starting transfers between devices, around(): return lax.ppermute(a, ('y', 'x'), pairs)  11.9 us
    pallas_call x1, Pallas kernels, weight_gradient(): pl.pallas_call(grad_kernel, grid_spec=pltpu.PrefetchScalarGridSpec(num_sc...  9.54 us
    all_to_all x1, starting transfers between devices, local(): lax.all_to_all(rest, 'z', split_axis=0, concat_axis=0, tiled=True)  5.64 us
    all_gather x1, waiting for transfers between devices, local(): weights = lax.all_gather(weights, 'z', axis=0)  2.99 us
    pallas_call x1, Pallas kernels, query_parts(): pl.pallas_call(query_kernel, grid_spec=pltpu.PrefetchScalarGridSpec(num_s...  2.78 us
  transfers between devices with their start and end apart: 21, of which 9 were waited for; matrix products, arithmetic and copies ran while one was open for 6% of the time, Pallas kernels for 15%

profile of v4, /device:TPU:2, one launch (start us, length us, event | category | flops | bytes accessed | tf_op | source)
XLA Modules:
  0.0 113.7 jit_solution(17013215180757805422)
XLA Ops:
  7.2 1.9 %shard_map.67 = bf16[192,768]{1,0:T(8,128)(2,1)} custom-call(bf16[192,768]{1,0:T(8,128)(2,1)} %v_ref.1, bf16[6,6]{1,0:T(8,128)(2,1)} %s_ref.1), custom_call_target="tpu_custom_call" | custom-call | tf_op jit(solution)/shard_map/pallas_call | solution.py:232
  9.1 3.1 %collective-permute-start.2 = (bf16[128,768]{1,0:T(8,128)(2,1)}, bf16[128,768]{1,0:T(8,128)(2,1)S(1)}, u32[]{:S(2)}, u32[]{:S(2)}) collective-permute-start(bf16[128,768]{1,0:T(8,128)(2,1)} %param.7), channel_id=1, source_target_pairs={{0,192},{64,0},{128,64},{192,128},{1,193},{65,1},{129,65},{193,129... | collective-permute-start | bytes 589832 | tf_op jit(solution)/shard_map/ppermute | solution.py:19
  12.2 6.4 %collective-permute-start = (bf16[768,128]{0,1:T(8,128)(2,1)}, bf16[768,128]{0,1:T(8,128)(2,1)S(1)}, u32[]{:S(2)}, u32[]{:S(2)}) collective-permute-start(bf16[768,128]{0,1:T(8,128)(2,1)} %bitcast.61), channel_id=1, source_target_pairs={{0,0},{2,64},{4,128},{6,192},{64,2},{66,66},{68,130},{70,194},{128... | collective-permute-start | bytes 589832 | tf_op jit(solution)/shard_map/ppermute | solution.py:211
  18.7 2.5 %collective-permute-start.6 = (bf16[128,768]{1,0:T(8,128)(2,1)}, bf16[128,768]{1,0:T(8,128)(2,1)S(1)}, u32[]{:S(2)}, u32[]{:S(2)}) collective-permute-start(bf16[128,768]{1,0:T(8,128)(2,1)} %param.7), channel_id=1, source_target_pairs={{0,64},{64,128},{128,192},{192,0},{1,65},{65,129},{129,193},{193,1... | collective-permute-start | bytes 589832 | tf_op jit(solution)/shard_map/ppermute | solution.py:19
  21.2 3.0 %collective-permute-done.2 = bf16[128,768]{1,0:T(8,128)(2,1)S(1)} collective-permute-done((bf16[128,768]{1,0:T(8,128)(2,1)}, bf16[128,768]{1,0:T(8,128)(2,1)S(1)}, u32[]{:S(2)}, u32[]{:S(2)}) %collective-permute-start.2) | collective-permute-done | bytes 196640 | tf_op jit(solution)/shard_map/ppermute | solution.py:19
  24.1 5.5 %collective-permute-start.3 = (bf16[768,128]{0,1:T(8,128)(2,1)}, bf16[768,128]{0,1:T(8,128)(2,1)S(1)}, u32[]{:S(2)}, u32[]{:S(2)}) collective-permute-start(bf16[768,128]{0,1:T(8,128)(2,1)} %bitcast.63), channel_id=1, source_target_pairs={{0,4},{2,68},{4,132},{6,196},{64,6},{66,70},{68,134},{70,198},{128... | collective-permute-start | bytes 589832 | tf_op jit(solution)/shard_map/ppermute | solution.py:211
  29.7 7.6 %collective-permute-done.5 = bf16[128,768]{1,0:T(8,128)(2,1)S(1)} collective-permute-done((bf16[128,768]{1,0:T(8,128)(2,1)}, bf16[128,768]{1,0:T(8,128)(2,1)S(1)}, u32[]{:S(2)}, u32[]{:S(2)}) %collective-permute-start.5) | collective-permute-done | bytes 196640 | tf_op jit(solution)/shard_map/ppermute | solution.py:19
  37.3 1.4 %collective-permute-done.6 = bf16[128,768]{1,0:T(8,128)(2,1)S(1)} collective-permute-done((bf16[128,768]{1,0:T(8,128)(2,1)}, bf16[128,768]{1,0:T(8,128)(2,1)S(1)}, u32[]{:S(2)}, u32[]{:S(2)}) %collective-permute-start.6) | collective-permute-done | bytes 196640 | tf_op jit(solution)/shard_map/ppermute | solution.py:19
  39.9 1.9 %collective-permute-done.7.other_ref = bf16[4,4,192,128]{3,2,1,0:T(8,128)(2,1)S(1)} collective-permute-done((bf16[4,4,192,128]{3,2,1,0:T(8,128)(2,1)S(1)}, bf16[4,4,192,128]{3,2,1,0:T(8,128)(2,1)S(1)}, u32[]{:S(2)}, u32[]{:S(2)}) %collective-permute-start.7) | collective-permute-done | bytes 786464 | tf_op jit(solution)/shard_map/ppermute | solution.py:19
  41.8 9.5 %shard_map.68 = (bf16[8,192,640]{2,1,0:T(8,128)(2,1)}, bf16[8,192,128]{2,1,0:T(8,128)(2,1)}) custom-call(s32[1]{0:T(128)} %bitcast.core_ref, bf16[4,4,192,128]{3,2,1,0:T(8,128)(2,1)S(1)} %pad_maximum_fusion.mine_ref, bf16[4,4,192,128]{3,2,1,0:T(8,128)(2,1)S(1)} %collective-permute-done.7.other_ref, bf16[4,128,768]{2,1,0:T(8,128)(2,1)S(1)} %pad_maximum_fusion.2.d_ref), custom_call_target="tpu_custom_call" | custom-call | flops 9663676416 | bytes 8388608 | tf_op jit(solution)/shard_map/pallas_call | solution.py:86
  51.4 3.0 %all-gather.3.cloned.1.call-done = bf16[1536,768]{1,0:T(8,128)(2,1)} async-done(((bf16[192,768]{1,0:T(8,128)(2,1)}), bf16[1536,768]{1,0:T(8,128)(2,1)}) %all-gather.3.cloned.1.call-update) | async-done | bytes 2359312 | tf_op jit(solution)/shard_map/all_gather | solution.py:235
  54.4 1.7 %copy-done = bf16[1536,768]{1,0:T(8,128)(2,1)S(1)} copy-done((bf16[1536,768]{1,0:T(8,128)(2,1)S(1)}, bf16[1536,768]{1,0:T(8,128)(2,1)}, u32[]{:S(2)}) %copy-start) | copy-done | bytes 2359320
  56.0 2.2 %shard_map.69 = bf16[2,4,4,192,128]{4,3,2,1,0:T(8,128)(2,1)S(1)} custom-call(s32[1]{0:T(128)} %bitcast.core_ref, bf16[8,192,768]{2,1,0:T(8,128)(2,1)S(1)} %bitcast.44, bf16[4,128,768]{2,1,0:T(8,128)(2,1)S(1)} %pad_maximum_fusion.2.d_ref), custom_call_target="tpu_custom_call" | custom-call | flops 9663676416 | bytes 4194304 | tf_op jit(solution)/shard_map/pallas_call | solution.py:157
  58.2 1.1 fusion.7
  59.3 1.2 %copy.11 = bf16[4,768,128]{1,2,0:T(8,128)(2,1)} copy(bf16[4,768,128]{2,1,0:T(8,128)(2,1)S(1)} %bitcast.46) | data formatting | bytes 1572864 | tf_op jit(solution)/shard_map/squeeze | solution.py:215
  60.4 5.6 %all-to-all-start = ((bf16[8,192,128]{2,1,0:T(8,128)(2,1)}), bf16[8,192,128]{2,1,0:T(8,128)(2,1)S(1)}, u32[]{:S(2)}, u32[]{:S(2)}) async-start(bf16[8,192,128]{2,1,0:T(8,128)(2,1)} %get-tuple-element.28), calls=%async_computation.1 | async-start | bytes 786432 | tf_op jit(solution)/shard_map/all_to_all | solution.py:251
  66.1 1.5 %copy.12 = f32[4,768,128]{1,2,0:T(8,128)S(1)} copy(bf16[4,768,128]{2,1,0:T(8,128)(2,1)} %bitcast.47) | data formatting | bytes 2359296 | tf_op jit(solution)/shard_map/convert_element_type | solution.py:205
  67.6 1.4 %add_convert_fusion = bf16[4,768,128]{1,2,0:T(8,128)(2,1)S(1)} fusion(f32[4,768,128]{1,2,0:T(8,128)S(1)} %copy.12, bf16[4,768,128]{1,2,0:T(8,128)(2,1)} %collective-permute-done.8), kind=kLoop, calls=%fused_computation | loop fusion | flops 1179648 | bytes 3145728 | tf_op jit(solution)/shard_map/convert_element_type | solution.py:205
  69.1 1.3 %collective-permute-start.14 = (bf16[768,128]{0,1:T(8,128)(2,1)S(1)}, bf16[768,128]{0,1:T(8,128)(2,1)S(1)}, u32[]{:S(2)}, u32[]{:S(2)}) collective-permute-start(bf16[768,128]{0,1:T(8,128)(2,1)S(1)} %get-tuple-element.35), channel_id=1, source_target_pairs={{0,192},{64,0},{128,64},{192,128},{1,193},{65,1},{129,65},{193,129... | collective-permute-start | bytes 589832 | tf_op jit(solution)/shard_map/ppermute | solution.py:19
  70.4 1.1 collective-permute-start.13
  71.5 0.9 collective-permute-start.12
  72.4 2.8 %shard_map.70 = bf16[4,128,768]{2,1,0:T(8,128)(2,1)S(1)} custom-call(s32[1]{0:T(128)} %bitcast.core_ref, bf16[4,4,192,128]{3,2,1,0:T(8,128)(2,1)S(1)} %pad_maximum_fusion.mine_ref, bf16[4,4,192,128]{3,2,1,0:T(8,128)(2,1)S(1)} %collective-permute-done.7.other_ref, bf16[8,192,768]{2,1,0:T(8,128)(2,1)S(1)} %bitcast.45), custom_call_target="tpu_custom_call" | custom-call | flops 9663676416 | bytes 4194304 | tf_op jit(solution)/shard_map/pallas_call | solution.py:183
  75.2 1.6 %collective-permute-start.9 = (bf16[128,768]{1,0:T(8,128)(2,1)S(1)}, bf16[128,768]{1,0:T(8,128)(2,1)S(1)}, u32[]{:S(2)}, u32[]{:S(2)}) collective-permute-start(bf16[128,768]{1,0:T(8,128)(2,1)S(1)} %get-tuple-element.38), channel_id=1, source_target_pairs={{0,64},{64,128},{128,192},{192,0},{1,65},{65,129},{129,193},{193,1... | collective-permute-start | bytes 589832 | tf_op jit(solution)/shard_map/ppermute | solution.py:19
  76.8 1.8 %collective-permute-start.11 = (bf16[128,768]{1,0:T(8,128)(2,1)S(1)}, bf16[128,768]{1,0:T(8,128)(2,1)S(1)}, u32[]{:S(2)}, u32[]{:S(2)}) collective-permute-start(bf16[128,768]{1,0:T(8,128)(2,1)S(1)} %get-tuple-element.39), channel_id=1, source_target_pairs={{0,192},{64,0},{128,64},{192,128},{1,193},{65,1},{129,65},{193,129... | collective-permute-start | bytes 589832 | tf_op jit(solution)/shard_map/ppermute | solution.py:19
  78.6 1.7 %collective-permute-start.10 = (bf16[128,768]{1,0:T(8,128)(2,1)S(1)}, bf16[128,768]{1,0:T(8,128)(2,1)S(1)}, u32[]{:S(2)}, u32[]{:S(2)}) collective-permute-start(bf16[128,768]{1,0:T(8,128)(2,1)S(1)} %get-tuple-element.40), channel_id=1, source_target_pairs={{0,128},{64,192},{128,0},{192,64},{1,129},{65,193},{129,1},{193,65... | collective-permute-start | bytes 589832 | tf_op jit(solution)/shard_map/ppermute | solution.py:19
  80.3 2.7 %collective-permute-done.12 = bf16[768,128]{0,1:T(8,128)(2,1)S(1)} collective-permute-done((bf16[768,128]{0,1:T(8,128)(2,1)S(1)}, bf16[768,128]{0,1:T(8,128)(2,1)S(1)}, u32[]{:S(2)}, u32[]{:S(2)}) %collective-permute-start.12) | collective-permute-done | bytes 196640 | tf_op jit(solution)/shard_map/ppermute | solution.py:19
  83.1 1.9 %collective-permute-start.15 = (bf16[768,128]{0,1:T(8,128)(2,1)S(1)}, bf16[768,128]{0,1:T(8,128)(2,1)S(1)}, u32[]{:S(2)}, u32[]{:S(2)}) collective-permute-start(bf16[768,128]{0,1:T(8,128)(2,1)S(1)} %get-tuple-element.31), channel_id=1, source_target_pairs={{0,2},{2,4},{4,6},{6,0},{1,3},{3,5},{5,7},{7,1},{8,10},{10,12},{12... | collective-permute-start | bytes 589832 | tf_op jit(solution)/shard_map/ppermute | solution.py:19
  85.2 2.8 %collective-permute-done.9 = bf16[128,768]{1,0:T(8,128)(2,1)S(1)} collective-permute-done((bf16[128,768]{1,0:T(8,128)(2,1)S(1)}, bf16[128,768]{1,0:T(8,128)(2,1)S(1)}, u32[]{:S(2)}, u32[]{:S(2)}) %collective-permute-start.9) | collective-permute-done | bytes 196640 | tf_op jit(solution)/shard_map/ppermute | solution.py:19
  88.0 2.4 %collective-permute-start.16 = (bf16[768,128]{0,1:T(8,128)(2,1)S(1)}, bf16[768,128]{0,1:T(8,128)(2,1)S(1)}, u32[]{:S(2)}, u32[]{:S(2)}) collective-permute-start(bf16[768,128]{0,1:T(8,128)(2,1)S(1)} %get-tuple-element.33), channel_id=1, source_target_pairs={{0,4},{2,6},{4,0},{6,2},{1,5},{3,7},{5,1},{7,3},{8,12},{10,14},{12... | collective-permute-start | bytes 589832 | tf_op jit(solution)/shard_map/ppermute | solution.py:19
  90.5 0.9 collective-permute-done.10
  92.1 11.9 %reduce-scatter.2.cloned.1.call-done = bf16[1,192,640]{2,1,0:T(8,128)(2,1)} async-done(((bf16[8,192,640]{2,1,0:T(8,128)(2,1)}), bf16[1,192,640]{2,1,0:T(8,128)(2,1)}) %reduce-scatter.2.cloned.1.call-update) | async-done | bytes 245776 | tf_op jit(solution)/shard_map/reduce_scatter | solution.py:248
  104.0 2.0 %shard_map.71 = f32[192,768]{1,0:T(8,128)} custom-call(bf16[192,640]{1,0:T(8,128)(2,1)} %bitcast.52, bf16[8,192,128]{2,1,0:T(8,128)(2,1)} %copy-done.2), custom_call_target="tpu_custom_call" | custom-call | tf_op jit(solution)/shard_map/pallas_call | solution.py:249
  (43 shorter events, 3.4 us)
Async XLA Ops:
  7.2 47.2 %all-gather.3.cloned.1.call-start = ((), (), s32[]{:S(2)}) async-start(), calls=%async_computation.3 | async-start | bytes 2654208 | tf_op jit(solution)/shard_map/all_gather | solution.py:235
  9.1 94.9 %reduce-scatter.2.cloned.1.call-start = ((), (), s32[]{:S(2)}) async-start(), calls=%async_computation.2 | async-start | bytes 2211840 | tf_op jit(solution)/shard_map/reduce_scatter | solution.py:248
  9.1 15.0 %collective-permute-start.2 = (bf16[128,768]{1,0:T(8,128)(2,1)}, bf16[128,768]{1,0:T(8,128)(2,1)S(1)}, u32[]{:S(2)}, u32[]{:S(2)}) collective-permute-start(bf16[128,768]{1,0:T(8,128)(2,1)} %param.7), channel_id=1, source_target_pairs={{0,192},{64,0},{128,64},{192,128},{1,193},{65,1},{129,65},{193,129... | collective-permute-start | bytes 589832 | tf_op jit(solution)/shard_map/ppermute | solution.py:19
  12.2 27.4 %copy-start.3 = (bf16[128,768]{1,0:T(8,128)(2,1)S(1)}, bf16[128,768]{1,0:T(8,128)(2,1)}, u32[]{:S(2)}) copy-start(bf16[128,768]{1,0:T(8,128)(2,1)} %param.7) | copy-start | bytes 589828
  12.2 11.9 %collective-permute-start.1 = (bf16[768,128]{0,1:T(8,128)(2,1)}, bf16[768,128]{0,1:T(8,128)(2,1)S(1)}, u32[]{:S(2)}, u32[]{:S(2)}) collective-permute-start(bf16[768,128]{0,1:T(8,128)(2,1)} %bitcast.60), channel_id=1, source_target_pairs={{0,2},{2,66},{4,130},{6,194},{64,4},{66,68},{68,132},{70,196},{128... | collective-permute-start | bytes 589832 | tf_op jit(solution)/shard_map/ppermute | solution.py:211
  12.2 17.4 %collective-permute-start = (bf16[768,128]{0,1:T(8,128)(2,1)}, bf16[768,128]{0,1:T(8,128)(2,1)S(1)}, u32[]{:S(2)}, u32[]{:S(2)}) collective-permute-start(bf16[768,128]{0,1:T(8,128)(2,1)} %bitcast.61), channel_id=1, source_target_pairs={{0,0},{2,64},{4,128},{6,192},{64,2},{66,66},{68,130},{70,194},{128... | collective-permute-start | bytes 589832 | tf_op jit(solution)/shard_map/ppermute | solution.py:211
  18.6 18.7 %collective-permute-start.5 = (bf16[128,768]{1,0:T(8,128)(2,1)}, bf16[128,768]{1,0:T(8,128)(2,1)S(1)}, u32[]{:S(2)}, u32[]{:S(2)}) collective-permute-start(bf16[128,768]{1,0:T(8,128)(2,1)} %param.7), channel_id=1, source_target_pairs={{0,128},{64,192},{128,0},{192,64},{1,129},{65,193},{129,1},{193,65... | collective-permute-start | bytes 589832 | tf_op jit(solution)/shard_map/ppermute | solution.py:19
  18.7 19.9 %collective-permute-start.6 = (bf16[128,768]{1,0:T(8,128)(2,1)}, bf16[128,768]{1,0:T(8,128)(2,1)S(1)}, u32[]{:S(2)}, u32[]{:S(2)}) collective-permute-start(bf16[128,768]{1,0:T(8,128)(2,1)} %param.7), channel_id=1, source_target_pairs={{0,64},{64,128},{128,192},{192,0},{1,65},{65,129},{129,193},{193,1... | collective-permute-start | bytes 589832 | tf_op jit(solution)/shard_map/ppermute | solution.py:19
  24.1 14.5 %collective-permute-start.4 = (bf16[768,128]{0,1:T(8,128)(2,1)}, bf16[768,128]{0,1:T(8,128)(2,1)S(1)}, u32[]{:S(2)}, u32[]{:S(2)}) collective-permute-start(bf16[768,128]{0,1:T(8,128)(2,1)} %bitcast.62), channel_id=1, source_target_pairs={{0,6},{2,70},{4,134},{6,198},{64,0},{66,64},{68,128},{70,192},{128... | collective-permute-start | bytes 589832 | tf_op jit(solution)/shard_map/ppermute | solution.py:211
  24.1 14.5 %collective-permute-start.3 = (bf16[768,128]{0,1:T(8,128)(2,1)}, bf16[768,128]{0,1:T(8,128)(2,1)S(1)}, u32[]{:S(2)}, u32[]{:S(2)}) collective-permute-start(bf16[768,128]{0,1:T(8,128)(2,1)} %bitcast.63), channel_id=1, source_target_pairs={{0,4},{2,68},{4,132},{6,196},{64,6},{66,70},{68,134},{70,198},{128... | collective-permute-start | bytes 589832 | tf_op jit(solution)/shard_map/ppermute | solution.py:211
  39.4 2.4 %collective-permute-start.7 = (bf16[4,4,192,128]{3,2,1,0:T(8,128)(2,1)S(1)}, bf16[4,4,192,128]{3,2,1,0:T(8,128)(2,1)S(1)}, u32[]{:S(2)}, u32[]{:S(2)}) collective-permute-start(bf16[4,4,192,128]{3,2,1,0:T(8,128)(2,1)S(1)} %pad_maximum_fusion.mine_ref), channel_id=1, source_target_pairs={{0,1},{1,0},{2,3},{3,2},{4,5},{5,4},{6,7},{7,6},{8,9},{9,8},{10,11... | collective-permute-start | bytes 2359304 | tf_op jit(solution)/shard_map/ppermute | solution.py:19
  54.4 1.7 %copy-start = (bf16[1536,768]{1,0:T(8,128)(2,1)S(1)}, bf16[1536,768]{1,0:T(8,128)(2,1)}, u32[]{:S(2)}) copy-start(bf16[1536,768]{1,0:T(8,128)(2,1)} %all-gather.3.cloned.1.call-done) | copy-start | bytes 7077892
  60.4 7.1 %collective-permute-start.8 = (bf16[4,768,128]{1,2,0:T(8,128)(2,1)}, bf16[4,768,128]{1,2,0:T(8,128)(2,1)}, u32[]{:S(2)}, u32[]{:S(2)}) collective-permute-start(bf16[4,768,128]{1,2,0:T(8,128)(2,1)} %copy.11), channel_id=1, source_target_pairs={{0,1},{1,0},{2,3},{3,2},{4,5},{5,4},{6,7},{7,6},{8,9},{9,8},{10,11... | collective-permute-start | bytes 2359304 | tf_op jit(solution)/shard_map/ppermute | solution.py:19
  60.4 31.7 %all-to-all-start = ((bf16[8,192,128]{2,1,0:T(8,128)(2,1)}), bf16[8,192,128]{2,1,0:T(8,128)(2,1)S(1)}, u32[]{:S(2)}, u32[]{:S(2)}) async-start(bf16[8,192,128]{2,1,0:T(8,128)(2,1)} %get-tuple-element.28), calls=%async_computation.1 | async-start | bytes 786432 | tf_op jit(solution)/shard_map/all_to_all | solution.py:251
  67.6 4.8 %copy-start.1 = (bf16[1536,768]{1,0:T(8,128)(2,1)S(1)}, bf16[1536,768]{1,0:T(8,128)(2,1)}, u32[]{:S(2)}) copy-start(bf16[1536,768]{1,0:T(8,128)(2,1)} %all-gather.3.cloned.1.call-done) | copy-start | bytes 7077892
  69.1 9.5 %collective-permute-start.14 = (bf16[768,128]{0,1:T(8,128)(2,1)S(1)}, bf16[768,128]{0,1:T(8,128)(2,1)S(1)}, u32[]{:S(2)}, u32[]{:S(2)}) collective-permute-start(bf16[768,128]{0,1:T(8,128)(2,1)S(1)} %get-tuple-element.35), channel_id=1, source_target_pairs={{0,192},{64,0},{128,64},{192,128},{1,193},{65,1},{129,65},{193,129... | collective-permute-start | bytes 589832 | tf_op jit(solution)/shard_map/ppermute | solution.py:19
  70.4 9.9 %collective-permute-start.13 = (bf16[768,128]{0,1:T(8,128)(2,1)S(1)}, bf16[768,128]{0,1:T(8,128)(2,1)S(1)}, u32[]{:S(2)}, u32[]{:S(2)}) collective-permute-start(bf16[768,128]{0,1:T(8,128)(2,1)S(1)} %get-tuple-element.36), channel_id=1, source_target_pairs={{0,128},{64,192},{128,0},{192,64},{1,129},{65,193},{129,1},{193,65... | collective-permute-start | bytes 589832 | tf_op jit(solution)/shard_map/ppermute | solution.py:19
  71.5 11.4 %collective-permute-start.12 = (bf16[768,128]{0,1:T(8,128)(2,1)S(1)}, bf16[768,128]{0,1:T(8,128)(2,1)S(1)}, u32[]{:S(2)}, u32[]{:S(2)}) collective-permute-start(bf16[768,128]{0,1:T(8,128)(2,1)S(1)} %get-tuple-element.37), channel_id=1, source_target_pairs={{0,64},{64,128},{128,192},{192,0},{1,65},{65,129},{129,193},{193,1... | collective-permute-start | bytes 589832 | tf_op jit(solution)/shard_map/ppermute | solution.py:19
  75.2 12.8 %collective-permute-start.9 = (bf16[128,768]{1,0:T(8,128)(2,1)S(1)}, bf16[128,768]{1,0:T(8,128)(2,1)S(1)}, u32[]{:S(2)}, u32[]{:S(2)}) collective-permute-start(bf16[128,768]{1,0:T(8,128)(2,1)S(1)} %get-tuple-element.38), channel_id=1, source_target_pairs={{0,64},{64,128},{128,192},{192,0},{1,65},{65,129},{129,193},{193,1... | collective-permute-start | bytes 589832 | tf_op jit(solution)/shard_map/ppermute | solution.py:19
  76.8 13.7 %collective-permute-start.11 = (bf16[128,768]{1,0:T(8,128)(2,1)S(1)}, bf16[128,768]{1,0:T(8,128)(2,1)S(1)}, u32[]{:S(2)}, u32[]{:S(2)}) collective-permute-start(bf16[128,768]{1,0:T(8,128)(2,1)S(1)} %get-tuple-element.39), channel_id=1, source_target_pairs={{0,192},{64,0},{128,64},{192,128},{1,193},{65,1},{129,65},{193,129... | collective-permute-start | bytes 589832 | tf_op jit(solution)/shard_map/ppermute | solution.py:19
  78.6 12.8 %collective-permute-start.10 = (bf16[128,768]{1,0:T(8,128)(2,1)S(1)}, bf16[128,768]{1,0:T(8,128)(2,1)S(1)}, u32[]{:S(2)}, u32[]{:S(2)}) collective-permute-start(bf16[128,768]{1,0:T(8,128)(2,1)S(1)} %get-tuple-element.40), channel_id=1, source_target_pairs={{0,128},{64,192},{128,0},{192,64},{1,129},{65,193},{129,1},{193,65... | collective-permute-start | bytes 589832 | tf_op jit(solution)/shard_map/ppermute | solution.py:19
  83.1 22.9 %collective-permute-start.15 = (bf16[768,128]{0,1:T(8,128)(2,1)S(1)}, bf16[768,128]{0,1:T(8,128)(2,1)S(1)}, u32[]{:S(2)}, u32[]{:S(2)}) collective-permute-start(bf16[768,128]{0,1:T(8,128)(2,1)S(1)} %get-tuple-element.31), channel_id=1, source_target_pairs={{0,2},{2,4},{4,6},{6,0},{1,3},{3,5},{5,7},{7,1},{8,10},{10,12},{12... | collective-permute-start | bytes 589832 | tf_op jit(solution)/shard_map/ppermute | solution.py:19
  85.0 21.1 %collective-permute-start.17 = (bf16[768,128]{0,1:T(8,128)(2,1)S(1)}, bf16[768,128]{0,1:T(8,128)(2,1)S(1)}, u32[]{:S(2)}, u32[]{:S(2)}) collective-permute-start(bf16[768,128]{0,1:T(8,128)(2,1)S(1)} %get-tuple-element.32), channel_id=1, source_target_pairs={{0,6},{2,0},{4,2},{6,4},{1,7},{3,1},{5,3},{7,5},{8,14},{10,8},{12,... | collective-permute-start | bytes 589832 | tf_op jit(solution)/shard_map/ppermute | solution.py:19
  88.0 18.0 %collective-permute-start.16 = (bf16[768,128]{0,1:T(8,128)(2,1)S(1)}, bf16[768,128]{0,1:T(8,128)(2,1)S(1)}, u32[]{:S(2)}, u32[]{:S(2)}) collective-permute-start(bf16[768,128]{0,1:T(8,128)(2,1)S(1)} %get-tuple-element.33), channel_id=1, source_target_pairs={{0,4},{2,6},{4,0},{6,2},{1,5},{3,7},{5,1},{7,3},{8,12},{10,14},{12... | collective-permute-start | bytes 589832 | tf_op jit(solution)/shard_map/ppermute | solution.py:19
  92.1 11.9 %copy-start.2 = (bf16[8,192,128]{2,1,0:T(8,128)(2,1)}, bf16[8,192,128]{2,1,0:T(8,128)(2,1)S(1)}, u32[]{:S(2)}) copy-start(bf16[8,192,128]{2,1,0:T(8,128)(2,1)S(1)} %all-to-all-done.parts_ref) | copy-start | bytes 1179652
Sparse Core Ops, SparseCore 0:
  9.8 44.5 all-gather.2
  56.9 47.0 reduce-scatter.1

commit v5 on v3

--- a/solution.py
+++ b/solution.py
@@ -240,7 +240,11 @@
     partial_grad = weight_gradient(core, mine, other, cots)
     weight_grad = lax.psum_scatter(partial_grad, "z", scatter_dimension=0, tiled=False)
     weight_grad = pl.pallas_call(
-        widen_kernel, out_shape=jax.ShapeDtypeStruct((rows, width), jnp.float32)
+        widen_kernel,
+        grid=(2,),
+        in_specs=[pl.BlockSpec((rows // 2, width), lambda i: (i, 0))],
+        out_specs=pl.BlockSpec((rows // 2, width), lambda i: (i, 0)),
+        out_shape=jax.ShapeDtypeStruct((rows, width), jnp.float32),
     )(weight_grad)
     weights = after(weights, partial_grad)
     dx = gradient_terms(core, weights, cots)

time: 108 us -> 108 us (level)
  no operation moved by 1% of the time
where the time goes in v5:
time: 108 us
  waiting for transfers between devices  36.3 us (34%)
  starting transfers between devices  29.7 us (28%)
  Pallas kernels  18.1 us (17%)
  between operations  14.3 us (13%)
  local copies, waits for them, and re-layouts  6.2 us (6%)
  other arithmetic  3.4 us (3%)
    ppermute x14, waiting for transfers between devices, shift(): return lax.ppermute(a, axis, [(i, (i + step) % n) for i in range(n)])  28 us
    ppermute x14, starting transfers between devices, shift(): return lax.ppermute(a, axis, [(i, (i + step) % n) for i in range(n)])  17.8 us
    ppermute x4, starting transfers between devices, around(): return lax.ppermute(a, ('y', 'x'), pairs)  11.9 us
    pallas_call x1, Pallas kernels, weight_gradient(): pl.pallas_call(grad_kernel, grid_spec=pltpu.PrefetchScalarGridSpec(num_sc...  9.57 us
    reduce_scatter x1, waiting for transfers between devices, local(): lax.psum_scatter(partial_grad, 'z', scatter_dimension=0, tiled=False)  4.64 us
    all_gather x1, waiting for transfers between devices, local(): weights = lax.all_gather(weights, 'z', axis=0)  3.55 us
    pallas_call x1, Pallas kernels, query_parts(): pl.pallas_call(query_kernel, grid_spec=pltpu.PrefetchScalarGridSpec(num_s...  2.77 us
    convert_element_type x2, other arithmetic, total(): return sum((p.astype(jnp.float32) for p in parts)).astype(jnp.bfloat16)  2.22 us
  transfers between devices with their start and end apart: 20, of which 12 were waited for; matrix products, arithmetic and copies ran while one was open for 7% of the time, Pallas kernels for 13%

profile of v5, /device:TPU:2, one launch (start us, length us, event | category | flops | bytes accessed | tf_op | source)
XLA Modules:
  0.0 108.0 jit_solution(12165996492358567577)
XLA Ops:
  7.2 1.8 %shard_map.67 = bf16[192,768]{1,0:T(8,128)(2,1)} custom-call(bf16[192,768]{1,0:T(8,128)(2,1)} %v_ref.1, bf16[6,6]{1,0:T(8,128)(2,1)} %s_ref.1), custom_call_target="tpu_custom_call" | custom-call | tf_op jit(solution)/shard_map/pallas_call | solution.py:225
  9.1 3.1 %collective-permute-start.2 = (bf16[128,768]{1,0:T(8,128)(2,1)}, bf16[128,768]{1,0:T(8,128)(2,1)S(1)}, u32[]{:S(2)}, u32[]{:S(2)}) collective-permute-start(bf16[128,768]{1,0:T(8,128)(2,1)} %param.7), channel_id=1, source_target_pairs={{0,192},{64,0},{128,64},{192,128},{1,193},{65,1},{129,65},{193,129... | collective-permute-start | bytes 589832 | tf_op jit(solution)/shard_map/ppermute | solution.py:18
  12.2 6.4 %collective-permute-start = (bf16[768,128]{0,1:T(8,128)(2,1)}, bf16[768,128]{0,1:T(8,128)(2,1)S(1)}, u32[]{:S(2)}, u32[]{:S(2)}) collective-permute-start(bf16[768,128]{0,1:T(8,128)(2,1)} %bitcast.61), channel_id=1, source_target_pairs={{0,0},{2,64},{4,128},{6,192},{64,2},{66,66},{68,130},{70,194},{128... | collective-permute-start | bytes 589832 | tf_op jit(solution)/shard_map/ppermute | solution.py:204
  18.7 2.5 %collective-permute-start.6 = (bf16[128,768]{1,0:T(8,128)(2,1)}, bf16[128,768]{1,0:T(8,128)(2,1)S(1)}, u32[]{:S(2)}, u32[]{:S(2)}) collective-permute-start(bf16[128,768]{1,0:T(8,128)(2,1)} %param.7), channel_id=1, source_target_pairs={{0,64},{64,128},{128,192},{192,0},{1,65},{65,129},{129,193},{193,1... | collective-permute-start | bytes 589832 | tf_op jit(solution)/shard_map/ppermute | solution.py:18
  21.2 3.0 %collective-permute-done.2 = bf16[128,768]{1,0:T(8,128)(2,1)S(1)} collective-permute-done((bf16[128,768]{1,0:T(8,128)(2,1)}, bf16[128,768]{1,0:T(8,128)(2,1)S(1)}, u32[]{:S(2)}, u32[]{:S(2)}) %collective-permute-start.2) | collective-permute-done | bytes 196640 | tf_op jit(solution)/shard_map/ppermute | solution.py:18
  24.1 5.5 %collective-permute-start.3 = (bf16[768,128]{0,1:T(8,128)(2,1)}, bf16[768,128]{0,1:T(8,128)(2,1)S(1)}, u32[]{:S(2)}, u32[]{:S(2)}) collective-permute-start(bf16[768,128]{0,1:T(8,128)(2,1)} %bitcast.63), channel_id=1, source_target_pairs={{0,4},{2,68},{4,132},{6,196},{64,6},{66,70},{68,134},{70,198},{128... | collective-permute-start | bytes 589832 | tf_op jit(solution)/shard_map/ppermute | solution.py:204
  29.7 7.6 %collective-permute-done.5 = bf16[128,768]{1,0:T(8,128)(2,1)S(1)} collective-permute-done((bf16[128,768]{1,0:T(8,128)(2,1)}, bf16[128,768]{1,0:T(8,128)(2,1)S(1)}, u32[]{:S(2)}, u32[]{:S(2)}) %collective-permute-start.5) | collective-permute-done | bytes 196640 | tf_op jit(solution)/shard_map/ppermute | solution.py:18
  37.2 1.4 %collective-permute-done.6 = bf16[128,768]{1,0:T(8,128)(2,1)S(1)} collective-permute-done((bf16[128,768]{1,0:T(8,128)(2,1)}, bf16[128,768]{1,0:T(8,128)(2,1)S(1)}, u32[]{:S(2)}, u32[]{:S(2)}) %collective-permute-start.6) | collective-permute-done | bytes 196640 | tf_op jit(solution)/shard_map/ppermute | solution.py:18
  39.9 1.9 %collective-permute-done.7.other_ref = bf16[4,4,192,128]{3,2,1,0:T(8,128)(2,1)S(1)} collective-permute-done((bf16[4,4,192,128]{3,2,1,0:T(8,128)(2,1)S(1)}, bf16[4,4,192,128]{3,2,1,0:T(8,128)(2,1)S(1)}, u32[]{:S(2)}, u32[]{:S(2)}) %collective-permute-start.7) | collective-permute-done | bytes 786464 | tf_op jit(solution)/shard_map/ppermute | solution.py:18
  41.8 9.6 %shard_map.68 = bf16[8,192,768]{2,1,0:T(8,128)(2,1)} custom-call(s32[1]{0:T(128)} %bitcast.core_ref, bf16[4,4,192,128]{3,2,1,0:T(8,128)(2,1)S(1)} %pad_maximum_fusion.mine_ref, bf16[4,4,192,128]{3,2,1,0:T(8,128)(2,1)S(1)} %collective-permute-done.7.other_ref, bf16[4,128,768]{2,1,0:T(8,128)(2,1)S(1)} %pad_maximum_fusion.2.d_ref), custom_call_target="tpu_custom_call" | custom-call | flops 9663676416 | bytes 8388608 | tf_op jit(solution)/shard_map/pallas_call | solution.py:79
  51.4 3.5 %all-gather.3.cloned.1.call-done = bf16[1536,768]{1,0:T(8,128)(2,1)} async-done(((bf16[192,768]{1,0:T(8,128)(2,1)}), bf16[1536,768]{1,0:T(8,128)(2,1)}) %all-gather.3.cloned.1.call-update) | async-done | bytes 2359312 | tf_op jit(solution)/shard_map/all_gather | solution.py:228
  54.9 1.7 %copy-done = bf16[1536,768]{1,0:T(8,128)(2,1)S(1)} copy-done((bf16[1536,768]{1,0:T(8,128)(2,1)S(1)}, bf16[1536,768]{1,0:T(8,128)(2,1)}, u32[]{:S(2)}) %copy-start) | copy-done | bytes 2359320
  56.6 2.2 %shard_map.69 = bf16[2,4,4,192,128]{4,3,2,1,0:T(8,128)(2,1)S(1)} custom-call(s32[1]{0:T(128)} %bitcast.core_ref, bf16[8,192,768]{2,1,0:T(8,128)(2,1)S(1)} %bitcast.44, bf16[4,128,768]{2,1,0:T(8,128)(2,1)S(1)} %pad_maximum_fusion.2.d_ref), custom_call_target="tpu_custom_call" | custom-call | flops 9663676416 | bytes 4194304 | tf_op jit(solution)/shard_map/pallas_call | solution.py:150
  58.8 1.1 fusion.7
  59.8 1.2 %copy.11 = bf16[4,768,128]{1,2,0:T(8,128)(2,1)} copy(bf16[4,768,128]{2,1,0:T(8,128)(2,1)S(1)} %bitcast.46) | data formatting | bytes 1572864 | tf_op jit(solution)/shard_map/squeeze | solution.py:208
  61.0 1.4 %copy.12 = f32[4,768,128]{1,2,0:T(8,128)S(1)} copy(bf16[4,768,128]{2,1,0:T(8,128)(2,1)} %bitcast.47) | data formatting | bytes 2359296 | tf_op jit(solution)/shard_map/convert_element_type | solution.py:198
  62.4 1.2 %collective-permute-done.8 = bf16[4,768,128]{1,2,0:T(8,128)(2,1)} collective-permute-done((bf16[4,768,128]{1,2,0:T(8,128)(2,1)}, bf16[4,768,128]{1,2,0:T(8,128)(2,1)}, u32[]{:S(2)}, u32[]{:S(2)}) %collective-permute-start.8) | collective-permute-done | bytes 786464 | tf_op jit(solution)/shard_map/ppermute | solution.py:18
  63.6 1.4 %add_convert_fusion = bf16[4,768,128]{1,2,0:T(8,128)(2,1)S(1)} fusion(f32[4,768,128]{1,2,0:T(8,128)S(1)} %copy.12, bf16[4,768,128]{1,2,0:T(8,128)(2,1)} %collective-permute-done.8), kind=kLoop, calls=%fused_computation | loop fusion | flops 1179648 | bytes 3145728 | tf_op jit(solution)/shard_map/convert_element_type | solution.py:198
  65.2 2.8 %collective-permute-start.14 = (bf16[768,128]{0,1:T(8,128)(2,1)S(1)}, bf16[768,128]{0,1:T(8,128)(2,1)S(1)}, u32[]{:S(2)}, u32[]{:S(2)}) collective-permute-start(bf16[768,128]{0,1:T(8,128)(2,1)S(1)} %get-tuple-element.31), channel_id=1, source_target_pairs={{0,192},{64,0},{128,64},{192,128},{1,193},{65,1},{129,65},{193,129... | collective-permute-start | bytes 589832 | tf_op jit(solution)/shard_map/ppermute | solution.py:18
  68.0 0.9 collective-permute-start.13
  69.7 2.8 %shard_map.70 = bf16[4,128,768]{2,1,0:T(8,128)(2,1)S(1)} custom-call(s32[1]{0:T(128)} %bitcast.core_ref, bf16[4,4,192,128]{3,2,1,0:T(8,128)(2,1)S(1)} %pad_maximum_fusion.mine_ref, bf16[4,4,192,128]{3,2,1,0:T(8,128)(2,1)S(1)} %collective-permute-done.7.other_ref, bf16[8,192,768]{2,1,0:T(8,128)(2,1)S(1)} %bitcast.45), custom_call_target="tpu_custom_call" | custom-call | flops 9663676416 | bytes 4194304 | tf_op jit(solution)/shard_map/pallas_call | solution.py:176
  72.5 1.9 %collective-permute-start.9 = (bf16[128,768]{1,0:T(8,128)(2,1)S(1)}, bf16[128,768]{1,0:T(8,128)(2,1)S(1)}, u32[]{:S(2)}, u32[]{:S(2)}) collective-permute-start(bf16[128,768]{1,0:T(8,128)(2,1)S(1)} %get-tuple-element.34), channel_id=1, source_target_pairs={{0,64},{64,128},{128,192},{192,0},{1,65},{65,129},{129,193},{193,1... | collective-permute-start | bytes 589832 | tf_op jit(solution)/shard_map/ppermute | solution.py:18
  74.4 1.4 %collective-permute-start.11 = (bf16[128,768]{1,0:T(8,128)(2,1)S(1)}, bf16[128,768]{1,0:T(8,128)(2,1)S(1)}, u32[]{:S(2)}, u32[]{:S(2)}) collective-permute-start(bf16[128,768]{1,0:T(8,128)(2,1)S(1)} %get-tuple-element.35), channel_id=1, source_target_pairs={{0,192},{64,0},{128,64},{192,128},{1,193},{65,1},{129,65},{193,129... | collective-permute-start | bytes 589832 | tf_op jit(solution)/shard_map/ppermute | solution.py:18
  75.8 1.6 %collective-permute-done.14 = bf16[768,128]{0,1:T(8,128)(2,1)S(1)} collective-permute-done((bf16[768,128]{0,1:T(8,128)(2,1)S(1)}, bf16[768,128]{0,1:T(8,128)(2,1)S(1)}, u32[]{:S(2)}, u32[]{:S(2)}) %collective-permute-start.14) | collective-permute-done | bytes 196640 | tf_op jit(solution)/shard_map/ppermute | solution.py:18
  77.4 3.0 %collective-permute-done.12 = bf16[768,128]{0,1:T(8,128)(2,1)S(1)} collective-permute-done((bf16[768,128]{0,1:T(8,128)(2,1)S(1)}, bf16[768,128]{0,1:T(8,128)(2,1)S(1)}, u32[]{:S(2)}, u32[]{:S(2)}) %collective-permute-start.12) | collective-permute-done | bytes 196640 | tf_op jit(solution)/shard_map/ppermute | solution.py:18
  80.6 1.5 %collective-permute-start.15 = (bf16[768,128]{0,1:T(8,128)(2,1)S(1)}, bf16[768,128]{0,1:T(8,128)(2,1)S(1)}, u32[]{:S(2)}, u32[]{:S(2)}) collective-permute-start(bf16[768,128]{0,1:T(8,128)(2,1)S(1)} %get-tuple-element.27), channel_id=1, source_target_pairs={{0,2},{2,4},{4,6},{6,0},{1,3},{3,5},{5,7},{7,1},{8,10},{10,12},{12... | collective-permute-start | bytes 589832 | tf_op jit(solution)/shard_map/ppermute | solution.py:18
  82.7 2.9 %collective-permute-done.9 = bf16[128,768]{1,0:T(8,128)(2,1)S(1)} collective-permute-done((bf16[128,768]{1,0:T(8,128)(2,1)S(1)}, bf16[128,768]{1,0:T(8,128)(2,1)S(1)}, u32[]{:S(2)}, u32[]{:S(2)}) %collective-permute-start.9) | collective-permute-done | bytes 196640 | tf_op jit(solution)/shard_map/ppermute | solution.py:18
  85.6 2.1 %collective-permute-start.16 = (bf16[768,128]{0,1:T(8,128)(2,1)S(1)}, bf16[768,128]{0,1:T(8,128)(2,1)S(1)}, u32[]{:S(2)}, u32[]{:S(2)}) collective-permute-start(bf16[768,128]{0,1:T(8,128)(2,1)S(1)} %get-tuple-element.29), channel_id=1, source_target_pairs={{0,4},{2,6},{4,0},{6,2},{1,5},{3,7},{5,1},{7,3},{8,12},{10,14},{12... | collective-permute-start | bytes 589832 | tf_op jit(solution)/shard_map/ppermute | solution.py:18
  87.7 1.1 %collective-permute-done.10 = bf16[128,768]{1,0:T(8,128)(2,1)S(1)} collective-permute-done((bf16[128,768]{1,0:T(8,128)(2,1)S(1)}, bf16[128,768]{1,0:T(8,128)(2,1)S(1)}, u32[]{:S(2)}, u32[]{:S(2)}) %collective-permute-start.10) | collective-permute-done | bytes 196640 | tf_op jit(solution)/shard_map/ppermute | solution.py:18
  89.6 4.4 %collective-permute-done.16 = bf16[768,128]{0,1:T(8,128)(2,1)S(1)} collective-permute-done((bf16[768,128]{0,1:T(8,128)(2,1)S(1)}, bf16[768,128]{0,1:T(8,128)(2,1)S(1)}, u32[]{:S(2)}, u32[]{:S(2)}) %collective-permute-start.16) | collective-permute-done | bytes 196640 | tf_op jit(solution)/shard_map/ppermute | solution.py:18
  94.7 4.6 %reduce-scatter.2.cloned.1.call-done = bf16[1,192,768]{2,1,0:T(8,128)(2,1)} async-done(((bf16[8,192,768]{2,1,0:T(8,128)(2,1)}), bf16[1,192,768]{2,1,0:T(8,128)(2,1)}) %reduce-scatter.2.cloned.1.call-update) | async-done | bytes 294928 | tf_op jit(solution)/shard_map/reduce_scatter | solution.py:241
  99.4 1.7 %shard_map.71 = f32[192,768]{1,0:T(8,128)} custom-call(bf16[192,768]{1,0:T(8,128)(2,1)} %bitcast.52), custom_call_target="tpu_custom_call" | custom-call | tf_op jit(solution)/shard_map/pallas_call | solution.py:242
  (39 shorter events, 4.5 us)
Async XLA Ops:
  7.2 47.8 %all-gather.3.cloned.1.call-start = ((), (), s32[]{:S(2)}) async-start(), calls=%async_computation.2 | async-start | bytes 2654208 | tf_op jit(solution)/shard_map/all_gather | solution.py:228
  9.1 90.3 %reduce-scatter.2.cloned.1.call-start = ((), (), s32[]{:S(2)}) async-start(), calls=%async_computation.1 | async-start | bytes 2654208 | tf_op jit(solution)/shard_map/reduce_scatter | solution.py:241
  9.1 15.0 %collective-permute-start.2 = (bf16[128,768]{1,0:T(8,128)(2,1)}, bf16[128,768]{1,0:T(8,128)(2,1)S(1)}, u32[]{:S(2)}, u32[]{:S(2)}) collective-permute-start(bf16[128,768]{1,0:T(8,128)(2,1)} %param.7), channel_id=1, source_target_pairs={{0,192},{64,0},{128,64},{192,128},{1,193},{65,1},{129,65},{193,129... | collective-permute-start | bytes 589832 | tf_op jit(solution)/shard_map/ppermute | solution.py:18
  12.2 27.4 %copy-start.2 = (bf16[128,768]{1,0:T(8,128)(2,1)S(1)}, bf16[128,768]{1,0:T(8,128)(2,1)}, u32[]{:S(2)}) copy-start(bf16[128,768]{1,0:T(8,128)(2,1)} %param.7) | copy-start | bytes 589828
  12.2 11.9 %collective-permute-start.1 = (bf16[768,128]{0,1:T(8,128)(2,1)}, bf16[768,128]{0,1:T(8,128)(2,1)S(1)}, u32[]{:S(2)}, u32[]{:S(2)}) collective-permute-start(bf16[768,128]{0,1:T(8,128)(2,1)} %bitcast.60), channel_id=1, source_target_pairs={{0,2},{2,66},{4,130},{6,194},{64,4},{66,68},{68,132},{70,196},{128... | collective-permute-start | bytes 589832 | tf_op jit(solution)/shard_map/ppermute | solution.py:204
  12.2 17.4 %collective-permute-start = (bf16[768,128]{0,1:T(8,128)(2,1)}, bf16[768,128]{0,1:T(8,128)(2,1)S(1)}, u32[]{:S(2)}, u32[]{:S(2)}) collective-permute-start(bf16[768,128]{0,1:T(8,128)(2,1)} %bitcast.61), channel_id=1, source_target_pairs={{0,0},{2,64},{4,128},{6,192},{64,2},{66,66},{68,130},{70,194},{128... | collective-permute-start | bytes 589832 | tf_op jit(solution)/shard_map/ppermute | solution.py:204
  18.6 18.7 %collective-permute-start.5 = (bf16[128,768]{1,0:T(8,128)(2,1)}, bf16[128,768]{1,0:T(8,128)(2,1)S(1)}, u32[]{:S(2)}, u32[]{:S(2)}) collective-permute-start(bf16[128,768]{1,0:T(8,128)(2,1)} %param.7), channel_id=1, source_target_pairs={{0,128},{64,192},{128,0},{192,64},{1,129},{65,193},{129,1},{193,65... | collective-permute-start | bytes 589832 | tf_op jit(solution)/shard_map/ppermute | solution.py:18
  18.7 19.9 %collective-permute-start.6 = (bf16[128,768]{1,0:T(8,128)(2,1)}, bf16[128,768]{1,0:T(8,128)(2,1)S(1)}, u32[]{:S(2)}, u32[]{:S(2)}) collective-permute-start(bf16[128,768]{1,0:T(8,128)(2,1)} %param.7), channel_id=1, source_target_pairs={{0,64},{64,128},{128,192},{192,0},{1,65},{65,129},{129,193},{193,1... | collective-permute-start | bytes 589832 | tf_op jit(solution)/shard_map/ppermute | solution.py:18
  24.1 14.5 %collective-permute-start.4 = (bf16[768,128]{0,1:T(8,128)(2,1)}, bf16[768,128]{0,1:T(8,128)(2,1)S(1)}, u32[]{:S(2)}, u32[]{:S(2)}) collective-permute-start(bf16[768,128]{0,1:T(8,128)(2,1)} %bitcast.62), channel_id=1, source_target_pairs={{0,6},{2,70},{4,134},{6,198},{64,0},{66,64},{68,128},{70,192},{128... | collective-permute-start | bytes 589832 | tf_op jit(solution)/shard_map/ppermute | solution.py:204
  24.1 14.5 %collective-permute-start.3 = (bf16[768,128]{0,1:T(8,128)(2,1)}, bf16[768,128]{0,1:T(8,128)(2,1)S(1)}, u32[]{:S(2)}, u32[]{:S(2)}) collective-permute-start(bf16[768,128]{0,1:T(8,128)(2,1)} %bitcast.63), channel_id=1, source_target_pairs={{0,4},{2,68},{4,132},{6,196},{64,6},{66,70},{68,134},{70,198},{128... | collective-permute-start | bytes 589832 | tf_op jit(solution)/shard_map/ppermute | solution.py:204
  39.4 2.4 %collective-permute-start.7 = (bf16[4,4,192,128]{3,2,1,0:T(8,128)(2,1)S(1)}, bf16[4,4,192,128]{3,2,1,0:T(8,128)(2,1)S(1)}, u32[]{:S(2)}, u32[]{:S(2)}) collective-permute-start(bf16[4,4,192,128]{3,2,1,0:T(8,128)(2,1)S(1)} %pad_maximum_fusion.mine_ref), channel_id=1, source_target_pairs={{0,1},{1,0},{2,3},{3,2},{4,5},{5,4},{6,7},{7,6},{8,9},{9,8},{10,11... | collective-permute-start | bytes 2359304 | tf_op jit(solution)/shard_map/ppermute | solution.py:18
  54.9 1.7 %copy-start = (bf16[1536,768]{1,0:T(8,128)(2,1)S(1)}, bf16[1536,768]{1,0:T(8,128)(2,1)}, u32[]{:S(2)}) copy-start(bf16[1536,768]{1,0:T(8,128)(2,1)} %all-gather.3.cloned.1.call-done) | copy-start | bytes 7077892
  61.0 2.6 %collective-permute-start.8 = (bf16[4,768,128]{1,2,0:T(8,128)(2,1)}, bf16[4,768,128]{1,2,0:T(8,128)(2,1)}, u32[]{:S(2)}, u32[]{:S(2)}) collective-permute-start(bf16[4,768,128]{1,2,0:T(8,128)(2,1)} %copy.11), channel_id=1, source_target_pairs={{0,1},{1,0},{2,3},{3,2},{4,5},{5,4},{6,7},{7,6},{8,9},{9,8},{10,11... | collective-permute-start | bytes 2359304 | tf_op jit(solution)/shard_map/ppermute | solution.py:18
  63.6 6.0 %copy-start.1 = (bf16[1536,768]{1,0:T(8,128)(2,1)S(1)}, bf16[1536,768]{1,0:T(8,128)(2,1)}, u32[]{:S(2)}) copy-start(bf16[1536,768]{1,0:T(8,128)(2,1)} %all-gather.3.cloned.1.call-done) | copy-start | bytes 7077892
  65.2 12.3 %collective-permute-start.14 = (bf16[768,128]{0,1:T(8,128)(2,1)S(1)}, bf16[768,128]{0,1:T(8,128)(2,1)S(1)}, u32[]{:S(2)}, u32[]{:S(2)}) collective-permute-start(bf16[768,128]{0,1:T(8,128)(2,1)S(1)} %get-tuple-element.31), channel_id=1, source_target_pairs={{0,192},{64,0},{128,64},{192,128},{1,193},{65,1},{129,65},{193,129... | collective-permute-start | bytes 589832 | tf_op jit(solution)/shard_map/ppermute | solution.py:18
  68.0 9.5 %collective-permute-start.13 = (bf16[768,128]{0,1:T(8,128)(2,1)S(1)}, bf16[768,128]{0,1:T(8,128)(2,1)S(1)}, u32[]{:S(2)}, u32[]{:S(2)}) collective-permute-start(bf16[768,128]{0,1:T(8,128)(2,1)S(1)} %get-tuple-element.32), channel_id=1, source_target_pairs={{0,128},{64,192},{128,0},{192,64},{1,129},{65,193},{129,1},{193,65... | collective-permute-start | bytes 589832 | tf_op jit(solution)/shard_map/ppermute | solution.py:18
  68.9 11.5 %collective-permute-start.12 = (bf16[768,128]{0,1:T(8,128)(2,1)S(1)}, bf16[768,128]{0,1:T(8,128)(2,1)S(1)}, u32[]{:S(2)}, u32[]{:S(2)}) collective-permute-start(bf16[768,128]{0,1:T(8,128)(2,1)S(1)} %get-tuple-element.33), channel_id=1, source_target_pairs={{0,64},{64,128},{128,192},{192,0},{1,65},{65,129},{129,193},{193,1... | collective-permute-start | bytes 589832 | tf_op jit(solution)/shard_map/ppermute | solution.py:18
  72.5 13.1 %collective-permute-start.9 = (bf16[128,768]{1,0:T(8,128)(2,1)S(1)}, bf16[128,768]{1,0:T(8,128)(2,1)S(1)}, u32[]{:S(2)}, u32[]{:S(2)}) collective-permute-start(bf16[128,768]{1,0:T(8,128)(2,1)S(1)} %get-tuple-element.34), channel_id=1, source_target_pairs={{0,64},{64,128},{128,192},{192,0},{1,65},{65,129},{129,193},{193,1... | collective-permute-start | bytes 589832 | tf_op jit(solution)/shard_map/ppermute | solution.py:18
  74.4 13.4 %collective-permute-start.11 = (bf16[128,768]{1,0:T(8,128)(2,1)S(1)}, bf16[128,768]{1,0:T(8,128)(2,1)S(1)}, u32[]{:S(2)}, u32[]{:S(2)}) collective-permute-start(bf16[128,768]{1,0:T(8,128)(2,1)S(1)} %get-tuple-element.35), channel_id=1, source_target_pairs={{0,192},{64,0},{128,64},{192,128},{1,193},{65,1},{129,65},{193,129... | collective-permute-start | bytes 589832 | tf_op jit(solution)/shard_map/ppermute | solution.py:18
  77.4 11.4 %collective-permute-start.10 = (bf16[128,768]{1,0:T(8,128)(2,1)S(1)}, bf16[128,768]{1,0:T(8,128)(2,1)S(1)}, u32[]{:S(2)}, u32[]{:S(2)}) collective-permute-start(bf16[128,768]{1,0:T(8,128)(2,1)S(1)} %get-tuple-element.36), channel_id=1, source_target_pairs={{0,128},{64,192},{128,0},{192,64},{1,129},{65,193},{129,1},{193,65... | collective-permute-start | bytes 589832 | tf_op jit(solution)/shard_map/ppermute | solution.py:18
  80.6 9.0 %collective-permute-start.15 = (bf16[768,128]{0,1:T(8,128)(2,1)S(1)}, bf16[768,128]{0,1:T(8,128)(2,1)S(1)}, u32[]{:S(2)}, u32[]{:S(2)}) collective-permute-start(bf16[768,128]{0,1:T(8,128)(2,1)S(1)} %get-tuple-element.27), channel_id=1, source_target_pairs={{0,2},{2,4},{4,6},{6,0},{1,3},{3,5},{5,7},{7,1},{8,10},{10,12},{12... | collective-permute-start | bytes 589832 | tf_op jit(solution)/shard_map/ppermute | solution.py:18
  82.1 7.4 %collective-permute-start.17 = (bf16[768,128]{0,1:T(8,128)(2,1)S(1)}, bf16[768,128]{0,1:T(8,128)(2,1)S(1)}, u32[]{:S(2)}, u32[]{:S(2)}) collective-permute-start(bf16[768,128]{0,1:T(8,128)(2,1)S(1)} %get-tuple-element.28), channel_id=1, source_target_pairs={{0,6},{2,0},{4,2},{6,4},{1,7},{3,1},{5,3},{7,5},{8,14},{10,8},{12,... | collective-permute-start | bytes 589832 | tf_op jit(solution)/shard_map/ppermute | solution.py:18
  85.6 8.3 %collective-permute-start.16 = (bf16[768,128]{0,1:T(8,128)(2,1)S(1)}, bf16[768,128]{0,1:T(8,128)(2,1)S(1)}, u32[]{:S(2)}, u32[]{:S(2)}) collective-permute-start(bf16[768,128]{0,1:T(8,128)(2,1)S(1)} %get-tuple-element.29), channel_id=1, source_target_pairs={{0,4},{2,6},{4,0},{6,2},{1,5},{3,7},{5,1},{7,3},{8,12},{10,14},{12... | collective-permute-start | bytes 589832 | tf_op jit(solution)/shard_map/ppermute | solution.py:18
Sparse Core Ops, SparseCore 0:
  10.4 44.5 all-gather.2
  57.5 41.8 reduce-scatter.1
